TPU v7x, 32 devices: a whole 2x2x4 slice. The times are simulated.
32 devices in a mesh: dp: 16 (over z, y, x), fsdp: 2 (over core).
Axes of the slice: x: 2, y: 2, z: 4, core: 2. Of those that a mesh axis runs over, the one named last changes fastest.
Arguments:
- mel_panels: bfloat16 [512, 10240], P(('dp', 'fsdp')), may hold values from -6 to 6
- frames: int32 [512], P(('dp', 'fsdp')), may hold values from 0 to 128, as said below
- target: int32 [512], P(('dp', 'fsdp')), may hold values from 0 to 15, as said below
- conv_first: bfloat16 [9, 256], P(None, 'fsdp'), may hold values from -2 to 2
- depth_a: bfloat16 [9, 256], P(None, 'fsdp'), may hold values from -3 to 3
- point_a: bfloat16 [256, 256], P(None, 'fsdp'), may hold values from -0.5 to 0.5
- depth_b: bfloat16 [9, 256], P(None, 'fsdp'), may hold values from -3 to 3
- point_b: bfloat16 [256, 256], P(None, 'fsdp'), may hold values from -0.5 to 0.5
- linear_weight: bfloat16 [2560, 1024], P(None, 'fsdp'), may hold values from -0.15625 to 0.15625
- norm_gain: bfloat16 [1024], P('fsdp'), may hold values from 0.099609375 to 1.8984375
- up_weight: bfloat16 [1024, 2048], P(None, 'fsdp'), may hold values from -0.1875 to 0.1875
- depth_kernel: bfloat16 [9, 1024], P(None, 'fsdp'), may hold values from -2 to 2
- conv_gain: bfloat16 [1024], P('fsdp'), may hold values from 0.099609375 to 1.8984375
- down_weight: bfloat16 [1024, 1024], P('fsdp'), may hold values from -0.1875 to 0.1875
- cotangent: bfloat16 [4096, 1024], P(('dp', 'fsdp')), may hold values from -6 to 6
Outputs:
- layer_out: bfloat16 [4096, 1024], P(('dp', 'fsdp'))
- grad_input: bfloat16 [4096, 1024], P(('dp', 'fsdp'))
- grad_down: float32 [1024, 1024], P('fsdp')
Inputs may be any that keep to these rules, and one draw needn't show every extreme that they name: The slots of one loader are those of one index of dp and fsdp. A live slot holds a panel of 8 * m frames with 8 * m >= 32; frames = 0 marks an empty slot. Every device receives exactly 8 panels from the loaders of its own fsdp index, at most one from any loader, and one of them has 128 frames. `target`: only live slots are sent.
All inputs are finite; a program needn't handle non-finite values.
Results may differ from a plain program's by a relative error of at most 0.017.
Values may be sent and summed in bfloat16 or wider, within the bound.
No kernel may reach another device: no remote copies, remote signals or barrier semaphores. Data moves between devices by JAX's collectives and lax.ppermute only.
A program may use at most 192 MiB of HBM per device.

v0:
```python
import math

import jax
import jax.numpy as jnp
from jax import lax
from jax.sharding import PartitionSpec as P

MELS = 80
PANEL = 128


EPSILON = 1e-05


def phase_rows(source):
    shape_in = source.shape
    split = source.reshape((shape_in[0], shape_in[1] // 2, 2) + shape_in[2:])
    even = split[:, :, 0]
    odd = split[:, :, 1]
    before = jnp.concatenate([jnp.zeros_like(odd[:, :1]), odd[:, :-1]], axis=1)
    return (before, even, odd)


def phase_cols(source):
    shape_in = source.shape
    split = source.reshape(shape_in[:2] + (shape_in[2] // 2, 2) + shape_in[3:])
    even = split[:, :, :, 0]
    odd = split[:, :, :, 1]
    before = jnp.concatenate([jnp.zeros_like(odd[:, :, :1]), odd[:, :, :-1]], axis=2)
    return (before, even, odd)


def first_section(masked, weights):
    height = masked.shape[1] // 2
    breadth = masked.shape[2] // 2
    summed = jnp.zeros((masked.shape[0], height, breadth, weights.shape[1]), jnp.float32)
    row_views = phase_rows(masked)
    for i in range(3):
        col_views = phase_cols(row_views[i])
        for j in range(3):
            window = col_views[j].astype(jnp.float32)
            summed = summed + window[:, :, :, None] * weights[3 * i + j].astype(jnp.float32)
    return jnp.maximum(summed, 0.0).astype(jnp.bfloat16)


def depth_stride(source, weights):
    height = source.shape[1] // 2
    breadth = source.shape[2] // 2
    summed = jnp.zeros((source.shape[0], height, breadth, source.shape[3]), jnp.float32)
    row_views = phase_rows(source)
    for i in range(3):
        col_views = phase_cols(row_views[i])
        for j in range(3):
            window = col_views[j].astype(jnp.float32)
            summed = summed + window * weights[3 * i + j].astype(jnp.float32)
    return summed.astype(jnp.bfloat16)


def point_relu(spread, weights):
    shape_in = spread.shape
    mapped = jnp.dot(spread.reshape(-1, shape_in[3]), weights, preferred_element_type=jnp.float32)
    return jnp.maximum(mapped, 0.0).astype(jnp.bfloat16).reshape(shape_in[:3] + (weights.shape[1],))


def subsample(block_panels, block_lengths, conv_first, depth_a, point_a, depth_b, point_b):
    number = block_panels.shape[0]
    frames_in = block_panels.reshape(number, PANEL, MELS)
    inside = jnp.arange(PANEL)[None, :] < block_lengths[:, None]
    masked = jnp.where(inside[:, :, None], frames_in, jnp.zeros_like(frames_in))
    first = first_section(masked, conv_first)
    second = point_relu(depth_stride(first, depth_a), point_a)
    fourth = point_relu(depth_stride(second, depth_b), point_b)
    return fourth.reshape(number * fourth.shape[1], fourth.shape[2] * fourth.shape[3])


def depth_forward(gated, kernel, span):
    groups_in = gated.shape[0] // span
    half_width = kernel.shape[0] // 2
    shaped = jnp.pad(gated.reshape(groups_in, span, -1), ((0, 0), (half_width, half_width), (0, 0)))
    summed = jnp.zeros((groups_in, span, gated.shape[1]), jnp.float32)
    for k in range(kernel.shape[0]):
        summed = summed + shaped[:, k : k + span].astype(jnp.float32) * kernel[k].astype(
            jnp.float32
        )
    return summed.reshape(gated.shape[0], -1)


def depth_backward(upstream, kernel, span):
    groups_in = upstream.shape[0] // span
    half_width = kernel.shape[0] // 2
    shaped = jnp.pad(
        upstream.reshape(groups_in, span, -1), ((0, 0), (half_width, half_width), (0, 0))
    )
    summed = jnp.zeros((groups_in, span, upstream.shape[1]), jnp.float32)
    for k in range(kernel.shape[0]):
        offset = 2 * half_width - k
        summed = summed + shaped[:, offset : offset + span] * kernel[k].astype(jnp.float32)
    return summed.reshape(upstream.shape[0], -1)


def module_pass(
    features, keep, cotangent, norm_gain, up_weight, depth_kernel, conv_gain, down_weight, span
):
    width = features.shape[1]
    values = features.astype(jnp.float32)
    centred = values - jnp.mean(values, axis=1, keepdims=True)
    scale_one = lax.rsqrt(jnp.mean(centred * centred, axis=1, keepdims=True) + EPSILON)
    standard = centred * scale_one
    normed = (standard * norm_gain.astype(jnp.float32)).astype(jnp.bfloat16)
    projected = jnp.dot(normed, up_weight, preferred_element_type=jnp.float32)
    value_half = projected[:, :width]
    gate_half = jax.nn.sigmoid(projected[:, width:])
    row_keep = keep[:, None]
    gated = (row_keep * value_half * gate_half).astype(jnp.bfloat16)
    depthwise = depth_forward(gated, depth_kernel, span)
    centred_two = depthwise - jnp.mean(depthwise, axis=1, keepdims=True)
    scale_two = lax.rsqrt(jnp.mean(centred_two * centred_two, axis=1, keepdims=True) + EPSILON)
    standard_two = centred_two * scale_two
    active = standard_two * conv_gain.astype(jnp.float32)
    swish_gate = jax.nn.sigmoid(active)
    hidden = (active * swish_gate).astype(jnp.bfloat16)
    mixed = jnp.dot(hidden, down_weight, preferred_element_type=jnp.float32)
    layer_out = (row_keep * (values + mixed)).astype(jnp.bfloat16)
    back_out = jnp.where(row_keep > 0, cotangent, jnp.zeros_like(cotangent))
    back_hidden = lax.dot_general(
        back_out, down_weight, (((1,), (1,)), ((), ())), preferred_element_type=jnp.float32
    )
    back_active = back_hidden * (swish_gate + active * swish_gate * (1.0 - swish_gate))
    gain_back = back_active * conv_gain.astype(jnp.float32)
    back_depth = scale_two * (
        gain_back
        - jnp.mean(gain_back, axis=1, keepdims=True)
        - standard_two * jnp.mean(gain_back * standard_two, axis=1, keepdims=True)
    )
    back_gated = row_keep * depth_backward(back_depth, depth_kernel, span)
    back_proj = jnp.concatenate(
        [back_gated * gate_half, back_gated * value_half * gate_half * (1.0 - gate_half)], axis=1
    ).astype(jnp.bfloat16)
    back_normed = lax.dot_general(
        back_proj, up_weight, (((1,), (1,)), ((), ())), preferred_element_type=jnp.float32
    )
    gain_front = back_normed * norm_gain.astype(jnp.float32)
    back_input = scale_one * (
        gain_front
        - jnp.mean(gain_front, axis=1, keepdims=True)
        - standard * jnp.mean(gain_front * standard, axis=1, keepdims=True)
    )
    grad_input = (back_out.astype(jnp.float32) + back_input).astype(jnp.bfloat16)
    return (layer_out, grad_input, hidden, back_out)


def local(
    mel_panels,
    frames,
    target,
    conv_first,
    depth_a,
    point_a,
    depth_b,
    point_b,
    linear_weight,
    norm_gain,
    up_weight,
    depth_kernel,
    conv_gain,
    down_weight,
    cotangent,
):
    groups = lax.axis_size("dp")
    members = lax.axis_size("fsdp")
    span = PANEL // 8
    panel_count = cotangent.shape[0] // span
    destinations = jnp.arange(groups, dtype=jnp.int32)
    selected = (target[None, :] == destinations[:, None]) & (frames[None, :] > 0)
    outgoing = jnp.dot(
        selected.astype(jnp.bfloat16), mel_panels, preferred_element_type=jnp.float32
    ).astype(jnp.bfloat16)
    sent_frames = jnp.sum(jnp.where(selected, frames[None, :], 0), axis=1)
    incoming, got_frames = (
        lax.all_to_all(outgoing, "dp", split_axis=0, concat_axis=0, tiled=True),
        lax.all_to_all(sent_frames, "dp", split_axis=0, concat_axis=0, tiled=True),
    )
    present = got_frames > 0
    position = jnp.cumsum(present.astype(jnp.int32)) - 1
    places = jnp.arange(panel_count, dtype=jnp.int32)
    placing = (position[None, :] == places[:, None]) & present[None, :]
    panels = jnp.dot(
        placing.astype(jnp.bfloat16), incoming, preferred_element_type=jnp.float32
    ).astype(jnp.bfloat16)
    lengths = jnp.sum(jnp.where(placing, got_frames[None, :], 0), axis=1).astype(jnp.int32)
    first_full, depth_one, point_one, depth_two, point_two, gain_front, kernel_full, gain_back = (
        lax.all_gather(conv_first, "fsdp", axis=1, tiled=True),
        lax.all_gather(depth_a, "fsdp", axis=1, tiled=True),
        lax.all_gather(point_a, "fsdp", axis=1, tiled=True),
        lax.all_gather(depth_b, "fsdp", axis=1, tiled=True),
        lax.all_gather(point_b, "fsdp", axis=1, tiled=True),
        lax.all_gather(norm_gain, "fsdp", axis=0, tiled=True),
        lax.all_gather(depth_kernel, "fsdp", axis=1, tiled=True),
        lax.all_gather(conv_gain, "fsdp", axis=0, tiled=True),
    )
    per_block = math.gcd(panel_count, 16)

    def sub_block(block_args):
        return subsample(
            block_args[0], block_args[1], first_full, depth_one, point_one, depth_two, point_two
        )

    flat_rows = lax.map(
        sub_block,
        (
            panels.reshape(panel_count // per_block, per_block, -1),
            lengths.reshape(panel_count // per_block, per_block),
        ),
    )
    flat_rows = flat_rows.reshape(panel_count * span, -1)
    features = jnp.dot(
        flat_rows,
        lax.all_gather(linear_weight, "fsdp", axis=1, tiled=True),
        preferred_element_type=jnp.float32,
    ).astype(jnp.bfloat16)
    keep = (jnp.arange(span)[None, :] < (lengths // 8)[:, None]).reshape(-1).astype(jnp.float32)
    up_full, down_full = (
        lax.all_gather(up_weight, "fsdp", axis=1, tiled=True),
        lax.all_gather(down_weight, "fsdp", axis=0, tiled=True),
    )
    layer_out, grad_input, hidden, back_out = module_pass(
        features, keep, cotangent, gain_front, up_full, kernel_full, gain_back, down_full, span
    )
    local_rows = lax.psum_scatter(
        lax.dot_general(
            hidden, back_out, (((0,), (0,)), ((), ())), preferred_element_type=jnp.float32
        ).astype(jnp.bfloat16),
        "fsdp",
        scatter_dimension=0,
        tiled=True,
    ).astype(jnp.float32)
    summed = lax.psum(local_rows, "dp")
    grad_down = summed / jnp.sqrt(jnp.float32(cotangent.shape[0] * groups * members))
    return (layer_out, grad_input, grad_down)


def solution(mesh):
    placed = (
        P(("dp", "fsdp"), None),
        P(("dp", "fsdp")),
        P(("dp", "fsdp")),
        P(None, "fsdp"),
        P(None, "fsdp"),
        P(None, "fsdp"),
        P(None, "fsdp"),
        P(None, "fsdp"),
        P(None, "fsdp"),
        P("fsdp"),
        P(None, "fsdp"),
        P(None, "fsdp"),
        P("fsdp"),
        P("fsdp", None),
        P(("dp", "fsdp"), None),
    )
    return jax.shard_map(
        local,
        mesh=mesh,
        in_specs=placed,
        out_specs=(P(("dp", "fsdp"), None), P(("dp", "fsdp"), None), P("fsdp", None)),
        check_vma=False,
    )
```

profile of v0, /device:TPU:0, one launch (start us, length us, event | category | flops | bytes accessed | tf_op | source)
XLA Modules:
  0.0 266.8 jit_solution(9805383357988610290)
XLA Ops:
  9.6 8.3 %all-to-all-start = ((s32[16,1,1]{2,1,0:T(1,128)}), s32[16,1,1]{2,1,0:T(1,128)S(1)}, u32[]{:S(2)}, u32[]{:S(2)}) async-start(s32[16,1,1]{2,1,0:T(1,128)} %copy.182), calls=%async_computation | async-start | bytes 16384 | tf_op jit(solution)/shard_map/all_to_all | solution.py:181
  21.3 1.8 all_gather.33
  23.7 1.8 all_gather.34
  26.1 1.9 all_gather.35
  28.0 1.8 all_gather.36
  30.4 2.0 all_gather.37
  32.4 1.8 all-gather
  34.2 1.8 all_gather.41
  38.5 6.9 %all-to-all-start.1 = ((bf16[16,2,5120]{2,1,0:T(2,128)(2,1)}), bf16[16,2,5120]{2,1,0:T(2,128)(2,1)S(1)}, u32[]{:S(2)}, u32[]{:S(2)}) async-start(bf16[16,2,5120]{2,1,0:T(2,128)(2,1)} %reshape.614), calls=%async_computation.1 | async-start | bytes 655360 | tf_op jit(solution)/shard_map/all_to_all | solution.py:180
  46.9 10.2 %all-to-all-done.1 = bf16[16,2,5120]{2,1,0:T(2,128)(2,1)S(1)} async-done(((bf16[16,2,5120]{2,1,0:T(2,128)(2,1)}), bf16[16,2,5120]{2,1,0:T(2,128)(2,1)S(1)}, u32[]{:S(2)}, u32[]{:S(2)}) %all-to-all-start.1) | async-done | bytes 327712 | tf_op jit(solution)/shard_map/all_to_all | solution.py:180
  62.3 28.5 %maximum_convert_fusion = bf16[8,32,2,40,256]{4,1,3,0,2:T(8,128)(2,1)} fusion(f32[256]{0:T(256)} %bitcast.244, f32[8,32,2,40]{1,3,0,2:T(8,128)S(1)} %copy.209, f32[256]{0:T(256)} %bitcast.245, f32[8,32,2,40]{1,3,0,2:T(8,128)S(1)} %copy.207, f32[256]{0:T(256)} %bitcast.246, f32[8,32,2,40]{1,3,0,2:T(8,128)S(1)} %copy.205, f32[256]{0:T(256)} %bitcast.247, ...), kind=kLoop, calls=%fused_computation | loop fusion | flops 99614720 | bytes 11232256 | tf_op jit(solution)/shard_map/while/body/eval_jaxpr/convert_element_type | solution.py:43
  90.7 11.1 %slice_bitcast_fusion.14 = (bf16[8,32,40,256]{3,1,2,0:T(8,128)(2,1)}, bf16[8,32,1,40,256]{4,1,3,0,2:T(8,128)(2,1)}, bf16[8,32,1,40,256]{4,1,3,0,2:T(8,128)(2,1)}) fusion(bf16[8,32,2,40,256]{4,1,3,0,2:T(8,128)(2,1)} %maximum_convert_fusion), kind=kLoop, calls=%fused_computation.201 | loop fusion | bytes 26214400 | tf_op jit(solution)/shard_map/while/body/eval_jaxpr/squeeze | solution.py:19
  101.8 6.0 %concatenate.56 = bf16[8,32,40,256]{3,1,2,0:T(8,128)(2,1)S(1)} pad(bf16[8,31,40,256]{3,1,2,0:T(8,128)(2,1)} %bitcast.188, bf16[]{:T(256)} %constant.67.clone.1), padding=0_0x1_0x0_0x0_0 | pad | bytes 10321922 | tf_op jit(solution)/shard_map/while/body/eval_jaxpr/concatenate | solution.py:20
  108.3 2.7 %slice-done = s8[4194304]{0:T(1024)(128)(4,1)S(1)} async-done(((s8[5242880]{0:T(1024)(128)(4,1)}), s8[4194304]{0:T(1024)(128)(4,1)S(1)}, s32[]{:S(2)}) %slice-start) | async-done | bytes 4194328
  115.1 6.9 %fusion.4 = bf16[8,32,20,256]{3,1,2,0:T(8,128)(2,1)S(1)} fusion(bf16[8,32,20,2,256]{4,1,3,2,0:T(8,128)(2,1)S(1)} %bitcast.185, bf16[8,32,20,2,256]{4,1,3,2,0:T(8,128)(2,1)S(1)} %bitcast.181, bf16[8,32,20,2,256]{4,1,3,2,0:T(8,128)(2,1)S(1)} %bitcast.187, f32[256]{0:T(256)S(1)} %bitcast.235, f32[256]{0:T(256)S(1)} %bitcast.236, f32[256]{0:T(256)S(1)} %bitcast.237, ...), kind=kLoop, calls=%fused_computation.9 | loop fusion | flops 35389440 | bytes 25830400 | tf_op jit(solution)/shard_map/while/body/eval_jaxpr/convert_element_type | solution.py:56
  122.1 3.3 %copy.214 = bf16[8,32,20,256]{3,2,1,0:T(8,128)(2,1)} copy(bf16[8,32,20,256]{3,1,2,0:T(8,128)(2,1)S(1)} %fusion.4) | data formatting | bytes 5242880 | tf_op jit(solution)/shard_map/while/body/eval_jaxpr/convert_element_type | solution.py:56
  125.4 3.6 %reshape.544 = bf16[5120,256]{1,0:T(8,128)(2,1)S(1)} reshape(bf16[8,32,20,256]{3,2,1,0:T(8,128)(2,1)} %copy.214) | data formatting | bytes 5242880 | tf_op jit(solution)/shard_map/while/body/eval_jaxpr/reshape | solution.py:61
  129.0 2.4 fusion.1
  131.4 3.5 %reshape.545 = bf16[8,16,2,20,256]{4,3,2,1,0:T(8,128)(2,1)S(1)} reshape(bf16[5120,256]{1,0:T(8,128)(2,1)} %fusion.1) | data formatting | bytes 5242880 | tf_op jit(solution)/shard_map/while/body/eval_jaxpr/reshape;while/body/eval_jaxpr/reshape | solution.py:17
  140.4 3.4 %fusion.73 = (f32[128]{0:T(128)S(1)}, f32[128,1024]{1,0:T(8,128)S(1)}) fusion(bf16[128,2560]{1,0:T(8,128)(2,1)S(1)} %reshape.548, bf16[2560,1024]{1,0:T(8,128)(2,1)} %all-gather.6.cloned.1.call-done), kind=kOutput, calls=%fused_computation.208 | convolution fusion | flops 671481728 | bytes 6423040 | tf_op jit(solution)/shard_map/dot_general | solution.py:216
  144.2 3.0 %fusion.51 = f32[128,2048]{1,0:T(8,128)S(1)} fusion(bf16[1024,2048]{1,0:T(8,128)(2,1)} %all-gather.8.cloned.1.call-done, f32[128,1024]{1,0:T(8,128)S(1)} %get-tuple-element.93, f32[1024]{0:T(1024)S(1)} %bitcast.231, f32[128]{0:T(128)S(1)} %add_rsqrt_fusion.1, f32[128]{0:T(128)S(1)} %broadcast_multiply_fusion.6), kind=kOutput, calls=%fused_computation.113 | convolution fusion | flops 537395200 | bytes 5772288 | tf_op jit(solution)/shard_map/dot_general | solution.py:110
  148.6 2.1 convolution_convert_fusion.2
  150.8 2.7 %fusion.68 = (f32[128]{0:T(128)S(1)}, f32[128]{0:T(128)S(1)}, f32[128,1024]{1,0:T(8,128)S(1)}) fusion(f32[128,1024]{1,0:T(8,128)S(1)} %fusion.47, f32[1024]{0:T(1024)S(1)} %bitcast.253, bf16[1024,1024]{1,0:T(8,128)(2,1)} %all-gather.10.cloned.1.call-done, bf16[128,1024]{1,0:T(8,128)(2,1)S(1)} %copy-done.5, pred[128]{0:T(512)(128)(4,1)S(1)} %copy-done.33), kind=kOutput, calls=%fused_computation.203 | convolution fusion | flops 270270208 | bytes 3413120 | tf_op jit(solution)/shard_map/dot_general | solution.py:125
  158.4 100.4 %all-reduce.15 = f32[512,1024]{1,0:T(8,128)S(1)} all-reduce(bf16[512,1024]{1,0:T(8,128)(2,1)} %reduce-scatter.2.cloned.1.call-done), channel_id=1, replica_groups=mesh['dp'=16,'fsdp'=2] {'dp'}, use_global_device_ids=true, to_apply=%region_12.13 | all-reduce | flops 524288 | bytes 3145728 | tf_op jit(solution)/shard_map/psum | solution.py:237
  (203 shorter events, 34.1 us)
Async XLA Ops:
  7.2 11.5 %copy-start = (bf16[16,10240]{1,0:T(8,128)(2,1)S(1)}, bf16[16,10240]{1,0:T(8,128)(2,1)}, u32[]{:S(2)}) copy-start(bf16[16,10240]{1,0:T(8,128)(2,1)} %param.15) | copy-start | bytes 983044
  7.2 14.1 %copy-start.17 = (bf16[9,128]{1,0:T(8,128)(2,1)S(1)}, bf16[9,128]{1,0:T(8,128)(2,1)}, u32[]{:S(2)}) copy-start(bf16[9,128]{1,0:T(8,128)(2,1)} %param.18) | copy-start | bytes 6916
  7.2 16.5 %copy-start.18 = (bf16[9,128]{1,0:T(8,128)(2,1)S(1)}, bf16[9,128]{1,0:T(8,128)(2,1)}, u32[]{:S(2)}) copy-start(bf16[9,128]{1,0:T(8,128)(2,1)} %param.19) | copy-start | bytes 6916
  7.2 18.9 %copy-start.6 = (bf16[256,128]{1,0:T(8,128)(2,1)S(1)}, bf16[256,128]{1,0:T(8,128)(2,1)}, u32[]{:S(2)}) copy-start(bf16[256,128]{1,0:T(8,128)(2,1)} %param.20) | copy-start | bytes 196612
  7.2 20.8 %copy-start.19 = (bf16[9,128]{1,0:T(8,128)(2,1)S(1)}, bf16[9,128]{1,0:T(8,128)(2,1)}, u32[]{:S(2)}) copy-start(bf16[9,128]{1,0:T(8,128)(2,1)} %param.21) | copy-start | bytes 6916
  7.2 23.2 %copy-start.7 = (bf16[256,128]{1,0:T(8,128)(2,1)S(1)}, bf16[256,128]{1,0:T(8,128)(2,1)}, u32[]{:S(2)}) copy-start(bf16[256,128]{1,0:T(8,128)(2,1)} %param.22) | copy-start | bytes 196612
  7.3 25.2 %copy-start.31 = (bf16[512]{0:T(512)(128)(2,1)S(1)}, bf16[512]{0:T(512)(128)(2,1)}, u32[]{:S(2)}) copy-start(bf16[512]{0:T(512)(128)(2,1)} %param.24) | copy-start | bytes 3076
  7.3 27.0 %copy-start.8 = (bf16[9,512]{1,0:T(8,128)(2,1)S(1)}, bf16[9,512]{1,0:T(8,128)(2,1)}, u32[]{:S(2)}) copy-start(bf16[9,512]{1,0:T(8,128)(2,1)} %param.26) | copy-start | bytes 27652
  7.3 28.8 %copy-start.32 = (bf16[512]{0:T(512)(128)(2,1)S(1)}, bf16[512]{0:T(512)(128)(2,1)}, u32[]{:S(2)}) copy-start(bf16[512]{0:T(512)(128)(2,1)} %param.27) | copy-start | bytes 3076
  7.3 133.2 %all-gather.6.cloned.1.call-start = ((), (), s32[]{:S(2)}) async-start(), calls=%async_computation.3 | async-start | bytes 7864320 | tf_op jit(solution)/shard_map/all_gather | solution.py:218
  8.0 136.1 %all-gather.8.cloned.1.call-start = ((), (), s32[]{:S(2)}) async-start(), calls=%async_computation.4 | async-start | bytes 6291456 | tf_op jit(solution)/shard_map/all_gather | solution.py:223
  9.6 28.9 %all-to-all-start = ((s32[16,1,1]{2,1,0:T(1,128)}), s32[16,1,1]{2,1,0:T(1,128)S(1)}, u32[]{:S(2)}, u32[]{:S(2)}) async-start(s32[16,1,1]{2,1,0:T(1,128)} %copy.182), calls=%async_computation | async-start | bytes 16384 | tf_op jit(solution)/shard_map/all_to_all | solution.py:181
  17.9 132.8 %all-gather.10.cloned.1.call-start = ((), (), s32[]{:S(2)}) async-start(), calls=%async_computation.5 | async-start | bytes 3145728 | tf_op jit(solution)/shard_map/all_gather | solution.py:224
  38.5 18.6 %all-to-all-start.1 = ((bf16[16,2,5120]{2,1,0:T(2,128)(2,1)}), bf16[16,2,5120]{2,1,0:T(2,128)(2,1)S(1)}, u32[]{:S(2)}, u32[]{:S(2)}) async-start(bf16[16,2,5120]{2,1,0:T(2,128)(2,1)} %reshape.614), calls=%async_computation.1 | async-start | bytes 655360 | tf_op jit(solution)/shard_map/all_to_all | solution.py:180
  45.4 113.0 %reduce-scatter.2.cloned.1.call-start = ((), (), s32[]{:S(2)}) async-start(), calls=%async_computation.6 | async-start | bytes 3145728 | tf_op jit(solution)/shard_map/reduce_scatter | solution.py:229
  107.9 3.1 %slice-start = ((s8[5242880]{0:T(1024)(128)(4,1)}), s8[4194304]{0:T(1024)(128)(4,1)S(1)}, s32[]{:S(2)}) async-start(s8[5242880]{0:T(1024)(128)(4,1)} %bitcast.178), calls=%async_computation.7 | async-start | bytes 8388608
  107.9 3.4 %slice-start.1 = ((s8[5242880]{0:T(1024)(128)(4,1)}), s8[1048576]{0:T(1024)(128)(4,1)S(1)}, s32[]{:S(2)}) async-start(s8[5242880]{0:T(1024)(128)(4,1)} %bitcast.178), calls=%async_computation.8 | async-start | bytes 2097152
  108.2 3.3 %copy-start.3 = (bf16[8,32,20,256]{3,1,2,0:T(8,128)(2,1)}, bf16[8,32,20,256]{3,1,2,0:T(8,128)(2,1)S(1)}, u32[]{:S(2)}) copy-start(bf16[8,32,20,256]{3,1,2,0:T(8,128)(2,1)S(1)} %slice_bitcast_fusion.5) | copy-start | bytes 7864324
  108.2 4.3 %slice-start.2 = ((s8[5242880]{0:T(1024)(128)(4,1)}), s8[4194304]{0:T(1024)(128)(4,1)S(1)}, s32[]{:S(2)}) async-start(s8[5242880]{0:T(1024)(128)(4,1)} %bitcast.182), calls=%async_computation.9 | async-start | bytes 8388608
  144.1 4.5 %copy-start.5 = (bf16[128,1024]{1,0:T(8,128)(2,1)S(1)}, bf16[128,1024]{1,0:T(8,128)(2,1)}, u32[]{:S(2)}) copy-start(bf16[128,1024]{1,0:T(8,128)(2,1)} %param.29) | copy-start | bytes 786436
  144.1 4.4 %copy-start.20 = (f32[2,1,512]{2,1,0:T(1,128)S(1)}, f32[2,1,512]{2,1,0:T(1,128)}, u32[]{:S(2)}) copy-start(f32[2,1,512]{2,1,0:T(1,128)} %convert_element_type.810) | copy-start | bytes 12292
  144.1 4.4 %copy-start.33 = (pred[128]{0:T(512)(128)(4,1)S(1)}, pred[128]{0:T(512)(128)(4,1)}, u32[]{:S(2)}) copy-start(pred[128]{0:T(512)(128)(4,1)} %broadcast_compare_fusion.1) | copy-start | bytes 388
  150.8 3.8 %copy-start.2 = (bf16[1024,2048]{1,0:T(8,128)(2,1)S(1)}, bf16[1024,2048]{1,0:T(8,128)(2,1)}, u32[]{:S(2)}) copy-start(bf16[1024,2048]{1,0:T(8,128)(2,1)} %all-gather.8.cloned.1.call-done) | copy-start | bytes 12582916
  157.1 103.1 %copy-start.1 = (bf16[16,10240]{1,0:T(8,128)(2,1)S(1)}, bf16[16,10240]{1,0:T(8,128)(2,1)}, u32[]{:S(2)}) copy-start(bf16[16,10240]{1,0:T(8,128)(2,1)} %param.15) | copy-start | bytes 983044
  (23 other events, 33.9 us)
Sparse Core Ops, SparseCore 0:
  9.7 17.9 all-gather.5
  29.2 14.8 all-gather.7
  45.6 11.7 all-gather.9
  150.8 7.4 reduce-scatter.1
where the time goes:
time: 267 us
  blocking collectives  115 us (43%)
  other arithmetic  46.7 us (17%)
  local copies, waits for them, and re-layouts  45.3 us (17%)
  matrix products  17.2 us (6%)
  starting transfers between devices  15.4 us (6%)
  between operations  14.7 us (6%)
  waiting for transfers between devices  12.4 us (5%)
    psum x1, blocking collectives, local(): summed = lax.psum(local_rows, 'dp')  100 us
    convert_element_type x1, other arithmetic, first_section(): return jnp.maximum(summed, 0.0).astype(jnp.bfloat16)  28.5 us
    squeeze x3, local copies, waits for them, and re-layouts, phase_rows(): odd = split[:, :, 1]  11.7 us
    all_to_all x1, waiting for transfers between devices, local(): lax.all_to_all(outgoing, 'dp', split_axis=0, concat_axis=0, tiled=True)  10.2 us
    all_to_all x1, starting transfers between devices, local(): lax.all_to_all(sent_frames, 'dp', split_axis=0, concat_axis=0, tiled=True)  8.31 us
    convert_element_type x2, other arithmetic, depth_stride(): return summed.astype(jnp.bfloat16)  8.07 us
    all_to_all x1, starting transfers between devices, local(): lax.all_to_all(outgoing, 'dp', split_axis=0, concat_axis=0, tiled=True)  6.91 us
    concatenate x3, local copies, waits for them, and re-layouts, phase_rows(): before = jnp.concatenate([jnp.zeros_like(odd[:, :1]), odd[:, :-1]], axis=1)  6.78 us
  transfers between devices with their start and end apart: 6, of which 1 were waited for; matrix products, arithmetic and copies ran while one was open for 39% of the time, Pallas kernels for 0%

commit v1 on v0

--- a/solution.py
+++ b/solution.py
@@ -98,55 +98,140 @@
     return summed.reshape(upstream.shape[0], -1)
 
 
-def module_pass(
-    features, keep, cotangent, norm_gain, up_weight, depth_kernel, conv_gain, down_weight, span
-):
-    width = features.shape[1]
+def module_forward(features, keep, gain_front, up_mine, up_other, kernel_full, gain_back, me, span):
     values = features.astype(jnp.float32)
     centred = values - jnp.mean(values, axis=1, keepdims=True)
     scale_one = lax.rsqrt(jnp.mean(centred * centred, axis=1, keepdims=True) + EPSILON)
     standard = centred * scale_one
-    normed = (standard * norm_gain.astype(jnp.float32)).astype(jnp.bfloat16)
-    projected = jnp.dot(normed, up_weight, preferred_element_type=jnp.float32)
-    value_half = projected[:, :width]
-    gate_half = jax.nn.sigmoid(projected[:, width:])
+    normed = (standard * gain_front).astype(jnp.bfloat16)
+    mine = jnp.dot(normed, up_mine, preferred_element_type=jnp.float32)
+    other = jnp.dot(normed, up_other, preferred_element_type=jnp.float32)
+    value_half = jnp.where(me == 0, mine, other)
+    gate_half = jax.nn.sigmoid(jnp.where(me == 0, other, mine))
     row_keep = keep[:, None]
     gated = (row_keep * value_half * gate_half).astype(jnp.bfloat16)
-    depthwise = depth_forward(gated, depth_kernel, span)
+    depthwise = depth_forward(gated, kernel_full, span)
     centred_two = depthwise - jnp.mean(depthwise, axis=1, keepdims=True)
     scale_two = lax.rsqrt(jnp.mean(centred_two * centred_two, axis=1, keepdims=True) + EPSILON)
     standard_two = centred_two * scale_two
-    active = standard_two * conv_gain.astype(jnp.float32)
+    active = standard_two * gain_back
     swish_gate = jax.nn.sigmoid(active)
     hidden = (active * swish_gate).astype(jnp.bfloat16)
-    mixed = jnp.dot(hidden, down_weight, preferred_element_type=jnp.float32)
+    return hidden, (values, standard, scale_one, value_half, gate_half, scale_two, standard_two, active, swish_gate)
+
+
+def module_backward(hidden, saved, keep, cotangent, gain_front, up_mine, up_other, kernel_full, gain_back, down_mine, down_other, me, span):
+    values, standard, scale_one, value_half, gate_half, scale_two, standard_two, active, swish_gate = saved
+    row_keep = keep[:, None]
+    half = down_mine.shape[0]
+    hidden_mine = lax.dynamic_slice_in_dim(hidden, me * half, half, axis=1)
+    hidden_other = lax.dynamic_slice_in_dim(hidden, (1 - me) * half, half, axis=1)
+    mixed = jnp.dot(hidden_mine, down_mine, preferred_element_type=jnp.float32) + jnp.dot(
+        hidden_other, down_other, preferred_element_type=jnp.float32
+    )
     layer_out = (row_keep * (values + mixed)).astype(jnp.bfloat16)
     back_out = jnp.where(row_keep > 0, cotangent, jnp.zeros_like(cotangent))
-    back_hidden = lax.dot_general(
-        back_out, down_weight, (((1,), (1,)), ((), ())), preferred_element_type=jnp.float32
+    across = (((1,), (1,)), ((), ()))
+    back_mine = lax.dot_general(back_out, down_mine, across, preferred_element_type=jnp.float32)
+    back_other = lax.dot_general(back_out, down_other, across, preferred_element_type=jnp.float32)
+    back_hidden = jnp.concatenate(
+        [jnp.where(me == 0, back_mine, back_other), jnp.where(me == 0, back_other, back_mine)], axis=1
     )
     back_active = back_hidden * (swish_gate + active * swish_gate * (1.0 - swish_gate))
-    gain_back = back_active * conv_gain.astype(jnp.float32)
+    gain_up = back_active * gain_back
     back_depth = scale_two * (
-        gain_back
-        - jnp.mean(gain_back, axis=1, keepdims=True)
-        - standard_two * jnp.mean(gain_back * standard_two, axis=1, keepdims=True)
-    )
-    back_gated = row_keep * depth_backward(back_depth, depth_kernel, span)
-    back_proj = jnp.concatenate(
-        [back_gated * gate_half, back_gated * value_half * gate_half * (1.0 - gate_half)], axis=1
-    ).astype(jnp.bfloat16)
+        gain_up
+        - jnp.mean(gain_up, axis=1, keepdims=True)
+        - standard_two * jnp.mean(gain_up * standard_two, axis=1, keepdims=True)
+    )
+    back_gated = row_keep * depth_backward(back_depth, kernel_full, span)
+    back_value = (back_gated * gate_half).astype(jnp.bfloat16)
+    back_gate = (back_gated * value_half * gate_half * (1.0 - gate_half)).astype(jnp.bfloat16)
     back_normed = lax.dot_general(
-        back_proj, up_weight, (((1,), (1,)), ((), ())), preferred_element_type=jnp.float32
-    )
-    gain_front = back_normed * norm_gain.astype(jnp.float32)
+        jnp.where(me == 0, back_value, back_gate), up_mine, across, preferred_element_type=jnp.float32
+    ) + lax.dot_general(
+        jnp.where(me == 0, back_gate, back_value), up_other, across, preferred_element_type=jnp.float32
+    )
+    gain_in = back_normed * gain_front
     back_input = scale_one * (
-        gain_front
-        - jnp.mean(gain_front, axis=1, keepdims=True)
-        - standard * jnp.mean(gain_front * standard, axis=1, keepdims=True)
+        gain_in
+        - jnp.mean(gain_in, axis=1, keepdims=True)
+        - standard * jnp.mean(gain_in * standard, axis=1, keepdims=True)
     )
     grad_input = (back_out.astype(jnp.float32) + back_input).astype(jnp.bfloat16)
-    return (layer_out, grad_input, hidden, back_out)
+    return layer_out, grad_input
+
+
+def swap_cores(block):
+    return lax.ppermute(block, "fsdp", [(0, 1), (1, 0)])
+
+
+def swap_bit(block, bit, groups):
+    return lax.ppermute(block, "dp", [(i, i ^ (1 << bit)) for i in range(groups)])
+
+
+def pick(block, index):
+    return lax.dynamic_index_in_dim(block, index, axis=0, keepdims=False)
+
+
+def halve(total, bit, groups):
+    side = (lax.axis_index("dp") >> bit) & 1
+    pair = total.reshape(2, total.shape[0] // 2, total.shape[1])
+    given = swap_bit(pick(pair, 1 - side).astype(jnp.bfloat16), bit, groups)
+    return pick(pair, side) + given.astype(jnp.float32)
+
+
+def double(block, bit, groups):
+    side = (lax.axis_index("dp") >> bit) & 1
+    given = swap_bit(block, bit, groups)
+    return jnp.concatenate(
+        [jnp.where(side == 0, block, given), jnp.where(side == 0, given, block)], axis=0
+    )
+
+
+def sum_over_dp(total, scale, groups):
+    bits = groups.bit_length() - 1
+    half = total.shape[1] // 2
+    orders = ([0, 1], [1, 0])
+    parts = [total[:, :half], total[:, half:]]
+    for step in range(2):
+        parts = [halve(part, order[step], groups) for part, order in zip(parts, orders)]
+    joined = jnp.concatenate(parts, axis=1)
+    for bit in range(2, bits - 1):
+        joined = halve(joined, bit, groups)
+    rounded = joined.astype(jnp.bfloat16)
+    given = swap_bit(rounded, bits - 1, groups)
+    block = ((rounded.astype(jnp.float32) + given.astype(jnp.float32)) * scale).astype(jnp.bfloat16)
+    for bit in reversed(range(2, bits - 1)):
+        block = double(block, bit, groups)
+    parts = [block[:, :half], block[:, half:]]
+    for step in reversed(range(2)):
+        parts = [double(part, order[step], groups) for part, order in zip(parts, orders)]
+    return jnp.concatenate(parts, axis=1).astype(jnp.float32)
+
+
+def pack_rows(arrays):
+    flat = []
+    for array in arrays:
+        rows = array.reshape(-1, 128)
+        flat.append(jnp.pad(rows, ((0, -rows.shape[0] % 16), (0, 0))))
+    return jnp.concatenate(flat, axis=0)
+
+
+def unpack_rows(packed, arrays):
+    out = []
+    at = 0
+    for array in arrays:
+        count = array.size // 128
+        out.append(packed[at : at + count].reshape(array.shape))
+        at += count + (-count % 16)
+    return out
+
+
+def both(mine, other, me, axis):
+    return jnp.concatenate(
+        [jnp.where(me == 0, mine, other), jnp.where(me == 0, other, mine)], axis=axis
+    )
 
 
 def local(
@@ -168,74 +253,64 @@
 ):
     groups = lax.axis_size("dp")
     members = lax.axis_size("fsdp")
+    me = lax.axis_index("fsdp")
     span = PANEL // 8
     panel_count = cotangent.shape[0] // span
+    width_in = mel_panels.shape[1]
     destinations = jnp.arange(groups, dtype=jnp.int32)
     selected = (target[None, :] == destinations[:, None]) & (frames[None, :] > 0)
+    carried = jnp.concatenate(
+        [mel_panels, jnp.broadcast_to(frames[:, None], (frames.shape[0], 128)).astype(jnp.bfloat16)], axis=1
+    )
     outgoing = jnp.dot(
-        selected.astype(jnp.bfloat16), mel_panels, preferred_element_type=jnp.float32
+        selected.astype(jnp.bfloat16), carried, preferred_element_type=jnp.float32
     ).astype(jnp.bfloat16)
-    sent_frames = jnp.sum(jnp.where(selected, frames[None, :], 0), axis=1)
-    incoming, got_frames = (
-        lax.all_to_all(outgoing, "dp", split_axis=0, concat_axis=0, tiled=True),
-        lax.all_to_all(sent_frames, "dp", split_axis=0, concat_axis=0, tiled=True),
-    )
+    incoming = lax.all_to_all(outgoing, "dp", split_axis=0, concat_axis=0, tiled=True)
+    got_frames = incoming[:, width_in].astype(jnp.int32)
     present = got_frames > 0
     position = jnp.cumsum(present.astype(jnp.int32)) - 1
     places = jnp.arange(panel_count, dtype=jnp.int32)
     placing = (position[None, :] == places[:, None]) & present[None, :]
     panels = jnp.dot(
-        placing.astype(jnp.bfloat16), incoming, preferred_element_type=jnp.float32
+        placing.astype(jnp.bfloat16), incoming[:, :width_in], preferred_element_type=jnp.float32
     ).astype(jnp.bfloat16)
     lengths = jnp.sum(jnp.where(placing, got_frames[None, :], 0), axis=1).astype(jnp.int32)
-    first_full, depth_one, point_one, depth_two, point_two, gain_front, kernel_full, gain_back = (
-        lax.all_gather(conv_first, "fsdp", axis=1, tiled=True),
-        lax.all_gather(depth_a, "fsdp", axis=1, tiled=True),
-        lax.all_gather(point_a, "fsdp", axis=1, tiled=True),
-        lax.all_gather(depth_b, "fsdp", axis=1, tiled=True),
-        lax.all_gather(point_b, "fsdp", axis=1, tiled=True),
-        lax.all_gather(norm_gain, "fsdp", axis=0, tiled=True),
-        lax.all_gather(depth_kernel, "fsdp", axis=1, tiled=True),
-        lax.all_gather(conv_gain, "fsdp", axis=0, tiled=True),
-    )
-    per_block = math.gcd(panel_count, 16)
-
-    def sub_block(block_args):
-        return subsample(
-            block_args[0], block_args[1], first_full, depth_one, point_one, depth_two, point_two
-        )
-
-    flat_rows = lax.map(
-        sub_block,
-        (
-            panels.reshape(panel_count // per_block, per_block, -1),
-            lengths.reshape(panel_count // per_block, per_block),
-        ),
-    )
-    flat_rows = flat_rows.reshape(panel_count * span, -1)
-    features = jnp.dot(
-        flat_rows,
-        lax.all_gather(linear_weight, "fsdp", axis=1, tiled=True),
-        preferred_element_type=jnp.float32,
-    ).astype(jnp.bfloat16)
+    small = [conv_first, depth_a, point_a, depth_b, point_b, norm_gain, depth_kernel, conv_gain]
+    packed = swap_cores(pack_rows(small))
+    linear_other = swap_cores(linear_weight)
+    up_other = swap_cores(up_weight)
+    down_other = swap_cores(down_weight)
+    cotangent_other = swap_cores(cotangent)
+    first_full, depth_one, point_one, depth_two, point_two, gain_front, kernel_full, gain_back = [
+        both(mine, other, me, mine.ndim - 1) for mine, other in zip(small, unpack_rows(packed, small))
+    ]
+    gain_front = gain_front.astype(jnp.float32)
+    gain_back = gain_back.astype(jnp.float32)
+    flat_rows = subsample(panels, lengths, first_full, depth_one, point_one, depth_two, point_two)
+    features = both(
+        jnp.dot(flat_rows, linear_weight, preferred_element_type=jnp.float32).astype(jnp.bfloat16),
+        jnp.dot(flat_rows, linear_other, preferred_element_type=jnp.float32).astype(jnp.bfloat16),
+        me,
+        1,
+    )
     keep = (jnp.arange(span)[None, :] < (lengths // 8)[:, None]).reshape(-1).astype(jnp.float32)
-    up_full, down_full = (
-        lax.all_gather(up_weight, "fsdp", axis=1, tiled=True),
-        lax.all_gather(down_weight, "fsdp", axis=0, tiled=True),
-    )
-    layer_out, grad_input, hidden, back_out = module_pass(
-        features, keep, cotangent, gain_front, up_full, kernel_full, gain_back, down_full, span
-    )
-    local_rows = lax.psum_scatter(
-        lax.dot_general(
-            hidden, back_out, (((0,), (0,)), ((), ())), preferred_element_type=jnp.float32
-        ).astype(jnp.bfloat16),
-        "fsdp",
-        scatter_dimension=0,
-        tiled=True,
-    ).astype(jnp.float32)
-    summed = lax.psum(local_rows, "dp")
-    grad_down = summed / jnp.sqrt(jnp.float32(cotangent.shape[0] * groups * members))
+    hidden, saved = module_forward(
+        features, keep, gain_front, up_weight, up_other, kernel_full, gain_back, me, span
+    )
+    half = hidden.shape[1] // members
+    kept = hidden * keep[:, None].astype(jnp.bfloat16)
+    kept_mine = lax.dynamic_slice_in_dim(kept, me * half, half, axis=1)
+    kept_other = swap_cores(lax.dynamic_slice_in_dim(kept, (1 - me) * half, half, axis=1))
+    down_rows = (((0,), (0,)), ((), ()))
+    product = lax.dot_general(
+        kept_mine, cotangent, down_rows, preferred_element_type=jnp.float32
+    ) + lax.dot_general(kept_other, cotangent_other, down_rows, preferred_element_type=jnp.float32)
+    scale = 1.0 / math.sqrt(cotangent.shape[0] * groups * members)
+    grad_down = sum_over_dp(product, scale, groups)
+    layer_out, grad_input = module_backward(
+        hidden, saved, keep, cotangent, gain_front, up_weight, up_other, kernel_full, gain_back,
+        down_weight, down_other, me, span,
+    )
     return (layer_out, grad_input, grad_down)
 
 

time: 267 us -> 193 us (0.72)
  blocking collectives: 115 us -> 0 us
  waiting for transfers between devices: 12.4 us -> 32.9 us
  between operations: 14.7 us -> 2.01 us
  matrix products: 17.2 us -> 27.8 us
  local copies, waits for them, and re-layouts: 45.3 us -> 55.9 us
  starting transfers between devices: 15.4 us -> 23.8 us
  other arithmetic: 46.7 us -> 49.6 us
    psum x1 -> x0, blocking collectives: 100 us -> none  [local(): summed = lax.psum(local_rows, 'dp')]
    ppermute x0 -> x17, waiting for transfers between devices: none -> 26.3 us  [the longest x11 26.2 us: swap_bit(): return lax.ppermute(block, 'dp', [(i, i ^ 1 << bit) for i in range(groups)])]
    ppermute x0 -> x17, starting transfers between devices: none -> 16 us  [the longest x11 14.3 us: swap_bit(): return lax.ppermute(block, 'dp', [(i, i ^ 1 << bit) for i in range(groups)])]
    all_gather x8 -> x0, blocking collectives: 14.7 us -> none  [the longest x1 2.02 us: local(): lax.all_gather(point_b, 'fsdp', axis=1, tiled=True)]
    dot_general x8 -> x14, matrix products: 14.6 us -> 25.1 us  [the longest x1 2.9 us: module_forward(): mine = jnp.dot(normed, up_mine, preferred_element_type=jnp.float32)]
    all_to_all x1 -> x0, starting transfers between devices: 8.31 us -> none  [local(): lax.all_to_all(sent_frames, 'dp', split_axis=0, concat_axis=0, tiled=True)]
    unnamed x86 -> x110, local copies, waits for them, and re-layouts: 6.27 us -> 11.8 us
    another operation x0 -> x2, local copies, waits for them, and re-layouts: none -> 4.27 us  [the longest x1 3.51 us: phase_rows(): split = source.reshape((shape_in[0], shape_in[1] // 2, 2) + shape_in[2:])]
  transfers between devices with their start and end apart: 6 -> 18, of which waited for: 1 -> 11; matrix products, arithmetic and copies ran while one was open for 39% -> 61% of each run, Pallas kernels for 0% -> 0%
where the time goes in v1:
time: 193 us; the launch traced here: 192 us
  local copies, waits for them, and re-layouts  55.9 us (29%)
  other arithmetic  49.6 us (26%)
  waiting for transfers between devices  32.9 us (17%)
  matrix products  27.8 us (14%)
  starting transfers between devices  23.8 us (12%)
  between operations  2.01 us (1%)
    convert_element_type x1, other arithmetic, first_section(): return jnp.maximum(summed, 0.0).astype(jnp.bfloat16)  27.4 us
    ppermute x11, waiting for transfers between devices, swap_bit(): return lax.ppermute(block, 'dp', [(i, i ^ 1 << bit) for i in range(groups)])  26.2 us
    ppermute x11, starting transfers between devices, swap_bit(): return lax.ppermute(block, 'dp', [(i, i ^ 1 << bit) for i in range(groups)])  14.3 us
    unnamed x110, local copies, waits for them, and re-layouts  11.8 us
    squeeze x3, local copies, waits for them, and re-layouts, phase_rows(): odd = split[:, :, 1]  11.6 us
    convert_element_type x2, other arithmetic, depth_stride(): return summed.astype(jnp.bfloat16)  8.06 us
    all_to_all x1, starting transfers between devices, local(): lax.all_to_all(outgoing, 'dp', split_axis=0, concat_axis=0, tiled=True)  7.86 us
    concatenate x3, local copies, waits for them, and re-layouts, phase_rows(): before = jnp.concatenate([jnp.zeros_like(odd[:, :1]), odd[:, :-1]], axis=1)  6.78 us
  transfers between devices with their start and end apart: 18, of which 11 were waited for; matrix products, arithmetic and copies ran while one was open for 61% of the time, Pallas kernels for 0%

profile of v1, /device:TPU:0, one launch (start us, length us, event | category | flops | bytes accessed | tf_op | source)
XLA Modules:
  0.0 192.0 jit_solution(12567336449859802365)
XLA Ops:
  12.2 7.9 %all-to-all-start = ((bf16[16,2,5184]{2,1,0:T(2,128)(2,1)}), bf16[16,2,5184]{2,1,0:T(2,128)(2,1)S(1)}, u32[]{:S(2)}, u32[]{:S(2)}) async-start(bf16[16,2,5184]{2,1,0:T(2,128)(2,1)} %reshape.732), calls=%async_computation | async-start | bytes 671744 | tf_op jit(solution)/shard_map/all_to_all | solution.py:268
  25.6 6.7 %all-to-all-done = bf16[16,2,5184]{2,1,0:T(2,128)(2,1)S(1)} async-done(((bf16[16,2,5184]{2,1,0:T(2,128)(2,1)}), bf16[16,2,5184]{2,1,0:T(2,128)(2,1)S(1)}, u32[]{:S(2)}, u32[]{:S(2)}) %all-to-all-start) | async-done | bytes 331808 | tf_op jit(solution)/shard_map/all_to_all | solution.py:268
  41.3 27.4 %maximum_convert_fusion = bf16[8,32,2,40,256]{4,1,3,0,2:T(8,128)(2,1)} fusion(f32[256]{0:T(256)S(1)} %bitcast.306, f32[8,32,2,40]{1,3,0,2:T(8,128)S(1)} %copy.200, f32[256]{0:T(256)S(1)} %bitcast.307, f32[8,32,2,40]{1,3,0,2:T(8,128)S(1)} %copy.198, f32[256]{0:T(256)S(1)} %bitcast.305, f32[8,32,2,40]{1,3,0,2:T(8,128)S(1)} %copy.196, f32[256]{0:T(256)S(1)} %bitcast.304, ...), kind=kLoop, calls=%fused_computation | loop fusion | flops 99614720 | bytes 11232256 | tf_op jit(solution)/shard_map/convert_element_type | solution.py:43
  68.7 11.0 %slice_bitcast_fusion.16 = (bf16[8,32,40,256]{3,1,2,0:T(8,128)(2,1)}, bf16[8,32,1,40,256]{4,1,3,0,2:T(8,128)(2,1)}, bf16[8,32,1,40,256]{4,1,3,0,2:T(8,128)(2,1)}) fusion(bf16[8,32,2,40,256]{4,1,3,0,2:T(8,128)(2,1)} %maximum_convert_fusion), kind=kLoop, calls=%fused_computation.401 | loop fusion | bytes 26214400 | tf_op jit(solution)/shard_map/squeeze | solution.py:19
  79.7 6.0 %concatenate.115 = bf16[8,32,40,256]{3,1,2,0:T(8,128)(2,1)S(1)} pad(bf16[8,31,40,256]{3,1,2,0:T(8,128)(2,1)} %bitcast.233, bf16[]{:T(256)} %constant.93.clone.1), padding=0_0x1_0x0_0x0_0 | pad | bytes 10321922 | tf_op jit(solution)/shard_map/concatenate | solution.py:20
  86.1 3.1 %copy-done = bf16[8,32,1,40,256]{4,1,3,0,2:T(8,128)(2,1)S(1)} copy-done((bf16[8,32,1,40,256]{4,1,3,0,2:T(8,128)(2,1)S(1)}, bf16[8,32,1,40,256]{4,1,3,0,2:T(8,128)(2,1)}, u32[]{:S(2)}) %copy-start) | copy-done | bytes 5242904
  93.7 6.9 %fusion.4 = bf16[8,32,20,256]{3,1,2,0:T(8,128)(2,1)S(1)} fusion(bf16[8,32,20,2,256]{4,1,3,2,0:T(8,128)(2,1)S(1)} %bitcast.230, bf16[8,32,20,2,256]{4,1,3,2,0:T(8,128)(2,1)S(1)} %bitcast.226, bf16[8,32,20,2,256]{4,1,3,2,0:T(8,128)(2,1)S(1)} %bitcast.232, f32[256]{0:T(256)S(1)} %bitcast.297, f32[256]{0:T(256)S(1)} %bitcast.298, f32[256]{0:T(256)S(1)} %bitcast.296, ...), kind=kLoop, calls=%fused_computation.9 | loop fusion | flops 35389440 | bytes 25830400 | tf_op jit(solution)/shard_map/convert_element_type | solution.py:56
  100.6 3.3 %copy.205 = bf16[8,32,20,256]{3,2,1,0:T(8,128)(2,1)} copy(bf16[8,32,20,256]{3,1,2,0:T(8,128)(2,1)S(1)} %fusion.4) | data formatting | bytes 5242880 | tf_op jit(solution)/shard_map/convert_element_type | solution.py:56
  103.9 3.6 %reshape.663 = bf16[5120,256]{1,0:T(8,128)(2,1)S(1)} reshape(bf16[8,32,20,256]{3,2,1,0:T(8,128)(2,1)} %copy.205) | data formatting | bytes 5242880 | tf_op jit(solution)/shard_map/reshape | solution.py:61
  107.6 2.3 %fusion.1 = bf16[5120,256]{1,0:T(8,128)(2,1)} fusion(bf16[5120,256]{1,0:T(8,128)(2,1)S(1)} %reshape.663, bf16[256,128]{1,0:T(8,128)(2,1)S(1)} %get-tuple-element.55, bf16[256,128]{1,0:T(8,128)(2,1)S(1)} %get-tuple-element.56), kind=kOutput, calls=%fused_computation.5 | convolution fusion | flops 673972224 | bytes 5373952 | tf_op jit(solution)/shard_map/dot_general | solution.py:61
  109.9 3.5 %reshape_reshape.6 = bf16[8,16,2,20,256]{4,3,2,1,0:T(8,128)(2,1)S(1)} reshape(bf16[5120,256]{1,0:T(8,128)(2,1)} %fusion.1) | data formatting | bytes 5242880 | tf_op jit(solution)/shard_map/reshape;reshape | solution.py:17
  126.1 2.3 %broadcast_select_fusion.15 = (bf16[128,512]{1,0:T(8,128)(2,1)S(1)}, bf16[128,512]{1,0:T(8,128)(2,1)S(1)}) fusion(bf16[128,512]{1,0:T(8,128)(2,1)S(1)} %convolution_convert_fusion.3, pred[]{:T(512)S(6)} %eq.26, bf16[128,2560]{1,0:T(8,128)(2,1)S(1)} %reshape_reshape.7, bf16[2560,512]{1,0:T(8,128)(2,1)} %collective-permute-done.1), kind=kOutput, calls=%fused_computation.179 | convolution fusion | flops 335740928 | bytes 3670017 | tf_op jit(solution)/shard_map/dot_general | solution.py:292
  130.9 2.9 %multiply_convert_fusion.3 = (bf16[128,1024]{1,0:T(8,128)(2,1)S(1)}, f32[128,1024]{1,0:T(8,128)}) fusion(f32[128]{0:T(128)S(1)} %reshape.678, f32[128,1024]{1,0:T(8,128)S(1)} %fusion.169, pred[]{:T(512)S(6)} %eq.26, bf16[1024,1024]{1,0:T(8,128)(2,1)} %param.25, f32[1024]{0:T(1024)S(1)} %copy-done.15, f32[128]{0:T(128)S(1)} %add_rsqrt_fusion.1, ...), kind=kOutput, calls=%fused_computation.118 | convolution fusion | flops 270532608 | bytes 3675649 | tf_op jit(solution)/shard_map/dot_general | solution.py:107
  136.9 2.4 %fusion.64 = f32[128,1024]{1,0:T(8,128)S(1)} fusion(bf16[1024,1024]{1,0:T(8,128)(2,1)} %param.25, bf16[128,1024]{1,0:T(8,128)(2,1)S(1)} %get-tuple-element.21, bf16[128,1024]{1,0:T(8,128)(2,1)S(1)} %get-tuple-element.20, pred[]{:T(512)S(6)} %eq.26), kind=kOutput, calls=%fused_computation.143 | convolution fusion | flops 268566528 | bytes 3145729 | tf_op jit(solution)/shard_map/dot_general | solution.py:150
  142.1 2.8 %fusion.173 = (f32[128]{0:T(128)S(1)}, f32[128]{0:T(128)S(1)}, f32[128,1024]{1,0:T(8,128)S(1)}) fusion(f32[128]{0:T(128)S(1)} %add_rsqrt_fusion.1, f32[128]{0:T(128)S(1)} %broadcast_multiply_fusion.6, bf16[128,512]{1,0:T(8,128)(2,1)S(1)} %get-tuple-element.37, bf16[128,512]{1,0:T(8,128)(2,1)S(1)} %get-tuple-element.36, f32[1024]{0:T(1024)S(1)} %copy-done.15, ...), kind=kOutput, calls=%fused_computation.402 | convolution fusion | flops 270008064 | bytes 3938305 | tf_op jit(solution)/shard_map/dot_general | solution.py:152
  145.8 4.5 %collective-permute-done.6 = bf16[256,512]{1,0:T(8,128)(2,1)S(1)} collective-permute-done((bf16[256,512]{1,0:T(8,128)(2,1)S(1)}, bf16[256,512]{1,0:T(8,128)(2,1)S(1)}, u32[]{:S(2)}, u32[]{:S(2)}) %collective-permute-start.6) | collective-permute-done | bytes 262176 | tf_op jit(solution)/shard_map/ppermute | solution.py:170
  151.2 2.8 %collective-permute-done.8 = bf16[256,512]{1,0:T(8,128)(2,1)S(1)} collective-permute-done((bf16[256,512]{1,0:T(8,128)(2,1)S(1)}, bf16[256,512]{1,0:T(8,128)(2,1)S(1)}, u32[]{:S(2)}, u32[]{:S(2)}) %collective-permute-start.8) | collective-permute-done | bytes 262176 | tf_op jit(solution)/shard_map/ppermute | solution.py:170
  156.3 2.9 %collective-permute-done.9 = bf16[128,512]{1,0:T(8,128)(2,1)S(1)} collective-permute-done((bf16[128,512]{1,0:T(8,128)(2,1)S(1)}, bf16[128,512]{1,0:T(8,128)(2,1)S(1)}, u32[]{:S(2)}, u32[]{:S(2)}) %collective-permute-start.9) | collective-permute-done | bytes 131104 | tf_op jit(solution)/shard_map/ppermute | solution.py:170
  161.9 2.4 %collective-permute-done.10 = bf16[64,1024]{1,0:T(8,128)(2,1)S(1)} collective-permute-done((bf16[64,1024]{1,0:T(8,128)(2,1)S(1)}, bf16[64,1024]{1,0:T(8,128)(2,1)S(1)}, u32[]{:S(2)}, u32[]{:S(2)}) %collective-permute-start.10) | collective-permute-done | bytes 131104 | tf_op jit(solution)/shard_map/ppermute | solution.py:170
  168.2 2.4 %collective-permute-done.11 = bf16[64,1024]{1,0:T(8,128)(2,1)S(1)} collective-permute-done((bf16[64,1024]{1,0:T(8,128)(2,1)S(1)}, bf16[64,1024]{1,0:T(8,128)(2,1)S(1)}, u32[]{:S(2)}, u32[]{:S(2)}) %collective-permute-start.11) | collective-permute-done | bytes 131104 | tf_op jit(solution)/shard_map/ppermute | solution.py:170
  170.7 2.4 %collective-permute-start.12 = (bf16[64,1024]{1,0:T(8,128)(2,1)S(1)}, bf16[64,1024]{1,0:T(8,128)(2,1)S(1)}, u32[]{:S(2)}, u32[]{:S(2)}) collective-permute-start(bf16[64,1024]{1,0:T(8,128)(2,1)S(1)} %multiply_convert_fusion.4), channel_id=1, source_target_pairs={{0,8},{2,10},{4,12},{6,14},{8,0},{10,2},{12,4},{14,6},{16,24},{18,... | collective-permute-start | bytes 393224 | tf_op jit(solution)/shard_map/ppermute | solution.py:170
  173.1 2.9 %collective-permute-done.12 = bf16[64,1024]{1,0:T(8,128)(2,1)S(1)} collective-permute-done((bf16[64,1024]{1,0:T(8,128)(2,1)S(1)}, bf16[64,1024]{1,0:T(8,128)(2,1)S(1)}, u32[]{:S(2)}, u32[]{:S(2)}) %collective-permute-start.12) | collective-permute-done | bytes 131104 | tf_op jit(solution)/shard_map/ppermute | solution.py:170
  178.6 3.8 %collective-permute-done.13 = bf16[128,512]{1,0:T(8,128)(2,1)S(1)} collective-permute-done((bf16[128,512]{1,0:T(8,128)(2,1)S(1)}, bf16[128,512]{1,0:T(8,128)(2,1)S(1)}, u32[]{:S(2)}, u32[]{:S(2)}) %collective-permute-start.13) | collective-permute-done | bytes 131104 | tf_op jit(solution)/shard_map/ppermute | solution.py:170
  186.1 2.7 %collective-permute-done.14 = bf16[256,512]{1,0:T(8,128)(2,1)S(1)} collective-permute-done((bf16[256,512]{1,0:T(8,128)(2,1)S(1)}, bf16[256,512]{1,0:T(8,128)(2,1)S(1)}, u32[]{:S(2)}, u32[]{:S(2)}) %collective-permute-start.14) | collective-permute-done | bytes 262176 | tf_op jit(solution)/shard_map/ppermute | solution.py:170
  (276 shorter events, 71.2 us)
Async XLA Ops:
  0.6 20.6 %copy-start.17 = (bf16[9,128]{1,0:T(8,128)(2,1)S(1)}, bf16[9,128]{1,0:T(8,128)(2,1)}, u32[]{:S(2)}) copy-start(bf16[9,128]{1,0:T(8,128)(2,1)} %param.18) | copy-start | bytes 6916
  0.6 23.6 %copy-start.9 = (bf16[9,512]{1,0:T(8,128)(2,1)S(1)}, bf16[9,512]{1,0:T(8,128)(2,1)}, u32[]{:S(2)}) copy-start(bf16[9,512]{1,0:T(8,128)(2,1)} %param.26) | copy-start | bytes 27652
  0.7 24.2 %copy-start.7 = (bf16[256,128]{1,0:T(8,128)(2,1)S(1)}, bf16[256,128]{1,0:T(8,128)(2,1)}, u32[]{:S(2)}) copy-start(bf16[256,128]{1,0:T(8,128)(2,1)} %param.20) | copy-start | bytes 196612
  0.7 24.2 %copy-start.8 = (bf16[256,128]{1,0:T(8,128)(2,1)S(1)}, bf16[256,128]{1,0:T(8,128)(2,1)}, u32[]{:S(2)}) copy-start(bf16[256,128]{1,0:T(8,128)(2,1)} %param.22) | copy-start | bytes 196612
  0.7 22.3 %copy-start.34 = (bf16[512]{0:T(512)(128)(2,1)S(1)}, bf16[512]{0:T(512)(128)(2,1)}, u32[]{:S(2)}) copy-start(bf16[512]{0:T(512)(128)(2,1)} %param.24) | copy-start | bytes 3076
  0.7 22.3 %copy-start.35 = (bf16[512]{0:T(512)(128)(2,1)S(1)}, bf16[512]{0:T(512)(128)(2,1)}, u32[]{:S(2)}) copy-start(bf16[512]{0:T(512)(128)(2,1)} %param.27) | copy-start | bytes 3076
  6.7 14.5 %collective-permute-start = (bf16[640,128]{1,0:T(8,128)(2,1)S(1)}, bf16[640,128]{1,0:T(8,128)(2,1)S(1)}, u32[]{:S(2)}, u32[]{:S(2)}) collective-permute-start(bf16[640,128]{1,0:T(8,128)(2,1)S(1)} %constant_dynamic-update-slice_fusion), channel_id=1, source_target_pairs={{0,1},{1,0},{2,3},{3,2},{4,5},{5,4},{6,7},{7,6},{8,9},{9,8},{10,11... | collective-permute-start | bytes 491528 | tf_op jit(solution)/shard_map/ppermute | solution.py:166
  12.2 20.0 %all-to-all-start = ((bf16[16,2,5184]{2,1,0:T(2,128)(2,1)}), bf16[16,2,5184]{2,1,0:T(2,128)(2,1)S(1)}, u32[]{:S(2)}, u32[]{:S(2)}) async-start(bf16[16,2,5184]{2,1,0:T(2,128)(2,1)} %reshape.732), calls=%async_computation | async-start | bytes 671744 | tf_op jit(solution)/shard_map/all_to_all | solution.py:268
  20.1 106.0 %collective-permute-start.1 = (bf16[2560,512]{1,0:T(8,128)(2,1)}, bf16[2560,512]{1,0:T(8,128)(2,1)}, u32[]{:S(2)}, u32[]{:S(2)}) collective-permute-start(bf16[2560,512]{1,0:T(8,128)(2,1)} %param.23), channel_id=1, source_target_pairs={{0,1},{1,0},{2,3},{3,2},{4,5},{5,4},{6,7},{7,6},{8,9},{9,8},{10,11... | collective-permute-start | bytes 7864328 | tf_op jit(solution)/shard_map/ppermute | solution.py:166
  20.4 108.4 %collective-permute-start.2 = (bf16[1024,1024]{1,0:T(8,128)(2,1)}, bf16[1024,1024]{1,0:T(8,128)(2,1)}, u32[]{:S(2)}, u32[]{:S(2)}) collective-permute-start(bf16[1024,1024]{1,0:T(8,128)(2,1)} %param.25), channel_id=1, source_target_pairs={{0,1},{1,0},{2,3},{3,2},{4,5},{5,4},{6,7},{7,6},{8,9},{9,8},{10,11... | collective-permute-start | bytes 6291464 | tf_op jit(solution)/shard_map/ppermute | solution.py:166
  20.7 119.1 %collective-permute-start.5 = (bf16[128,1024]{1,0:T(8,128)(2,1)S(1)}, bf16[128,1024]{1,0:T(8,128)(2,1)}, u32[]{:S(2)}, u32[]{:S(2)}) collective-permute-start(bf16[128,1024]{1,0:T(8,128)(2,1)S(1)} %copy-done.2), channel_id=1, source_target_pairs={{0,1},{1,0},{2,3},{3,2},{4,5},{5,4},{6,7},{7,6},{8,9},{9,8},{10,11... | collective-permute-start | bytes 786440 | tf_op jit(solution)/shard_map/ppermute | solution.py:166
  20.9 103.5 %collective-permute-start.3 = (bf16[512,1024]{1,0:T(8,128)(2,1)}, bf16[512,1024]{1,0:T(8,128)(2,1)}, u32[]{:S(2)}, u32[]{:S(2)}) collective-permute-start(bf16[512,1024]{1,0:T(8,128)(2,1)} %param.28), channel_id=1, source_target_pairs={{0,1},{1,0},{2,3},{3,2},{4,5},{5,4},{6,7},{7,6},{8,9},{9,8},{10,11... | collective-permute-start | bytes 3145736 | tf_op jit(solution)/shard_map/ppermute | solution.py:166
  135.3 4.5 %collective-permute-start.4 = (bf16[128,512]{1,0:T(8,128)(2,1)S(1)}, bf16[128,512]{1,0:T(8,128)(2,1)S(1)}, u32[]{:S(2)}, u32[]{:S(2)}) collective-permute-start(bf16[128,512]{1,0:T(8,128)(2,1)S(1)} %constant_dynamic-slice_fusion), channel_id=1, source_target_pairs={{0,1},{1,0},{2,3},{3,2},{4,5},{5,4},{6,7},{7,6},{8,9},{9,8},{10,11... | collective-permute-start | bytes 393224 | tf_op jit(solution)/shard_map/ppermute | solution.py:166
  141.5 8.8 %collective-permute-start.6 = (bf16[256,512]{1,0:T(8,128)(2,1)S(1)}, bf16[256,512]{1,0:T(8,128)(2,1)S(1)}, u32[]{:S(2)}, u32[]{:S(2)}) collective-permute-start(bf16[256,512]{1,0:T(8,128)(2,1)S(1)} %fusion.60), channel_id=1, source_target_pairs={{0,2},{2,0},{4,6},{6,4},{8,10},{10,8},{12,14},{14,12},{16,18},{18,... | collective-permute-start | bytes 786440 | tf_op jit(solution)/shard_map/ppermute | solution.py:170
  144.9 9.1 %collective-permute-start.8 = (bf16[256,512]{1,0:T(8,128)(2,1)S(1)}, bf16[256,512]{1,0:T(8,128)(2,1)S(1)}, u32[]{:S(2)}, u32[]{:S(2)}) collective-permute-start(bf16[256,512]{1,0:T(8,128)(2,1)S(1)} %fusion.61), channel_id=1, source_target_pairs={{0,4},{2,6},{4,0},{6,2},{8,12},{10,14},{12,8},{14,10},{16,20},{18,... | collective-permute-start | bytes 786440 | tf_op jit(solution)/shard_map/ppermute | solution.py:170
  150.4 5.9 %collective-permute-start.7 = (bf16[128,512]{1,0:T(8,128)(2,1)S(1)}, bf16[128,512]{1,0:T(8,128)(2,1)S(1)}, u32[]{:S(2)}, u32[]{:S(2)}) collective-permute-start(bf16[128,512]{1,0:T(8,128)(2,1)S(1)} %fusion.68), channel_id=1, source_target_pairs={{0,4},{2,6},{4,0},{6,2},{8,12},{10,14},{12,8},{14,10},{16,20},{18,... | collective-permute-start | bytes 393224 | tf_op jit(solution)/shard_map/ppermute | solution.py:170
  154.1 5.0 %collective-permute-start.9 = (bf16[128,512]{1,0:T(8,128)(2,1)S(1)}, bf16[128,512]{1,0:T(8,128)(2,1)S(1)}, u32[]{:S(2)}, u32[]{:S(2)}) collective-permute-start(bf16[128,512]{1,0:T(8,128)(2,1)S(1)} %fusion.69), channel_id=1, source_target_pairs={{0,2},{2,0},{4,6},{6,4},{8,10},{10,8},{12,14},{14,12},{16,18},{18,... | collective-permute-start | bytes 393224 | tf_op jit(solution)/shard_map/ppermute | solution.py:170
  159.3 5.0 %collective-permute-start.10 = (bf16[64,1024]{1,0:T(8,128)(2,1)S(1)}, bf16[64,1024]{1,0:T(8,128)(2,1)S(1)}, u32[]{:S(2)}, u32[]{:S(2)}) collective-permute-start(bf16[64,1024]{1,0:T(8,128)(2,1)S(1)} %fusion.70), channel_id=1, source_target_pairs={{0,8},{2,10},{4,12},{6,14},{8,0},{10,2},{12,4},{14,6},{16,24},{18,... | collective-permute-start | bytes 393224 | tf_op jit(solution)/shard_map/ppermute | solution.py:170
  164.3 6.3 %collective-permute-start.11 = (bf16[64,1024]{1,0:T(8,128)(2,1)S(1)}, bf16[64,1024]{1,0:T(8,128)(2,1)S(1)}, u32[]{:S(2)}, u32[]{:S(2)}) collective-permute-start(bf16[64,1024]{1,0:T(8,128)(2,1)S(1)} %fusion.62), channel_id=1, source_target_pairs={{0,16},{2,18},{4,20},{6,22},{8,24},{10,26},{12,28},{14,30},{16,0},... | collective-permute-start | bytes 393224 | tf_op jit(solution)/shard_map/ppermute | solution.py:170
  170.7 5.4 %collective-permute-start.12 = (bf16[64,1024]{1,0:T(8,128)(2,1)S(1)}, bf16[64,1024]{1,0:T(8,128)(2,1)S(1)}, u32[]{:S(2)}, u32[]{:S(2)}) collective-permute-start(bf16[64,1024]{1,0:T(8,128)(2,1)S(1)} %multiply_convert_fusion.4), channel_id=1, source_target_pairs={{0,8},{2,10},{4,12},{6,14},{8,0},{10,2},{12,4},{14,6},{16,24},{18,... | collective-permute-start | bytes 393224 | tf_op jit(solution)/shard_map/ppermute | solution.py:170
  176.1 6.3 %collective-permute-start.13 = (bf16[128,512]{1,0:T(8,128)(2,1)S(1)}, bf16[128,512]{1,0:T(8,128)(2,1)S(1)}, u32[]{:S(2)}, u32[]{:S(2)}) collective-permute-start(bf16[128,512]{1,0:T(8,128)(2,1)S(1)} %get-tuple-element.30), channel_id=1, source_target_pairs={{0,4},{2,6},{4,0},{6,2},{8,12},{10,14},{12,8},{14,10},{16,20},{18,... | collective-permute-start | bytes 393224 | tf_op jit(solution)/shard_map/ppermute | solution.py:170
  177.1 6.7 %collective-permute-start.15 = (bf16[128,512]{1,0:T(8,128)(2,1)S(1)}, bf16[128,512]{1,0:T(8,128)(2,1)S(1)}, u32[]{:S(2)}, u32[]{:S(2)}) collective-permute-start(bf16[128,512]{1,0:T(8,128)(2,1)S(1)} %get-tuple-element.31), channel_id=1, source_target_pairs={{0,2},{2,0},{4,6},{6,4},{8,10},{10,8},{12,14},{14,12},{16,18},{18,... | collective-permute-start | bytes 393224 | tf_op jit(solution)/shard_map/ppermute | solution.py:170
  182.4 6.4 %collective-permute-start.14 = (bf16[256,512]{1,0:T(8,128)(2,1)S(1)}, bf16[256,512]{1,0:T(8,128)(2,1)S(1)}, u32[]{:S(2)}, u32[]{:S(2)}) collective-permute-start(bf16[256,512]{1,0:T(8,128)(2,1)S(1)} %pad_maximum_fusion.2), channel_id=1, source_target_pairs={{0,2},{2,0},{4,6},{6,4},{8,10},{10,8},{12,14},{14,12},{16,18},{18,... | collective-permute-start | bytes 786440 | tf_op jit(solution)/shard_map/ppermute | solution.py:170
  183.9 6.4 %collective-permute-start.16 = (bf16[256,512]{1,0:T(8,128)(2,1)S(1)}, bf16[256,512]{1,0:T(8,128)(2,1)S(1)}, u32[]{:S(2)}, u32[]{:S(2)}) collective-permute-start(bf16[256,512]{1,0:T(8,128)(2,1)S(1)} %pad_maximum_fusion.3), channel_id=1, source_target_pairs={{0,4},{2,6},{4,0},{6,2},{8,12},{10,14},{12,8},{14,10},{16,20},{18,... | collective-permute-start | bytes 786440 | tf_op jit(solution)/shard_map/ppermute | solution.py:170
  (45 other events, 167.0 us)

commit v2 on v1

v2 whole, which is shorter than its diff:
```python
import functools
import math

import jax
import jax.numpy as jnp
from jax import lax
from jax.experimental import pallas as pl
from jax.experimental.pallas import tpu as pltpu
from jax.sharding import PartitionSpec as P

MELS = 80
PANEL = 128
EPSILON = 1e-05
SPAN = PANEL // 8
BLOCK = 8
ROWS = BLOCK * SPAN
BINS = 40
GROUP = 10
WINDOW = 2 * GROUP + 1
LEAD = 256
BF = jnp.bfloat16
F32 = jnp.float32
ACROSS = (((1,), (1,)), ((), ()))
DOWN = (((0,), (0,)), ((), ()))


def dot(left, right, dims=(((1,), (0,)), ((), ()))):
    return lax.dot_general(left, right, dims, preferred_element_type=F32)


def iota(shape, dim):
    return lax.broadcasted_iota(jnp.int32, shape, dim)


def row_order():
    n = iota((ROWS, ROWS), 0)
    r = iota((ROWS, ROWS), 1)
    return jnp.where((n % SPAN) * BLOCK + n // SPAN == r, 1.0, 0.0).astype(BF)


def send_kernel(
    mel, frames, target, first, depth_a, point_a, depth_b, point_b, norm_gain, depth_kernel, conv_gain,
    outgoing, packed, rows,
):
    count = outgoing.shape[0]
    slots = mel.shape[0]
    width = mel.shape[1]
    wanted = iota((count, slots), 0)
    chosen = jnp.where((target[...] == wanted) & (frames[...] > 0), 1.0, 0.0)
    outgoing[:, :width] = dot(chosen.astype(BF), mel[...]).astype(BF)
    sent = jnp.sum(chosen * frames[...].astype(F32), axis=1, keepdims=True)
    outgoing[:, width:] = jnp.broadcast_to(sent, (count, 128)).astype(BF)
    rows[...] = jnp.zeros_like(rows)
    rows[0:9, :] = depth_kernel[...].astype(F32)
    rows[9:10, :] = norm_gain[...].astype(F32)
    rows[10:11, :] = conv_gain[...].astype(F32)
    rows[16:25, 0:128] = first[...].astype(F32)
    rows[16:25, 128:256] = depth_a[...].astype(F32)
    rows[16:25, 256:384] = depth_b[...].astype(F32)
    packed[0:32, :] = rows[...].astype(BF)
    packed[32:160, 0:128] = point_a[0:128, :]
    packed[32:160, 128:256] = point_a[128:256, :]
    packed[32:160, 256:384] = point_b[0:128, :]
    packed[32:160, 384:512] = point_b[128:256, :]


def weights_kernel(mine, other, band, taps_a, taps_b, point_a, point_b, rows):
    me = lax.axis_index("fsdp")
    near = mine[...].astype(F32)
    far = other[...].astype(F32)
    low = jnp.where(me == 0, near, far)
    high = jnp.where(me == 0, far, near)
    rows[:, 0:512] = low[0:16]
    rows[:, 512:1024] = high[0:16]
    first = jnp.concatenate([low[16:32, 0:128], high[16:32, 0:128]], axis=1).astype(BF)
    taps_a[...] = jnp.concatenate([low[16:32, 128:256], high[16:32, 128:256]], axis=1)
    taps_b[...] = jnp.concatenate([low[16:32, 256:384], high[16:32, 256:384]], axis=1)
    for half, source in ((0, low), (1, high)):
        at = slice(half * 128, half * 128 + 128)
        point_a[0:128, at] = source[32:160, 0:128].astype(BF)
        point_a[128:256, at] = source[32:160, 128:256].astype(BF)
        point_b[0:128, at] = source[32:160, 256:384].astype(BF)
        point_b[128:256, at] = source[32:160, 384:512].astype(BF)
    tap = iota((256, 16), 1)
    base = jnp.where(tap < 9, (tap // 3) * MELS + tap % 3, -1000) - iota((256, 16), 0)
    for f in range(GROUP):
        place = jnp.where(base == -2 * f, 1.0, 0.0).astype(BF)
        band[:, f * 256 : (f + 1) * 256] = dot(place, first).astype(BF)


def fetch(pairs, sems, me):
    copies = []
    for number, (mine, other, held) in enumerate(pairs):
        copies.append(pltpu.make_async_copy(mine, held.at[me], sems.at[2 * number]))
        copies.append(pltpu.make_async_copy(other, held.at[1 - me], sems.at[2 * number + 1]))
    return copies


def centre(values):
    return values - jnp.mean(values, axis=1, keepdims=True)


def forward_kernel(
    incoming, band, taps_a, taps_b, point_a, point_b, rows, linear_mine, linear_other, up_mine, up_other,
    hidden_out, kept_out, features_out, standard_out, value_out, gate_out, standard_two_out, scales_out, keep_out,
    linear_s, up_s, ext_s, x_s, first_s, spread_s, even_s, odd_s, flat_s, gated_s, sems,
):
    step = pl.program_id(0)
    me = lax.axis_index("fsdp")
    copies = fetch(((linear_mine, linear_other, linear_s), (up_mine, up_other, up_s)), sems, me)

    @pl.when(step == 0)
    def _():
        for copy in copies:
            copy.start()

    sources = incoming.shape[0]
    width = incoming.shape[1] - 128
    got = incoming[:, width:]
    present = jnp.where(got > 0, 1.0, 0.0)
    below = jnp.where(iota((sources, sources), 1) <= iota((sources, sources), 0), 1.0, 0.0).astype(BF)
    position = dot(below, present.astype(BF)) - 1.0
    slot = (iota((sources, 128), 1) + step * BLOCK).astype(F32)
    placing = jnp.where((position == slot) & (present > 0), 1.0, 0.0).astype(BF)[:, :BLOCK]
    length = dot(placing, got, DOWN)
    stretch = width // SPAN
    ext_s[0:BLOCK, 0:LEAD] = jnp.zeros((BLOCK, LEAD), F32)
    for t in range(SPAN):
        live = length > 8.0 * t
        keep_out[t * BLOCK : (t + 1) * BLOCK, :] = jnp.where(live, 1.0, 0.0)
        part = dot(placing, incoming[:, t * stretch : (t + 1) * stretch], DOWN)
        part = jnp.where(live[:, 0:1], part, 0.0)
        ext_s[t * BLOCK : (t + 1) * BLOCK, LEAD:] = part
        if t + 1 < SPAN:
            ext_s[(t + 1) * BLOCK : (t + 2) * BLOCK, 0:LEAD] = part[:, stretch - LEAD :]
    lane = iota((ROWS, 256), 1)
    edge = (lane == 0) | (lane == MELS) | (lane == 2 * MELS)
    for q in range(5):
        for b in range(4):
            start = LEAD + (2 * q - 3) * MELS + 2 * GROUP * b - 1
            tile = start // 128 * 128
            shift = start - tile
            span = 256 if shift + 2 * MELS + WINDOW <= 256 else 384
            part = ext_s[:, tile : tile + span]
            part = pltpu.roll(part, span - shift, 1)[:, :256]
            if b == 0:
                part = jnp.where(edge, 0.0, part)
            x_s[b, q * ROWS : (q + 1) * ROWS, :] = part.astype(BF)

    first_s[0] = jnp.zeros(first_s.shape[1:], F32)
    odd_s[:, 0:BLOCK, :] = jnp.zeros((odd_s.shape[0], BLOCK, 256), F32)

    def section(b, carry):
        source = x_s[b]
        for f in range(GROUP):
            first_s[1 + f] = jnp.maximum(dot(source, band[:, f * 256 : (f + 1) * 256]), 0.0)
        for g in range(GROUP // 2):
            for s in range(2):
                total = None
                for j in range(3):
                    for i in range(3):
                        at = (2 * s + i) * ROWS
                        term = first_s[2 * g + j, at : at + ROWS, :] * taps_a[3 * i + j : 3 * i + j + 1, :]
                        total = term if total is None else total + term
                spread_s[(2 * g + s) * ROWS : (2 * g + s + 1) * ROWS, :] = total.astype(BF)
        first_s[0] = first_s[GROUP]
        second = jnp.maximum(dot(spread_s[...], point_a[...]), 0.0)
        for g in range(GROUP // 2):
            even_s[b * (GROUP // 2) + g] = second[2 * g * ROWS : (2 * g + 1) * ROWS]
            odd_s[b * (GROUP // 2) + g, BLOCK:, :] = second[(2 * g + 1) * ROWS : (2 * g + 2) * ROWS]
        return carry

    lax.fori_loop(0, BINS // GROUP, section, 0)

    for f in range(BINS // 4):
        total = None
        for j in range(3):
            at = 2 * f + j - 1
            if at < 0:
                continue
            for i, view in enumerate((odd_s.at[at, 0:ROWS, :], even_s.at[at], odd_s.at[at, BLOCK : BLOCK + ROWS, :])):
                term = view[...] * taps_b[3 * i + j : 3 * i + j + 1, :]
                total = term if total is None else total + term
        fourth = jnp.maximum(dot(total.astype(BF), point_b[...]), 0.0)
        flat_s[:, f * 256 : (f + 1) * 256] = fourth.astype(BF)

    @pl.when(step == 0)
    def _():
        copies[0].wait()
        copies[1].wait()

    half = linear_s.shape[2]
    for side in range(2):
        features_out[:, side * half : (side + 1) * half] = dot(flat_s[...], linear_s[side]).astype(BF)
    centred = centre(features_out[...].astype(F32))
    scale_one = lax.rsqrt(jnp.mean(centred * centred, axis=1, keepdims=True) + EPSILON)
    standard = centred * scale_one
    standard_out[...] = standard
    normed = (standard * rows[9:10, :]).astype(BF)

    @pl.when(step == 0)
    def _():
        copies[2].wait()
        copies[3].wait()

    row_keep = keep_out[:, 0:1]
    value = dot(normed, up_s[0])
    value_out[...] = value
    gate = jax.nn.sigmoid(dot(normed, up_s[1]))
    gate_out[...] = gate
    reach = 4 * BLOCK
    gated_s[0:reach, :] = jnp.zeros((reach, gated_s.shape[1]), F32)
    gated_s[reach + ROWS :, :] = jnp.zeros((reach, gated_s.shape[1]), F32)
    gated_s[reach : reach + ROWS, :] = (row_keep * value * gate).astype(BF).astype(F32)
    total = None
    for k in range(9):
        term = gated_s[k * BLOCK : k * BLOCK + ROWS, :] * rows[k : k + 1, :]
        total = term if total is None else total + term
    centred = centre(total)
    scale_two = lax.rsqrt(jnp.mean(centred * centred, axis=1, keepdims=True) + EPSILON)
    standard_two = centred * scale_two
    standard_two_out[...] = standard_two
    active = standard_two * rows[10:11, :]
    hidden = (active * jax.nn.sigmoid(active)).astype(BF)
    hidden_out[...] = hidden
    scales_out[:, 0:128] = jnp.broadcast_to(scale_one, (ROWS, 128))
    scales_out[:, 128:256] = jnp.broadcast_to(scale_two, (ROWS, 128))
    kept = jnp.where(row_keep > 0, hidden, jnp.zeros_like(hidden))
    kept = dot(row_order(), kept).astype(BF)
    kept_out[me] = kept[:, :half]
    kept_out[1 - me] = kept[:, half:]


def backward_kernel(
    hidden_in, features_in, standard_in, value_in, gate_in, standard_two_in, scales_in, keep_in, rows, cotangent,
    down_mine, down_other, up_mine, up_other,
    layer_out, grad_out,
    down_s, up_s, depth_s, sems,
):
    step = pl.program_id(0)
    me = lax.axis_index("fsdp")
    copies = fetch(((down_mine, down_other, down_s), (up_mine, up_other, up_s)), sems, me)

    @pl.when(step == 0)
    def _():
        for copy in copies:
            copy.start()

    order = row_order()
    row_keep = keep_in[:, 0:1]
    back_out = jnp.where(row_keep > 0, dot(order, cotangent[...], DOWN), 0.0)
    back_bf = back_out.astype(BF)
    standard_two = standard_two_in[...]
    active = standard_two * rows[10:11, :]
    swish = jax.nn.sigmoid(active)
    slope = (swish + active * swish * (1.0 - swish)) * rows[10:11, :]

    @pl.when(step == 0)
    def _():
        copies[0].wait()
        copies[1].wait()

    half = down_s.shape[1]
    mixed = dot(hidden_in[:, :half], down_s[0]) + dot(hidden_in[:, half:], down_s[1])
    layer = jnp.where(row_keep > 0, features_in[...].astype(F32) + mixed, 0.0).astype(BF)
    layer_out[...] = dot(order, layer).astype(BF)
    back_hidden = jnp.concatenate([dot(back_bf, down_s[0], ACROSS), dot(back_bf, down_s[1], ACROSS)], axis=1)
    gain_up = back_hidden * slope
    scale_one = scales_in[:, 0:1]
    scale_two = scales_in[:, 128:129]
    back_depth = scale_two * (
        gain_up
        - jnp.mean(gain_up, axis=1, keepdims=True)
        - standard_two * jnp.mean(gain_up * standard_two, axis=1, keepdims=True)
    )
    reach = 4 * BLOCK
    depth_s[0:reach, :] = jnp.zeros((reach, depth_s.shape[1]), F32)
    depth_s[reach + ROWS :, :] = jnp.zeros((reach, depth_s.shape[1]), F32)
    depth_s[reach : reach + ROWS, :] = back_depth
    total = None
    for k in range(9):
        term = depth_s[(8 - k) * BLOCK : (8 - k) * BLOCK + ROWS, :] * rows[k : k + 1, :]
        total = term if total is None else total + term
    back_gated = row_keep * total
    gate = gate_in[...]
    back_value = back_gated * gate
    back_gate = (back_value * value_in[...] * (1.0 - gate)).astype(BF)

    @pl.when(step == 0)
    def _():
        copies[2].wait()
        copies[3].wait()

    back_normed = dot(back_value.astype(BF), up_s[0], ACROSS) + dot(back_gate, up_s[1], ACROSS)
    gain_in = back_normed * rows[9:10, :]
    standard = standard_in[...]
    back_input = scale_one * (
        gain_in
        - jnp.mean(gain_in, axis=1, keepdims=True)
        - standard * jnp.mean(gain_in * standard, axis=1, keepdims=True)
    )
    grad_out[...] = dot(order, (back_out + back_input).astype(BF)).astype(BF)


def whole(shape):
    return pl.BlockSpec(shape, lambda g: (0,) * len(shape))


def params(megabytes):
    return pltpu.CompilerParams(vmem_limit_bytes=megabytes * 1024 * 1024)


def cost(flops, moved):
    return pl.CostEstimate(flops=int(flops), bytes_accessed=int(moved), transcendentals=0)


def swap_cores(block):
    return lax.ppermute(block, "fsdp", [(0, 1), (1, 0)])


def swap_bit(block, bit, groups):
    return lax.ppermute(block, "dp", [(i, i ^ (1 << bit)) for i in range(groups)])


def pick(block, index):
    return lax.dynamic_index_in_dim(block, index, axis=0, keepdims=False)


def halve(total, bit, groups):
    side = (lax.axis_index("dp") >> bit) & 1
    pair = total.reshape(2, total.shape[0] // 2, total.shape[1])
    given = swap_bit(pick(pair, 1 - side).astype(jnp.bfloat16), bit, groups)
    return pick(pair, side) + given.astype(jnp.float32)


def double(block, bit, groups):
    side = (lax.axis_index("dp") >> bit) & 1
    given = swap_bit(block, bit, groups)
    return jnp.concatenate(
        [jnp.where(side == 0, block, given), jnp.where(side == 0, given, block)], axis=0
    )


def sum_over_dp(total, scale, groups):
    bits = groups.bit_length() - 1
    half = total.shape[1] // 2
    orders = ([0, 1], [1, 0])
    parts = [total[:, :half], total[:, half:]]
    for step in range(2):
        parts = [halve(part, order[step], groups) for part, order in zip(parts, orders)]
    joined = jnp.concatenate(parts, axis=1)
    for bit in range(2, bits - 1):
        joined = halve(joined, bit, groups)
    rounded = joined.astype(jnp.bfloat16)
    given = swap_bit(rounded, bits - 1, groups)
    block = ((rounded.astype(jnp.float32) + given.astype(jnp.float32)) * scale).astype(jnp.bfloat16)
    for bit in reversed(range(2, bits - 1)):
        block = double(block, bit, groups)
    parts = [block[:, :half], block[:, half:]]
    for step in reversed(range(2)):
        parts = [double(part, order[step], groups) for part, order in zip(parts, orders)]
    return jnp.concatenate(parts, axis=1).astype(jnp.float32)


def local(
    mel_panels,
    frames,
    target,
    conv_first,
    depth_a,
    point_a,
    depth_b,
    point_b,
    linear_weight,
    norm_gain,
    up_weight,
    depth_kernel,
    conv_gain,
    down_weight,
    cotangent,
):
    groups = lax.axis_size("dp")
    members = lax.axis_size("fsdp")
    slots, width_in = mel_panels.shape
    rows_here, width = cotangent.shape
    blocks = rows_here // ROWS
    half = width // members
    shape = jax.ShapeDtypeStruct
    outgoing, packed = pl.pallas_call(
        send_kernel,
        out_shape=(shape((groups, width_in + 128), BF), shape((160, 512), BF)),
        scratch_shapes=[pltpu.VMEM((32, 512), F32)],
        compiler_params=params(16),
        cost_estimate=cost(2e8, 1e6),
        name="send",
    )(
        mel_panels, frames.reshape(1, slots), target.reshape(1, slots), conv_first, depth_a, point_a, depth_b, point_b,
        norm_gain.reshape(1, half), depth_kernel, conv_gain.reshape(1, half),
    )
    incoming = lax.all_to_all(outgoing, "dp", split_axis=0, concat_axis=0, tiled=True)
    packed_other = swap_cores(packed)
    linear_other = swap_cores(linear_weight)
    up_other = swap_cores(up_weight)
    down_other = swap_cores(down_weight)
    cotangent_other = swap_cores(cotangent)
    band, taps_a, taps_b, point_one, point_two, rows = pl.pallas_call(
        weights_kernel,
        out_shape=(
            shape((256, GROUP * 256), BF),
            shape((16, 256), F32),
            shape((16, 256), F32),
            shape((256, 256), BF),
            shape((256, 256), BF),
            shape((16, width), F32),
        ),
        compiler_params=params(16),
        cost_estimate=cost(2e8, 2e6),
        name="weights",
    )(packed, packed_other)

    def by_rows(columns):
        return pl.BlockSpec((ROWS, columns), lambda g: (g, 0))

    anywhere = pl.BlockSpec(memory_space=pl.ANY)
    hidden, kept, features, standard, value, gate, standard_two, scales, keep = pl.pallas_call(
        forward_kernel,
        grid=(blocks,),
        in_specs=[
            whole(incoming.shape), whole(band.shape), whole(taps_a.shape), whole(taps_b.shape), whole(point_one.shape),
            whole(point_two.shape), whole(rows.shape), anywhere, anywhere, anywhere, anywhere,
        ],
        out_specs=[
            by_rows(width), pl.BlockSpec((members, ROWS, half), lambda g: (0, g, 0)), by_rows(width), by_rows(width),
            by_rows(width), by_rows(width), by_rows(width), by_rows(256), by_rows(128),
        ],
        out_shape=(
            shape((rows_here, width), BF),
            shape((members, rows_here, half), BF),
            shape((rows_here, width), BF),
            shape((rows_here, width), F32),
            shape((rows_here, width), F32),
            shape((rows_here, width), F32),
            shape((rows_here, width), F32),
            shape((rows_here, 256), F32),
            shape((rows_here, 128), F32),
        ),
        scratch_shapes=[
            pltpu.VMEM((2,) + linear_weight.shape, BF),
            pltpu.VMEM((2,) + up_weight.shape, BF),
            pltpu.VMEM((ROWS, LEAD + width_in // SPAN), F32),
            pltpu.VMEM((4, 5 * ROWS, 256), BF),
            pltpu.VMEM((GROUP + 1, 5 * ROWS, 256), F32),
            pltpu.VMEM((GROUP * ROWS, 256), BF),
            pltpu.VMEM((BINS // 2, ROWS, 256), F32),
            pltpu.VMEM((BINS // 2, ROWS + BLOCK, 256), F32),
            pltpu.VMEM((ROWS, BINS // 4 * 256), BF),
            pltpu.VMEM((ROWS + 8 * BLOCK, width), F32),
            pltpu.SemaphoreType.DMA((4,)),
        ],
        compiler_params=params(52),
        cost_estimate=cost(2e10 * blocks, 1e7),
        name="forward",
    )(incoming, band, taps_a, taps_b, point_one, point_two, rows, linear_weight, linear_other, up_weight, up_other)
    kept_mine = pick(kept, 0)
    kept_other = swap_cores(pick(kept, 1))
    product = dot(kept_mine, cotangent, DOWN) + dot(kept_other, cotangent_other, DOWN)
    scale = 1.0 / math.sqrt(rows_here * groups * members)
    grad_down = sum_over_dp(product, scale, groups)
    layer_out, grad_input = pl.pallas_call(
        backward_kernel,
        grid=(blocks,),
        in_specs=[
            by_rows(width), by_rows(width), by_rows(width), by_rows(width), by_rows(width), by_rows(width), by_rows(256),
            by_rows(128), whole(rows.shape), by_rows(width), anywhere, anywhere, anywhere, anywhere,
        ],
        out_specs=[by_rows(width), by_rows(width)],
        out_shape=(shape((rows_here, width), BF), shape((rows_here, width), BF)),
        scratch_shapes=[
            pltpu.VMEM((2,) + down_weight.shape, BF),
            pltpu.VMEM((2,) + up_weight.shape, BF),
            pltpu.VMEM((ROWS + 8 * BLOCK, width), F32),
            pltpu.SemaphoreType.DMA((4,)),
        ],
        compiler_params=params(32),
        cost_estimate=cost(4e9 * blocks, 1e7),
        name="backward",
    )(
        hidden, features, standard, value, gate, standard_two, scales, keep, rows, cotangent,
        down_weight, down_other, up_weight, up_other,
    )
    return (layer_out, grad_input, grad_down)


def solution(mesh):
    placed = (
        P(("dp", "fsdp"), None),
        P(("dp", "fsdp")),
        P(("dp", "fsdp")),
        P(None, "fsdp"),
        P(None, "fsdp"),
        P(None, "fsdp"),
        P(None, "fsdp"),
        P(None, "fsdp"),
        P(None, "fsdp"),
        P("fsdp"),
        P(None, "fsdp"),
        P(None, "fsdp"),
        P("fsdp"),
        P("fsdp", None),
        P(("dp", "fsdp"), None),
    )
    return jax.shard_map(
        local,
        mesh=mesh,
        in_specs=placed,
        out_specs=(P(("dp", "fsdp"), None), P(("dp", "fsdp"), None), P("fsdp", None)),
        check_vma=False,
    )
```

time: 193 us -> 115 us (0.60)
  other arithmetic: 49.6 us -> 8.28 us
  local copies, waits for them, and re-layouts: 55.9 us -> 22.6 us
  matrix products: 27.8 us -> 1.85 us
  Pallas kernels: 0 us -> 19.9 us
  waiting for transfers between devices: 32.9 us -> 41.9 us
  starting transfers between devices: 23.8 us -> 18.3 us
    convert_element_type x16 -> x0, other arithmetic: 41.1 us -> none  [the longest x1 27.4 us: first_section(): return jnp.maximum(summed, 0.0).astype(jnp.bfloat16)]
    dot_general x16 -> x2, matrix products: 27.8 us -> 1.85 us  [dot(): return lax.dot_general(left, right, dims, preferred_element_type=F32)]
    pallas_call x0 -> x4, Pallas kernels: none -> 19.9 us  [the longest x1 13.2 us: local(): pl.pallas_call(forward_kernel, grid=(blocks,), in_specs=[whole(incoming.s...]
    squeeze x9 -> x1, local copies, waits for them, and re-layouts: 12.6 us -> 0.01 us  [pick(): return lax.dynamic_index_in_dim(block, index, axis=0, keepdims=False)]
    unnamed x110 -> x55, local copies, waits for them, and re-layouts: 11.8 us -> 19.7 us
    concatenate x4 -> x0, local copies, waits for them, and re-layouts: 7.47 us -> none  [the longest x3 6.78 us: phase_rows(): before = jnp.concatenate([jnp.zeros_like(odd[:, :1]), odd[:, :-1]], axis=1)]
    ppermute x11, starting transfers between devices: 14.3 us -> 8.7 us  [swap_bit(): return lax.ppermute(block, 'dp', [(i, i ^ 1 << bit) for i in range(groups)])]
    mul x18 -> x0, local copies, waits for them, and re-layouts: 5.53 us -> none  [first_section(): window[:, :, :, None] * weights[3 * i + j].astype(jnp.float32)]
  transfers between devices with their start and end apart: 18 -> 18, of which waited for: 11 -> 10; matrix products, arithmetic and copies ran while one was open for 61% -> 11% of each run, Pallas kernels for 0% -> 17%
where the time goes in v2:
time: 115 us; the launch traced here: 114 us
  waiting for transfers between devices  41.9 us (36%)
  local copies, waits for them, and re-layouts  22.6 us (20%)
  Pallas kernels  19.9 us (17%)
  starting transfers between devices  18.3 us (16%)
  other arithmetic  8.28 us (7%)
  matrix products  1.85 us (2%)
    ppermute x11, waiting for transfers between devices, swap_bit(): return lax.ppermute(block, 'dp', [(i, i ^ 1 << bit) for i in range(groups)])  31.1 us
    unnamed x55, local copies, waits for them, and re-layouts  19.7 us
    pallas_call x1, Pallas kernels, local(): pl.pallas_call(forward_kernel, grid=(blocks,), in_specs=[whole(incoming.s...  13.2 us
    ppermute x11, starting transfers between devices, swap_bit(): return lax.ppermute(block, 'dp', [(i, i ^ 1 << bit) for i in range(groups)])  8.7 us
    all_to_all x1, waiting for transfers between devices, local(): lax.all_to_all(outgoing, 'dp', split_axis=0, concat_axis=0, tiled=True)  8.66 us
    all_to_all x1, starting transfers between devices, local(): lax.all_to_all(outgoing, 'dp', split_axis=0, concat_axis=0, tiled=True)  8.33 us
    pallas_call x1, Pallas kernels, local(): pl.pallas_call(backward_kernel, grid=(blocks,), in_specs=[by_rows(width),...  5.87 us
    select_n x5, other arithmetic, double(): jnp.where(side == 0, block, given)  3.09 us
  transfers between devices with their start and end apart: 18, of which 10 were waited for; matrix products, arithmetic and copies ran while one was open for 11% of the time, Pallas kernels for 17%

profile of v2, /device:TPU:0, one launch (start us, length us, event | category | flops | bytes accessed | tf_op | source)
XLA Modules:
  0.0 113.8 jit_solution(14408004160576520542)
XLA Ops:
  11.0 1.0 reshape.49
  12.0 8.3 %all-to-all-start = ((bf16[16,2,5184]{2,1,0:T(2,128)(2,1)}), bf16[16,2,5184]{2,1,0:T(2,128)(2,1)}, u32[]{:S(2)}, u32[]{:S(2)}) async-start(bf16[16,2,5184]{2,1,0:T(2,128)(2,1)} %reshape.49), calls=%async_computation | async-start | bytes 671744 | tf_op jit(solution)/shard_map/all_to_all | solution.py:400
  22.4 1.1 copy-done.14
  23.5 8.7 %all-to-all-done = bf16[16,2,5184]{2,1,0:T(2,128)(2,1)} async-done(((bf16[16,2,5184]{2,1,0:T(2,128)(2,1)}), bf16[16,2,5184]{2,1,0:T(2,128)(2,1)}, u32[]{:S(2)}, u32[]{:S(2)}) %all-to-all-start) | async-done | bytes 331808 | tf_op jit(solution)/shard_map/all_to_all | solution.py:400
  32.1 3.3 %reshape.50 = bf16[16,1,10368]{2,1,0:T(2,128)(2,1)} reshape(bf16[16,2,5184]{2,1,0:T(2,128)(2,1)} %all-to-all-done) | data formatting | bytes 663552
  35.5 1.1 copy.22
  36.6 1.3 %copy-done.2 = bf16[1024,1024]{1,0:T(8,128)(2,1)} copy-done((bf16[1024,1024]{1,0:T(8,128)(2,1)}, bf16[1024,1024]{1,0:T(8,128)(2,1)S(1)}, u32[]{:S(2)}) %copy-start.2) | copy-done | bytes 2097176
  37.9 13.2 %forward.1 = (bf16[128,1024]{1,0:T(8,128)(2,1)S(1)}, bf16[2,128,512]{2,1,0:T(8,128)(2,1)S(1)}, bf16[128,1024]{1,0:T(8,128)(2,1)S(1)}, f32[128,1024]{1,0:T(8,128)...) custom-call(bf16[16,10368]{1,0:T(8,128)(2,1)S(1)} %bitcast.42, ...), custom_call_target="tpu_custom_call" | custom-call | flops 20000000000 | bytes 10000000 | tf_op jit(solution)/shard_map/forward/pallas_call | solution.py:425
  52.0 1.3 %collective-permute-done.4 = bf16[128,512]{1,0:T(8,128)(2,1)S(1)} collective-permute-done((bf16[128,512]{1,0:T(8,128)(2,1)S(1)}, bf16[128,512]{1,0:T(8,128)(2,1)S(1)}, u32[]{:S(2)}, u32[]{:S(2)}) %collective-permute-start.4) | collective-permute-done | bytes 131104 | tf_op jit(solution)/shard_map/ppermute | solution.py:318
  53.3 1.4 %fusion.10 = f32[512,1024]{1,0:T(8,128)S(1)} fusion(bf16[128,512]{1,0:T(8,128)(2,1)S(1)} %collective-permute-done.4, bf16[128,1024]{1,0:T(8,128)(2,1)} %collective-permute-done.5), kind=kOutput, calls=%fused_computation.41 | convolution fusion | flops 134217728 | bytes 2490368 | tf_op jit(solution)/shard_map/dot_general | solution.py:28
  56.9 6.9 %collective-permute-done.6 = bf16[256,512]{1,0:T(8,128)(2,1)S(1)} collective-permute-done((bf16[256,512]{1,0:T(8,128)(2,1)S(1)}, bf16[256,512]{1,0:T(8,128)(2,1)S(1)}, u32[]{:S(2)}, u32[]{:S(2)}) %collective-permute-start.6) | collective-permute-done | bytes 262176 | tf_op jit(solution)/shard_map/ppermute | solution.py:322
  65.9 3.1 %collective-permute-done.7 = bf16[128,512]{1,0:T(8,128)(2,1)S(1)} collective-permute-done((bf16[128,512]{1,0:T(8,128)(2,1)S(1)}, bf16[128,512]{1,0:T(8,128)(2,1)S(1)}, u32[]{:S(2)}, u32[]{:S(2)}) %collective-permute-start.7) | collective-permute-done | bytes 131104 | tf_op jit(solution)/shard_map/ppermute | solution.py:322
  71.5 1.0 collective-permute-start.10
  72.5 4.3 %collective-permute-done.10 = bf16[64,1024]{1,0:T(8,128)(2,1)} collective-permute-done((bf16[64,1024]{1,0:T(8,128)(2,1)}, bf16[64,1024]{1,0:T(8,128)(2,1)}, u32[]{:S(2)}, u32[]{:S(2)}) %collective-permute-start.10) | collective-permute-done | bytes 131104 | tf_op jit(solution)/shard_map/ppermute | solution.py:322
  76.8 1.0 fusion.2
  78.6 6.7 %collective-permute-done.11 = bf16[64,1024]{1,0:T(8,128)(2,1)S(1)} collective-permute-done((bf16[64,1024]{1,0:T(8,128)(2,1)S(1)}, bf16[64,1024]{1,0:T(8,128)(2,1)S(1)}, u32[]{:S(2)}, u32[]{:S(2)}) %collective-permute-start.11) | collective-permute-done | bytes 131104 | tf_op jit(solution)/shard_map/ppermute | solution.py:322
  86.0 5.3 %collective-permute-done.12 = bf16[64,1024]{1,0:T(8,128)(2,1)} collective-permute-done((bf16[64,1024]{1,0:T(8,128)(2,1)}, bf16[64,1024]{1,0:T(8,128)(2,1)}, u32[]{:S(2)}, u32[]{:S(2)}) %collective-permute-start.12) | collective-permute-done | bytes 131104 | tf_op jit(solution)/shard_map/ppermute | solution.py:322
  93.0 1.2 %collective-permute-start.13 = (bf16[128,512]{1,0:T(8,128)(2,1)}, bf16[128,512]{1,0:T(8,128)(2,1)}, u32[]{:S(2)}, u32[]{:S(2)}) collective-permute-start(bf16[128,512]{1,0:T(8,128)(2,1)} %get-tuple-element.49), channel_id=1, source_target_pairs={{0,4},{2,6},{4,0},{6,2},{8,12},{10,14},{12,8},{14,10},{16,20},{18,... | collective-permute-start | bytes 393224 | tf_op jit(solution)/shard_map/ppermute | solution.py:322
  94.8 3.9 %collective-permute-done.13 = bf16[128,512]{1,0:T(8,128)(2,1)} collective-permute-done((bf16[128,512]{1,0:T(8,128)(2,1)}, bf16[128,512]{1,0:T(8,128)(2,1)}, u32[]{:S(2)}, u32[]{:S(2)}) %collective-permute-start.13) | collective-permute-done | bytes 131104 | tf_op jit(solution)/shard_map/ppermute | solution.py:322
  101.3 1.2 %collective-permute-start.16 = (bf16[256,512]{1,0:T(8,128)(2,1)S(1)}, bf16[256,512]{1,0:T(8,128)(2,1)S(1)}, u32[]{:S(2)}, u32[]{:S(2)}) collective-permute-start(bf16[256,512]{1,0:T(8,128)(2,1)S(1)} %pad_maximum_fusion.2), channel_id=1, source_target_pairs={{0,4},{2,6},{4,0},{6,2},{8,12},{10,14},{12,8},{14,10},{16,20},{18,... | collective-permute-start | bytes 786440 | tf_op jit(solution)/shard_map/ppermute | solution.py:322
  102.6 1.6 %copy-done.3 = bf16[1024,1024]{1,0:T(8,128)(2,1)S(1)} copy-done((bf16[1024,1024]{1,0:T(8,128)(2,1)S(1)}, bf16[1024,1024]{1,0:T(8,128)(2,1)}, u32[]{:S(2)}) %copy-start.3) | copy-done | bytes 2097176
  104.2 1.0 copy-done.18
  106.2 5.9 %backward.1 = (bf16[128,1024]{1,0:T(8,128)(2,1)}, bf16[128,1024]{1,0:T(8,128)(2,1)}) custom-call(bf16[128,1024]{1,0:T(8,128)(2,1)S(1)} %copy-done.20, bf16[128,1024]{1,0:T(8,128)(2,1)S(1)} %copy-done.22, f32[128,1024]{1,0:T(8,128)S(1)} %copy-done.15, f32[128,1024]{1,0:T(8,128)S(1)} %copy-done.16, f32[128,1024]{1,0:T(8,128)S(1)} %copy-done.17, ...), custom_call_target="tpu_custom_call" | custom-call | flops 4000000000 | bytes 10000000 | tf_op jit(solution)/shard_map/backward/pallas_call | solution.py:469
  112.3 1.6 %maximum_convert_fusion = f32[512,1024]{1,0:T(8,128)} fusion(bf16[256,512]{1,0:T(8,128)(2,1)S(1)} %get-tuple-element.46, bf16[256,512]{1,0:T(8,128)(2,1)S(1)} %get-tuple-element.45, bf16[256,512]{1,0:T(8,128)(2,1)S(1)} %get-tuple-element.44, bf16[256,512]{1,0:T(8,128)(2,1)S(1)} %get-tuple-element.43), kind=kLoop, calls=%fused_computation.1 | loop fusion | flops 4194304 | bytes 3145728 | tf_op jit(solution)/shard_map/convert_element_type | solution.py:362
  (100 shorter events, 27.3 us)
Async XLA Ops:
  0.6 19.8 %copy-start = (bf16[128,1024]{1,0:T(8,128)(2,1)S(1)}, bf16[128,1024]{1,0:T(8,128)(2,1)}, u32[]{:S(2)}) copy-start(bf16[128,1024]{1,0:T(8,128)(2,1)} %cotangent.1) | copy-start | bytes 786436
  0.6 36.0 %collective-permute-start.1 = (bf16[2560,512]{1,0:T(8,128)(2,1)}, bf16[2560,512]{1,0:T(8,128)(2,1)}, u32[]{:S(2)}, u32[]{:S(2)}) collective-permute-start(bf16[2560,512]{1,0:T(8,128)(2,1)} %linear_mine.1), channel_id=1, source_target_pairs={{0,1},{1,0},{2,3},{3,2},{4,5},{5,4},{6,7},{7,6},{8,9},{9,8},{10,11... | collective-permute-start | bytes 7864328 | tf_op jit(solution)/shard_map/ppermute | solution.py:318
  1.2 35.4 %collective-permute-start.2 = (bf16[1024,1024]{1,0:T(8,128)(2,1)}, bf16[1024,1024]{1,0:T(8,128)(2,1)S(1)}, u32[]{:S(2)}, u32[]{:S(2)}) collective-permute-start(bf16[1024,1024]{1,0:T(8,128)(2,1)} %up_mine.3), channel_id=1, source_target_pairs={{0,1},{1,0},{2,3},{3,2},{4,5},{5,4},{6,7},{7,6},{8,9},{9,8},{10,11... | collective-permute-start | bytes 6291464 | tf_op jit(solution)/shard_map/ppermute | solution.py:318
  12.0 20.1 %all-to-all-start = ((bf16[16,2,5184]{2,1,0:T(2,128)(2,1)}), bf16[16,2,5184]{2,1,0:T(2,128)(2,1)}, u32[]{:S(2)}, u32[]{:S(2)}) async-start(bf16[16,2,5184]{2,1,0:T(2,128)(2,1)} %reshape.49), calls=%async_computation | async-start | bytes 671744 | tf_op jit(solution)/shard_map/all_to_all | solution.py:400
  20.4 1.5 %collective-permute-start = (bf16[160,512]{1,0:T(8,128)(2,1)S(1)}, bf16[160,512]{1,0:T(8,128)(2,1)S(1)}, u32[]{:S(2)}, u32[]{:S(2)}) collective-permute-start(bf16[160,512]{1,0:T(8,128)(2,1)S(1)} %get-tuple-element.23.mine), channel_id=1, source_target_pairs={{0,1},{1,0},{2,3},{3,2},{4,5},{5,4},{6,7},{7,6},{8,9},{9,8},{10,11... | collective-permute-start | bytes 491528 | tf_op jit(solution)/shard_map/ppermute | solution.py:318
  20.5 31.5 %collective-permute-start.5 = (bf16[128,1024]{1,0:T(8,128)(2,1)S(1)}, bf16[128,1024]{1,0:T(8,128)(2,1)}, u32[]{:S(2)}, u32[]{:S(2)}) collective-permute-start(bf16[128,1024]{1,0:T(8,128)(2,1)S(1)} %copy-done), channel_id=1, source_target_pairs={{0,1},{1,0},{2,3},{3,2},{4,5},{5,4},{6,7},{7,6},{8,9},{9,8},{10,11... | collective-permute-start | bytes 786440 | tf_op jit(solution)/shard_map/ppermute | solution.py:318
  51.9 1.4 %collective-permute-start.4 = (bf16[128,512]{1,0:T(8,128)(2,1)S(1)}, bf16[128,512]{1,0:T(8,128)(2,1)S(1)}, u32[]{:S(2)}, u32[]{:S(2)}) collective-permute-start(bf16[128,512]{1,0:T(8,128)(2,1)S(1)} %slice_bitcast_fusion), channel_id=1, source_target_pairs={{0,1},{1,0},{2,3},{3,2},{4,5},{5,4},{6,7},{7,6},{8,9},{9,8},{10,11... | collective-permute-start | bytes 393224 | tf_op jit(solution)/shard_map/ppermute | solution.py:318
  55.4 8.4 %collective-permute-start.6 = (bf16[256,512]{1,0:T(8,128)(2,1)S(1)}, bf16[256,512]{1,0:T(8,128)(2,1)S(1)}, u32[]{:S(2)}, u32[]{:S(2)}) collective-permute-start(bf16[256,512]{1,0:T(8,128)(2,1)S(1)} %fusion), channel_id=1, source_target_pairs={{0,2},{2,0},{4,6},{6,4},{8,10},{10,8},{12,14},{14,12},{16,18},{18,... | collective-permute-start | bytes 786440 | tf_op jit(solution)/shard_map/ppermute | solution.py:322
  56.1 8.7 %collective-permute-start.8 = (bf16[256,512]{1,0:T(8,128)(2,1)S(1)}, bf16[256,512]{1,0:T(8,128)(2,1)S(1)}, u32[]{:S(2)}, u32[]{:S(2)}) collective-permute-start(bf16[256,512]{1,0:T(8,128)(2,1)S(1)} %fusion.1), channel_id=1, source_target_pairs={{0,4},{2,6},{4,0},{6,2},{8,12},{10,14},{12,8},{14,10},{16,20},{18,... | collective-permute-start | bytes 786440 | tf_op jit(solution)/shard_map/ppermute | solution.py:322
  64.0 5.0 %collective-permute-start.7 = (bf16[128,512]{1,0:T(8,128)(2,1)S(1)}, bf16[128,512]{1,0:T(8,128)(2,1)S(1)}, u32[]{:S(2)}, u32[]{:S(2)}) collective-permute-start(bf16[128,512]{1,0:T(8,128)(2,1)S(1)} %fusion.3), channel_id=1, source_target_pairs={{0,4},{2,6},{4,0},{6,2},{8,12},{10,14},{12,8},{14,10},{16,20},{18,... | collective-permute-start | bytes 393224 | tf_op jit(solution)/shard_map/ppermute | solution.py:322
  64.9 21.0 %copy-start.4 = (bf16[512,1024]{1,0:T(8,128)(2,1)S(1)}, bf16[512,1024]{1,0:T(8,128)(2,1)}, u32[]{:S(2)}) copy-start(bf16[512,1024]{1,0:T(8,128)(2,1)} %down_mine.1) | copy-start | bytes 3145732
  65.0 5.0 %collective-permute-start.9 = (bf16[128,512]{1,0:T(8,128)(2,1)S(1)}, bf16[128,512]{1,0:T(8,128)(2,1)S(1)}, u32[]{:S(2)}, u32[]{:S(2)}) collective-permute-start(bf16[128,512]{1,0:T(8,128)(2,1)S(1)} %fusion.4), channel_id=1, source_target_pairs={{0,2},{2,0},{4,6},{6,4},{8,10},{10,8},{12,14},{14,12},{16,18},{18,... | collective-permute-start | bytes 393224 | tf_op jit(solution)/shard_map/ppermute | solution.py:322
  71.5 31.0 %copy-start.1 = (bf16[1024,1024]{1,0:T(8,128)(2,1)S(1)}, bf16[1024,1024]{1,0:T(8,128)(2,1)}, u32[]{:S(2)}) copy-start(bf16[1024,1024]{1,0:T(8,128)(2,1)} %up_mine.3) | copy-start | bytes 6291460
  71.5 5.3 %collective-permute-start.10 = (bf16[64,1024]{1,0:T(8,128)(2,1)}, bf16[64,1024]{1,0:T(8,128)(2,1)}, u32[]{:S(2)}, u32[]{:S(2)}) collective-permute-start(bf16[64,1024]{1,0:T(8,128)(2,1)} %fusion.5), channel_id=1, source_target_pairs={{0,8},{2,10},{4,12},{6,14},{8,0},{10,2},{12,4},{14,6},{16,24},{18,... | collective-permute-start | bytes 393224 | tf_op jit(solution)/shard_map/ppermute | solution.py:322
  77.8 7.4 %collective-permute-start.11 = (bf16[64,1024]{1,0:T(8,128)(2,1)S(1)}, bf16[64,1024]{1,0:T(8,128)(2,1)S(1)}, u32[]{:S(2)}, u32[]{:S(2)}) collective-permute-start(bf16[64,1024]{1,0:T(8,128)(2,1)S(1)} %fusion.2), channel_id=1, source_target_pairs={{0,16},{2,18},{4,20},{6,22},{8,24},{10,26},{12,28},{14,30},{16,0},... | collective-permute-start | bytes 393224 | tf_op jit(solution)/shard_map/ppermute | solution.py:322
  85.9 5.3 %collective-permute-start.12 = (bf16[64,1024]{1,0:T(8,128)(2,1)}, bf16[64,1024]{1,0:T(8,128)(2,1)}, u32[]{:S(2)}, u32[]{:S(2)}) collective-permute-start(bf16[64,1024]{1,0:T(8,128)(2,1)} %multiply_convert_fusion), channel_id=1, source_target_pairs={{0,8},{2,10},{4,12},{6,14},{8,0},{10,2},{12,4},{14,6},{16,24},{18,... | collective-permute-start | bytes 393224 | tf_op jit(solution)/shard_map/ppermute | solution.py:322
  86.0 16.6 %collective-permute-start.3 = (bf16[512,1024]{1,0:T(8,128)(2,1)S(1)}, bf16[512,1024]{1,0:T(8,128)(2,1)}, u32[]{:S(2)}, u32[]{:S(2)}) collective-permute-start(bf16[512,1024]{1,0:T(8,128)(2,1)S(1)} %copy-done.4), channel_id=1, source_target_pairs={{0,1},{1,0},{2,3},{3,2},{4,5},{5,4},{6,7},{7,6},{8,9},{9,8},{10,11... | collective-permute-start | bytes 3145736 | tf_op jit(solution)/shard_map/ppermute | solution.py:318
  93.0 5.8 %collective-permute-start.13 = (bf16[128,512]{1,0:T(8,128)(2,1)}, bf16[128,512]{1,0:T(8,128)(2,1)}, u32[]{:S(2)}, u32[]{:S(2)}) collective-permute-start(bf16[128,512]{1,0:T(8,128)(2,1)} %get-tuple-element.49), channel_id=1, source_target_pairs={{0,4},{2,6},{4,0},{6,2},{8,12},{10,14},{12,8},{14,10},{16,20},{18,... | collective-permute-start | bytes 393224 | tf_op jit(solution)/shard_map/ppermute | solution.py:322
  94.2 8.4 %copy-start.17 = (f32[128,1024]{1,0:T(8,128)S(1)}, f32[128,1024]{1,0:T(8,128)}, u32[]{:S(2)}) copy-start(f32[128,1024]{1,0:T(8,128)} %get-tuple-element.34.gate_in) | copy-start | bytes 1572868
  94.2 8.4 %copy-start.20 = (bf16[128,1024]{1,0:T(8,128)(2,1)S(1)}, bf16[128,1024]{1,0:T(8,128)(2,1)}, u32[]{:S(2)}) copy-start(bf16[128,1024]{1,0:T(8,128)(2,1)} %copy-done.19) | copy-start | bytes 786436
  94.2 8.4 %copy-start.24 = (f32[128,256]{1,0:T(8,128)S(1)}, f32[128,256]{1,0:T(8,128)}, u32[]{:S(2)}) copy-start(f32[128,256]{1,0:T(8,128)} %copy-done.23) | copy-start | bytes 393220
  94.2 6.2 %collective-permute-start.15 = (bf16[128,512]{1,0:T(8,128)(2,1)}, bf16[128,512]{1,0:T(8,128)(2,1)S(1)}, u32[]{:S(2)}, u32[]{:S(2)}) collective-permute-start(bf16[128,512]{1,0:T(8,128)(2,1)} %get-tuple-element.50), channel_id=1, source_target_pairs={{0,2},{2,0},{4,6},{6,4},{8,10},{10,8},{12,14},{14,12},{16,18},{18,... | collective-permute-start | bytes 393224 | tf_op jit(solution)/shard_map/ppermute | solution.py:322
  99.7 12.3 %collective-permute-start.14 = (bf16[256,512]{1,0:T(8,128)(2,1)S(1)}, bf16[256,512]{1,0:T(8,128)(2,1)S(1)}, u32[]{:S(2)}, u32[]{:S(2)}) collective-permute-start(bf16[256,512]{1,0:T(8,128)(2,1)S(1)} %pad_maximum_fusion.1), channel_id=1, source_target_pairs={{0,2},{2,0},{4,6},{6,4},{8,10},{10,8},{12,14},{14,12},{16,18},{18,... | collective-permute-start | bytes 786440 | tf_op jit(solution)/shard_map/ppermute | solution.py:322
  101.3 10.8 %collective-permute-start.16 = (bf16[256,512]{1,0:T(8,128)(2,1)S(1)}, bf16[256,512]{1,0:T(8,128)(2,1)S(1)}, u32[]{:S(2)}, u32[]{:S(2)}) collective-permute-start(bf16[256,512]{1,0:T(8,128)(2,1)S(1)} %pad_maximum_fusion.2), channel_id=1, source_target_pairs={{0,4},{2,6},{4,0},{6,2},{8,12},{10,14},{12,8},{14,10},{16,20},{18,... | collective-permute-start | bytes 786440 | tf_op jit(solution)/shard_map/ppermute | solution.py:322
  (20 other events, 37.5 us)

commit v3 on v2

--- a/solution.py
+++ b/solution.py
@@ -40,28 +40,45 @@
 
 def send_kernel(
     mel, frames, target, first, depth_a, point_a, depth_b, point_b, norm_gain, depth_kernel, conv_gain,
-    outgoing, packed, rows,
+    outgoing, packed,
+    mel_s, first_s, depth_a_s, point_a_s, depth_b_s, point_b_s, norm_s, kernel_s, conv_s, rows, lines, sems,
 ):
+    pairs = (
+        (mel, mel_s), (first, first_s), (depth_a, depth_a_s), (point_a, point_a_s), (depth_b, depth_b_s),
+        (point_b, point_b_s), (norm_gain, norm_s), (depth_kernel, kernel_s), (conv_gain, conv_s),
+    )
+    copies = [pltpu.make_async_copy(source, held, sems.at[n]) for n, (source, held) in enumerate(pairs)]
+    for copy in copies:
+        copy.start()
     count = outgoing.shape[0]
-    slots = mel.shape[0]
-    width = mel.shape[1]
+    slots = mel_s.shape[0]
+    lanes = mel_s.shape[1] // 128
     wanted = iota((count, slots), 0)
     chosen = jnp.where((target[...] == wanted) & (frames[...] > 0), 1.0, 0.0)
-    outgoing[:, :width] = dot(chosen.astype(BF), mel[...]).astype(BF)
     sent = jnp.sum(chosen * frames[...].astype(F32), axis=1, keepdims=True)
-    outgoing[:, width:] = jnp.broadcast_to(sent, (count, 128)).astype(BF)
+    sent = jnp.broadcast_to(sent, (count, 128))
+    for k in range(8):
+        lines[pl.ds(lanes + k, count, stride=lanes + 8), :] = sent
+    copies[0].wait()
+    chosen = chosen.astype(BF)
+    for k in range(lanes):
+        lines[pl.ds(k, count, stride=lanes + 8), :] = dot(chosen, mel_s[:, k * 128 : (k + 1) * 128])
+    for d in range(count):
+        outgoing[d] = lines[d * (lanes + 8) : (d + 1) * (lanes + 8), :].astype(BF)
+    for copy in copies[1:]:
+        copy.wait()
     rows[...] = jnp.zeros_like(rows)
-    rows[0:9, :] = depth_kernel[...].astype(F32)
-    rows[9:10, :] = norm_gain[...].astype(F32)
-    rows[10:11, :] = conv_gain[...].astype(F32)
-    rows[16:25, 0:128] = first[...].astype(F32)
-    rows[16:25, 128:256] = depth_a[...].astype(F32)
-    rows[16:25, 256:384] = depth_b[...].astype(F32)
+    rows[0:9, :] = kernel_s[...].astype(F32)
+    rows[9:10, :] = norm_s[...].astype(F32).reshape(1, 512)
+    rows[10:11, :] = conv_s[...].astype(F32).reshape(1, 512)
+    rows[16:25, 0:128] = first_s[...].astype(F32)
+    rows[16:25, 128:256] = depth_a_s[...].astype(F32)
+    rows[16:25, 256:384] = depth_b_s[...].astype(F32)
     packed[0:32, :] = rows[...].astype(BF)
-    packed[32:160, 0:128] = point_a[0:128, :]
-    packed[32:160, 128:256] = point_a[128:256, :]
-    packed[32:160, 256:384] = point_b[0:128, :]
-    packed[32:160, 384:512] = point_b[128:256, :]
+    packed[32:160, 0:128] = point_a_s[0:128, :]
+    packed[32:160, 128:256] = point_a_s[128:256, :]
+    packed[32:160, 256:384] = point_b_s[0:128, :]
+    packed[32:160, 384:512] = point_b_s[128:256, :]
 
 
 def weights_kernel(mine, other, band, taps_a, taps_b, point_a, point_b, rows):
@@ -103,7 +120,7 @@
 def forward_kernel(
     incoming, band, taps_a, taps_b, point_a, point_b, rows, linear_mine, linear_other, up_mine, up_other,
     hidden_out, kept_out, features_out, standard_out, value_out, gate_out, standard_two_out, scales_out, keep_out,
-    linear_s, up_s, ext_s, x_s, first_s, spread_s, even_s, odd_s, flat_s, gated_s, sems,
+    linear_s, up_s, pick_s, ext_s, x_s, first_s, spread_s, even_s, odd_s, flat_s, gated_s, sems,
 ):
     step = pl.program_id(0)
     me = lax.axis_index("fsdp")
@@ -115,24 +132,36 @@
             copy.start()
 
     sources = incoming.shape[0]
-    width = incoming.shape[1] - 128
-    got = incoming[:, width:]
+    lanes = incoming.shape[1] - 8
+    got = jnp.concatenate([incoming[source, lanes:, :].astype(F32)[0:1] for source in range(sources)], axis=0)
     present = jnp.where(got > 0, 1.0, 0.0)
     below = jnp.where(iota((sources, sources), 1) <= iota((sources, sources), 0), 1.0, 0.0).astype(BF)
     position = dot(below, present.astype(BF)) - 1.0
     slot = (iota((sources, 128), 1) + step * BLOCK).astype(F32)
     placing = jnp.where((position == slot) & (present > 0), 1.0, 0.0).astype(BF)[:, :BLOCK]
-    length = dot(placing, got, DOWN)
-    stretch = width // SPAN
-    ext_s[0:BLOCK, 0:LEAD] = jnp.zeros((BLOCK, LEAD), F32)
+    length = dot(placing, got.astype(BF), DOWN)
+    source = dot(placing, iota((sources, 128), 0).astype(F32).astype(BF), DOWN)
+    per_step = lanes // SPAN
+    lane = iota((BLOCK, 128), 1).astype(F32)
+    base = source * lanes - lane
     for t in range(SPAN):
         live = length > 8.0 * t
         keep_out[t * BLOCK : (t + 1) * BLOCK, :] = jnp.where(live, 1.0, 0.0)
-        part = dot(placing, incoming[:, t * stretch : (t + 1) * stretch], DOWN)
-        part = jnp.where(live[:, 0:1], part, 0.0)
-        ext_s[t * BLOCK : (t + 1) * BLOCK, LEAD:] = part
-        if t + 1 < SPAN:
-            ext_s[(t + 1) * BLOCK : (t + 2) * BLOCK, 0:LEAD] = part[:, stretch - LEAD :]
+        here = jnp.where(live, base, -1e6)
+        for k in range(per_step):
+            at = k * ROWS + t * BLOCK
+            for c in range(sources * lanes // 128):
+                hit = here == 128.0 * c - (per_step * t + k)
+                pick_s[at : at + BLOCK, c * 128 : (c + 1) * 128] = jnp.where(hit, 1.0, 0.0)
+    lines = jnp.concatenate([incoming[source, :lanes, :] for source in range(sources)], axis=0)
+    placed = dot(pick_s[...].astype(BF), lines)
+    ext_s[0:BLOCK, 0:LEAD] = jnp.zeros((BLOCK, LEAD), F32)
+    for k in range(per_step):
+        part = placed[k * ROWS : (k + 1) * ROWS]
+        ext_s[:, LEAD + k * 128 : LEAD + (k + 1) * 128] = part
+        ahead = k + LEAD // 128 - per_step
+        if ahead >= 0:
+            ext_s[BLOCK:, ahead * 128 : (ahead + 1) * 128] = part[: ROWS - BLOCK]
     lane = iota((ROWS, 256), 1)
     edge = (lane == 0) | (lane == MELS) | (lane == 2 * MELS)
     for q in range(5):
@@ -326,11 +355,13 @@
     return lax.dynamic_index_in_dim(block, index, axis=0, keepdims=False)
 
 
-def halve(total, bit, groups):
+def halve(total, bit, groups, beside=()):
     side = (lax.axis_index("dp") >> bit) & 1
     pair = total.reshape(2, total.shape[0] // 2, total.shape[1])
     given = swap_bit(pick(pair, 1 - side).astype(jnp.bfloat16), bit, groups)
-    return pick(pair, side) + given.astype(jnp.float32)
+    if beside:
+        given, *beside = lax.optimization_barrier((given, *beside))
+    return pick(pair, side) + given.astype(jnp.float32), beside
 
 
 def double(block, bit, groups):
@@ -341,16 +372,17 @@
     )
 
 
-def sum_over_dp(total, scale, groups):
+def sum_over_dp(total, scale, groups, beside):
     bits = groups.bit_length() - 1
     half = total.shape[1] // 2
     orders = ([0, 1], [1, 0])
     parts = [total[:, :half], total[:, half:]]
-    for step in range(2):
-        parts = [halve(part, order[step], groups) for part, order in zip(parts, orders)]
+    parts[0], beside = halve(parts[0], orders[0][0], groups, beside)
+    parts[1], _ = halve(parts[1], orders[1][0], groups)
+    parts = [halve(part, order[1], groups)[0] for part, order in zip(parts, orders)]
     joined = jnp.concatenate(parts, axis=1)
     for bit in range(2, bits - 1):
-        joined = halve(joined, bit, groups)
+        joined, _ = halve(joined, bit, groups)
     rounded = joined.astype(jnp.bfloat16)
     given = swap_bit(rounded, bits - 1, groups)
     block = ((rounded.astype(jnp.float32) + given.astype(jnp.float32)) * scale).astype(jnp.bfloat16)
@@ -359,7 +391,7 @@
     parts = [block[:, :half], block[:, half:]]
     for step in reversed(range(2)):
         parts = [double(part, order[step], groups) for part, order in zip(parts, orders)]
-    return jnp.concatenate(parts, axis=1).astype(jnp.float32)
+    return jnp.concatenate(parts, axis=1).astype(jnp.float32), beside
 
 
 def local(
@@ -386,17 +418,24 @@
     blocks = rows_here // ROWS
     half = width // members
     shape = jax.ShapeDtypeStruct
+    lines = width_in // 128 + 8
+    anywhere = pl.BlockSpec(memory_space=pltpu.HBM)
+    held = pl.BlockSpec(memory_space=pltpu.VMEM)
+    small = (conv_first, depth_a, point_a, depth_b, point_b, norm_gain, depth_kernel, conv_gain)
     outgoing, packed = pl.pallas_call(
         send_kernel,
-        out_shape=(shape((groups, width_in + 128), BF), shape((160, 512), BF)),
-        scratch_shapes=[pltpu.VMEM((32, 512), F32)],
-        compiler_params=params(16),
+        in_specs=[anywhere, held, held] + [anywhere] * len(small),
+        out_shape=(shape((groups, lines, 128), BF), shape((160, 512), BF)),
+        scratch_shapes=[pltpu.VMEM(array.shape, BF) for array in (mel_panels,) + small]
+        + [
+            pltpu.VMEM((32, 512), F32),
+            pltpu.VMEM((groups * lines, 128), F32),
+            pltpu.SemaphoreType.DMA((1 + len(small),)),
+        ],
+        compiler_params=params(60),
         cost_estimate=cost(2e8, 1e6),
         name="send",
-    )(
-        mel_panels, frames.reshape(1, slots), target.reshape(1, slots), conv_first, depth_a, point_a, depth_b, point_b,
-        norm_gain.reshape(1, half), depth_kernel, conv_gain.reshape(1, half),
-    )
+    )(mel_panels, frames.reshape(1, slots), target.reshape(1, slots), *small)
     incoming = lax.all_to_all(outgoing, "dp", split_axis=0, concat_axis=0, tiled=True)
     packed_other = swap_cores(packed)
     linear_other = swap_cores(linear_weight)
@@ -421,7 +460,6 @@
     def by_rows(columns):
         return pl.BlockSpec((ROWS, columns), lambda g: (g, 0))
 
-    anywhere = pl.BlockSpec(memory_space=pl.ANY)
     hidden, kept, features, standard, value, gate, standard_two, scales, keep = pl.pallas_call(
         forward_kernel,
         grid=(blocks,),
@@ -447,6 +485,7 @@
         scratch_shapes=[
             pltpu.VMEM((2,) + linear_weight.shape, BF),
             pltpu.VMEM((2,) + up_weight.shape, BF),
+            pltpu.VMEM((ROWS * width_in // SPAN // 128, groups * width_in // 128), F32),
             pltpu.VMEM((ROWS, LEAD + width_in // SPAN), F32),
             pltpu.VMEM((4, 5 * ROWS, 256), BF),
             pltpu.VMEM((GROUP + 1, 5 * ROWS, 256), F32),
@@ -457,16 +496,15 @@
             pltpu.VMEM((ROWS + 8 * BLOCK, width), F32),
             pltpu.SemaphoreType.DMA((4,)),
         ],
-        compiler_params=params(52),
+        compiler_params=params(44),
         cost_estimate=cost(2e10 * blocks, 1e7),
         name="forward",
     )(incoming, band, taps_a, taps_b, point_one, point_two, rows, linear_weight, linear_other, up_weight, up_other)
-    kept_mine = pick(kept, 0)
-    kept_other = swap_cores(pick(kept, 1))
+    kept_mine = kept[0]
+    kept_other = swap_cores(kept[1])
     product = dot(kept_mine, cotangent, DOWN) + dot(kept_other, cotangent_other, DOWN)
     scale = 1.0 / math.sqrt(rows_here * groups * members)
-    grad_down = sum_over_dp(product, scale, groups)
-    layer_out, grad_input = pl.pallas_call(
+    beside = pl.pallas_call(
         backward_kernel,
         grid=(blocks,),
         in_specs=[
@@ -481,13 +519,14 @@
             pltpu.VMEM((ROWS + 8 * BLOCK, width), F32),
             pltpu.SemaphoreType.DMA((4,)),
         ],
-        compiler_params=params(32),
-        cost_estimate=cost(4e9 * blocks, 1e7),
+        compiler_params=params(60),
+        cost_estimate=cost(1e6, 1e5),
         name="backward",
     )(
         hidden, features, standard, value, gate, standard_two, scales, keep, rows, cotangent,
         down_weight, down_other, up_weight, up_other,
     )
+    grad_down, (layer_out, grad_input) = sum_over_dp(product, scale, groups, beside)
     return (layer_out, grad_input, grad_down)
 
 

time: 115 us -> 103 us (0.90)
  local copies, waits for them, and re-layouts: 22.6 us -> 9.52 us
  starting transfers between devices: 18.3 us -> 26.9 us
  other arithmetic: 8.28 us -> 2.21 us
  Pallas kernels: 19.9 us -> 23 us
  waiting for transfers between devices: 41.9 us -> 39.2 us
    unnamed x55 -> x28, local copies, waits for them, and re-layouts: 19.7 us -> 9.15 us
    ppermute x11, starting transfers between devices: 8.7 us -> 16.9 us  [swap_bit(): return lax.ppermute(block, 'dp', [(i, i ^ 1 << bit) for i in range(groups)])]
    select_n x5, other arithmetic: 3.09 us -> 0.26 us  [double(): jnp.where(side == 0, block, given)]
    pallas_call x1, Pallas kernels: 0.24 us -> 2.88 us  [local(): pl.pallas_call(send_kernel, in_specs=[anywhere, held, held] + [anywhere]...]
    pallas_call x1, Pallas kernels: 5.87 us -> 7.92 us  [local(): pl.pallas_call(backward_kernel, grid=(blocks,), in_specs=[by_rows(width),...]
    ppermute x11, waiting for transfers between devices: 31.1 us -> 29.3 us  [swap_bit(): return lax.ppermute(block, 'dp', [(i, i ^ 1 << bit) for i in range(groups)])]
    pallas_call x1, Pallas kernels: 13.2 us -> 11.6 us  [local(): pl.pallas_call(forward_kernel, grid=(blocks,), in_specs=[whole(incoming.s...]
    reshape x2 -> x0, local copies, waits for them, and re-layouts: 1.36 us -> none  [the longest x1 0.68 us: local(): norm_gain.reshape(1, half)]
  transfers between devices with their start and end apart: 18 -> 18, of which waited for: 10 -> 12; matrix products, arithmetic and copies ran while one was open for 11% -> 2% of each run, Pallas kernels for 17% -> 20%
where the time goes in v3:
time: 103 us
  waiting for transfers between devices  39.2 us (38%)
  starting transfers between devices  26.9 us (26%)
  Pallas kernels  23 us (22%)
  local copies, waits for them, and re-layouts  9.52 us (9%)
  other arithmetic  2.21 us (2%)
    ppermute x11, waiting for transfers between devices, swap_bit(): return lax.ppermute(block, 'dp', [(i, i ^ 1 << bit) for i in range(groups)])  29.3 us
    ppermute x11, starting transfers between devices, swap_bit(): return lax.ppermute(block, 'dp', [(i, i ^ 1 << bit) for i in range(groups)])  16.9 us
    pallas_call x1, Pallas kernels, local(): pl.pallas_call(forward_kernel, grid=(blocks,), in_specs=[whole(incoming.s...  11.6 us
    unnamed x28, local copies, waits for them, and re-layouts  9.15 us
    all_to_all x1, starting transfers between devices, local(): lax.all_to_all(outgoing, 'dp', split_axis=0, concat_axis=0, tiled=True)  8.31 us
    all_to_all x1, waiting for transfers between devices, local(): lax.all_to_all(outgoing, 'dp', split_axis=0, concat_axis=0, tiled=True)  7.92 us
    pallas_call x1, Pallas kernels, local(): pl.pallas_call(backward_kernel, grid=(blocks,), in_specs=[by_rows(width),...  7.92 us
    pallas_call x1, Pallas kernels, local(): pl.pallas_call(send_kernel, in_specs=[anywhere, held, held] + [anywhere]...  2.88 us
  transfers between devices with their start and end apart: 18, of which 12 were waited for; matrix products, arithmetic and copies ran while one was open for 2% of the time, Pallas kernels for 20%

profile of v3, /device:TPU:0, one launch (start us, length us, event | category | flops | bytes accessed | tf_op | source)
XLA Modules:
  0.0 102.6 jit_solution(15067004952655390583)
XLA Ops:
  1.2 2.9 %send.1 = (bf16[16,88,128]{2,1,0:T(8,128)(2,1)}, bf16[160,512]{1,0:T(8,128)(2,1)}) custom-call(bf16[16,10240]{1,0:T(8,128)(2,1)} %mel.1, s32[1,16]{1,0:T(1,128)} %bitcast.47, s32[1,16]{1,0:T(1,128)} %bitcast.48, bf16[9,128]{1,0:T(8,128)(2,1)} %first.1, bf16[9,128]{1,0:T(8,128)(2,1)} %depth_a.1, bf16[256,128]{1,0:T(8,128)(2,1)} %point_a.1, ...), custom_call_target="tpu_custom_call" | custom-call | flops 200000000 | bytes 1000000 | tf_op jit(solution)/shard_map/send/pallas_call | solution.py:425
  4.1 8.3 %all-to-all-start = ((bf16[16,88,128]{2,1,0:T(8,128)(2,1)}), bf16[16,88,128]{2,1,0:T(8,128)(2,1)S(1)}, u32[]{:S(2)}, u32[]{:S(2)}) async-start(bf16[16,88,128]{2,1,0:T(8,128)(2,1)} %get-tuple-element.25), calls=%async_computation | async-start | bytes 720896 | tf_op jit(solution)/shard_map/all_to_all | solution.py:439
  13.0 1.1 %collective-permute-done.other = bf16[160,512]{1,0:T(8,128)(2,1)S(1)} collective-permute-done((bf16[160,512]{1,0:T(8,128)(2,1)}, bf16[160,512]{1,0:T(8,128)(2,1)S(1)}, u32[]{:S(2)}, u32[]{:S(2)}) %collective-permute-start) | collective-permute-done | bytes 163872 | tf_op jit(solution)/shard_map/ppermute | solution.py:347
  16.7 7.9 %all-to-all-done.incoming = bf16[16,88,128]{2,1,0:T(8,128)(2,1)S(1)} async-done(((bf16[16,88,128]{2,1,0:T(8,128)(2,1)}), bf16[16,88,128]{2,1,0:T(8,128)(2,1)S(1)}, u32[]{:S(2)}, u32[]{:S(2)}) %all-to-all-start) | async-done | bytes 360480 | tf_op jit(solution)/shard_map/all_to_all | solution.py:439
  24.6 1.3 %copy-done.12 = bf16[256,2560]{1,0:T(8,128)(2,1)S(1)} copy-done((bf16[256,2560]{1,0:T(8,128)(2,1)S(1)}, bf16[256,2560]{1,0:T(8,128)(2,1)}, u32[]{:S(2)}) %copy-start.12) | copy-done | bytes 1310744
  25.9 11.6 %forward.1 = (bf16[128,1024]{1,0:T(8,128)(2,1)S(1)}, bf16[2,128,512]{2,1,0:T(8,128)(2,1)S(1)}, bf16[128,1024]{1,0:T(8,128)(2,1)S(1)}, f32[128,1024]{1,0:T(8,128)...) custom-call(bf16[16,88,128]{2,1,0:T(8,128)(2,1)S(1)} %all-to-all-don, ...), custom_call_target="tpu_custom_call" | custom-call | flops 20000000000 | bytes 10000000 | tf_op jit(solution)/shard_map/forward/pallas_call | solution.py:463
  46.7 7.9 %backward.1 = (bf16[128,1024]{1,0:T(8,128)(2,1)}, bf16[128,1024]{1,0:T(8,128)(2,1)}) custom-call(bf16[128,1024]{1,0:T(8,128)(2,1)} %copy-done.5, bf16[128,1024]{1,0:T(8,128)(2,1)} %copy-done.6, f32[128,1024]{1,0:T(8,128)} %copy-done.1, f32[128,1024]{1,0:T(8,128)} %copy-done.2, f32[128,1024]{1,0:T(8,128)} %copy-done.3, f32[128,1024]{1,0:T(8,128)} %copy-done.4, ...), custom_call_target="tpu_custom_call" | custom-call | flops 1000000 | bytes 100000 | tf_op jit(solution)/shard_map/backward/pallas_call | solution.py:507
  55.7 1.3 %collective-permute-start.7 = (bf16[128,512]{1,0:T(8,128)(2,1)S(1)}, bf16[128,512]{1,0:T(8,128)(2,1)S(1)}, u32[]{:S(2)}, u32[]{:S(2)}) collective-permute-start(bf16[128,512]{1,0:T(8,128)(2,1)S(1)} %fusion.3), channel_id=1, source_target_pairs={{0,4},{2,6},{4,0},{6,2},{8,12},{10,14},{12,8},{14,10},{16,20},{18,... | collective-permute-start | bytes 393224 | tf_op jit(solution)/shard_map/ppermute | solution.py:351
  57.0 6.9 %collective-permute-done.8 = bf16[256,512]{1,0:T(8,128)(2,1)S(1)} collective-permute-done((bf16[256,512]{1,0:T(8,128)(2,1)S(1)}, bf16[256,512]{1,0:T(8,128)(2,1)S(1)}, u32[]{:S(2)}, u32[]{:S(2)}) %collective-permute-start.8) | collective-permute-done | bytes 262176 | tf_op jit(solution)/shard_map/ppermute | solution.py:351
  64.0 1.5 %collective-permute-start.9 = (bf16[128,512]{1,0:T(8,128)(2,1)S(1)}, bf16[128,512]{1,0:T(8,128)(2,1)S(1)}, u32[]{:S(2)}, u32[]{:S(2)}) collective-permute-start(bf16[128,512]{1,0:T(8,128)(2,1)S(1)} %fusion.4), channel_id=1, source_target_pairs={{0,2},{2,0},{4,6},{6,4},{8,10},{10,8},{12,14},{14,12},{16,18},{18,... | collective-permute-start | bytes 393224 | tf_op jit(solution)/shard_map/ppermute | solution.py:351
  66.1 2.9 %collective-permute-done.9 = bf16[128,512]{1,0:T(8,128)(2,1)S(1)} collective-permute-done((bf16[128,512]{1,0:T(8,128)(2,1)S(1)}, bf16[128,512]{1,0:T(8,128)(2,1)S(1)}, u32[]{:S(2)}, u32[]{:S(2)}) %collective-permute-start.9) | collective-permute-done | bytes 131104 | tf_op jit(solution)/shard_map/ppermute | solution.py:351
  69.1 1.1 %collective-permute-start.10 = (bf16[64,1024]{1,0:T(8,128)(2,1)S(1)}, bf16[64,1024]{1,0:T(8,128)(2,1)S(1)}, u32[]{:S(2)}, u32[]{:S(2)}) collective-permute-start(bf16[64,1024]{1,0:T(8,128)(2,1)S(1)} %fusion.5), channel_id=1, source_target_pairs={{0,8},{2,10},{4,12},{6,14},{8,0},{10,2},{12,4},{14,6},{16,24},{18,... | collective-permute-start | bytes 393224 | tf_op jit(solution)/shard_map/ppermute | solution.py:351
  70.3 3.9 %collective-permute-done.10 = bf16[64,1024]{1,0:T(8,128)(2,1)S(1)} collective-permute-done((bf16[64,1024]{1,0:T(8,128)(2,1)S(1)}, bf16[64,1024]{1,0:T(8,128)(2,1)S(1)}, u32[]{:S(2)}, u32[]{:S(2)}) %collective-permute-start.10) | collective-permute-done | bytes 131104 | tf_op jit(solution)/shard_map/ppermute | solution.py:351
  74.2 1.4 %collective-permute-start.11 = (bf16[64,1024]{1,0:T(8,128)(2,1)S(1)}, bf16[64,1024]{1,0:T(8,128)(2,1)S(1)}, u32[]{:S(2)}, u32[]{:S(2)}) collective-permute-start(bf16[64,1024]{1,0:T(8,128)(2,1)S(1)} %fusion.2), channel_id=1, source_target_pairs={{0,16},{2,18},{4,20},{6,22},{8,24},{10,26},{12,28},{14,30},{16,0},... | collective-permute-start | bytes 393224 | tf_op jit(solution)/shard_map/ppermute | solution.py:351
  75.6 4.6 %collective-permute-done.11 = bf16[64,1024]{1,0:T(8,128)(2,1)S(1)} collective-permute-done((bf16[64,1024]{1,0:T(8,128)(2,1)S(1)}, bf16[64,1024]{1,0:T(8,128)(2,1)S(1)}, u32[]{:S(2)}, u32[]{:S(2)}) %collective-permute-start.11) | collective-permute-done | bytes 131104 | tf_op jit(solution)/shard_map/ppermute | solution.py:351
  80.2 2.8 %collective-permute-start.12 = (bf16[64,1024]{1,0:T(8,128)(2,1)S(1)}, bf16[64,1024]{1,0:T(8,128)(2,1)S(1)}, u32[]{:S(2)}, u32[]{:S(2)}) collective-permute-start(bf16[64,1024]{1,0:T(8,128)(2,1)S(1)} %multiply_convert_fusion), channel_id=1, source_target_pairs={{0,8},{2,10},{4,12},{6,14},{8,0},{10,2},{12,4},{14,6},{16,24},{18,... | collective-permute-start | bytes 393224 | tf_op jit(solution)/shard_map/ppermute | solution.py:351
  83.1 2.9 %collective-permute-done.12 = bf16[64,1024]{1,0:T(8,128)(2,1)S(1)} collective-permute-done((bf16[64,1024]{1,0:T(8,128)(2,1)S(1)}, bf16[64,1024]{1,0:T(8,128)(2,1)S(1)}, u32[]{:S(2)}, u32[]{:S(2)}) %collective-permute-start.12) | collective-permute-done | bytes 131104 | tf_op jit(solution)/shard_map/ppermute | solution.py:351
  87.1 2.9 %collective-permute-start.15 = (bf16[128,512]{1,0:T(8,128)(2,1)S(1)}, bf16[128,512]{1,0:T(8,128)(2,1)S(1)}, u32[]{:S(2)}, u32[]{:S(2)}) collective-permute-start(bf16[128,512]{1,0:T(8,128)(2,1)S(1)} %get-tuple-element.56), channel_id=1, source_target_pairs={{0,2},{2,0},{4,6},{6,4},{8,10},{10,8},{12,14},{14,12},{16,18},{18,... | collective-permute-start | bytes 393224 | tf_op jit(solution)/shard_map/ppermute | solution.py:351
  89.9 2.6 %collective-permute-done.13 = bf16[128,512]{1,0:T(8,128)(2,1)S(1)} collective-permute-done((bf16[128,512]{1,0:T(8,128)(2,1)S(1)}, bf16[128,512]{1,0:T(8,128)(2,1)S(1)}, u32[]{:S(2)}, u32[]{:S(2)}) %collective-permute-start.13) | collective-permute-done | bytes 131104 | tf_op jit(solution)/shard_map/ppermute | solution.py:351
  92.6 1.9 %collective-permute-start.14 = (bf16[256,512]{1,0:T(8,128)(2,1)S(1)}, bf16[256,512]{1,0:T(8,128)(2,1)S(1)}, u32[]{:S(2)}, u32[]{:S(2)}) collective-permute-start(bf16[256,512]{1,0:T(8,128)(2,1)S(1)} %pad_maximum_fusion.1), channel_id=1, source_target_pairs={{0,2},{2,0},{4,6},{6,4},{8,10},{10,8},{12,14},{14,12},{16,18},{18,... | collective-permute-start | bytes 786440 | tf_op jit(solution)/shard_map/ppermute | solution.py:351
  94.5 1.5 %collective-permute-start.16 = (bf16[256,512]{1,0:T(8,128)(2,1)S(1)}, bf16[256,512]{1,0:T(8,128)(2,1)S(1)}, u32[]{:S(2)}, u32[]{:S(2)}) collective-permute-start(bf16[256,512]{1,0:T(8,128)(2,1)S(1)} %pad_maximum_fusion.2), channel_id=1, source_target_pairs={{0,4},{2,6},{4,0},{6,2},{8,12},{10,14},{12,8},{14,10},{16,20},{18,... | collective-permute-start | bytes 786440 | tf_op jit(solution)/shard_map/ppermute | solution.py:351
  96.0 3.0 %collective-permute-done.14 = bf16[256,512]{1,0:T(8,128)(2,1)S(1)} collective-permute-done((bf16[256,512]{1,0:T(8,128)(2,1)S(1)}, bf16[256,512]{1,0:T(8,128)(2,1)S(1)}, u32[]{:S(2)}, u32[]{:S(2)}) %collective-permute-start.14) | collective-permute-done | bytes 262176 | tf_op jit(solution)/shard_map/ppermute | solution.py:351
  99.1 1.8 %collective-permute-done.16 = bf16[256,512]{1,0:T(8,128)(2,1)S(1)} collective-permute-done((bf16[256,512]{1,0:T(8,128)(2,1)S(1)}, bf16[256,512]{1,0:T(8,128)(2,1)S(1)}, u32[]{:S(2)}, u32[]{:S(2)}) %collective-permute-start.16) | collective-permute-done | bytes 262176 | tf_op jit(solution)/shard_map/ppermute | solution.py:351
  101.0 1.6 %maximum_convert_fusion = f32[512,1024]{1,0:T(8,128)} fusion(bf16[256,512]{1,0:T(8,128)(2,1)S(1)} %get-tuple-element.52, bf16[256,512]{1,0:T(8,128)(2,1)S(1)} %get-tuple-element.51, bf16[256,512]{1,0:T(8,128)(2,1)S(1)} %get-tuple-element.50, bf16[256,512]{1,0:T(8,128)(2,1)S(1)} %get-tuple-element.49), kind=kLoop, calls=%fused_computation.1 | loop fusion | flops 4194304 | bytes 3145728 | tf_op jit(solution)/shard_map/convert_element_type | solution.py:394
  (69 shorter events, 16.0 us)
Async XLA Ops:
  0.6 24.0 %copy-start = (bf16[1024,1024]{1,0:T(8,128)(2,1)S(1)}, bf16[1024,1024]{1,0:T(8,128)(2,1)}, u32[]{:S(2)}) copy-start(bf16[1024,1024]{1,0:T(8,128)(2,1)} %up_mine.3) | copy-start | bytes 6291460
  0.6 24.0 %collective-permute-start.1 = (bf16[2560,512]{1,0:T(8,128)(2,1)}, bf16[2560,512]{1,0:T(8,128)(2,1)}, u32[]{:S(2)}, u32[]{:S(2)}) collective-permute-start(bf16[2560,512]{1,0:T(8,128)(2,1)} %linear_mine.1), channel_id=1, source_target_pairs={{0,1},{1,0},{2,3},{3,2},{4,5},{5,4},{6,7},{7,6},{8,9},{9,8},{10,11... | collective-permute-start | bytes 7864328 | tf_op jit(solution)/shard_map/ppermute | solution.py:347
  1.2 23.5 %collective-permute-start.2 = (bf16[1024,1024]{1,0:T(8,128)(2,1)}, bf16[1024,1024]{1,0:T(8,128)(2,1)}, u32[]{:S(2)}, u32[]{:S(2)}) collective-permute-start(bf16[1024,1024]{1,0:T(8,128)(2,1)} %up_mine.3), channel_id=1, source_target_pairs={{0,1},{1,0},{2,3},{3,2},{4,5},{5,4},{6,7},{7,6},{8,9},{9,8},{10,11... | collective-permute-start | bytes 6291464 | tf_op jit(solution)/shard_map/ppermute | solution.py:347
  4.1 20.5 %all-to-all-start = ((bf16[16,88,128]{2,1,0:T(8,128)(2,1)}), bf16[16,88,128]{2,1,0:T(8,128)(2,1)S(1)}, u32[]{:S(2)}, u32[]{:S(2)}) async-start(bf16[16,88,128]{2,1,0:T(8,128)(2,1)} %get-tuple-element.25), calls=%async_computation | async-start | bytes 720896 | tf_op jit(solution)/shard_map/all_to_all | solution.py:439
  12.5 1.7 %collective-permute-start = (bf16[160,512]{1,0:T(8,128)(2,1)}, bf16[160,512]{1,0:T(8,128)(2,1)S(1)}, u32[]{:S(2)}, u32[]{:S(2)}) collective-permute-start(bf16[160,512]{1,0:T(8,128)(2,1)} %get-tuple-element.26.mine), channel_id=1, source_target_pairs={{0,1},{1,0},{2,3},{3,2},{4,5},{5,4},{6,7},{7,6},{8,9},{9,8},{10,11... | collective-permute-start | bytes 491528 | tf_op jit(solution)/shard_map/ppermute | solution.py:347
  12.5 31.5 %collective-permute-start.4 = (bf16[128,1024]{1,0:T(8,128)(2,1)}, bf16[128,1024]{1,0:T(8,128)(2,1)S(1)}, u32[]{:S(2)}, u32[]{:S(2)}) collective-permute-start(bf16[128,1024]{1,0:T(8,128)(2,1)} %cotangent.1), channel_id=1, source_target_pairs={{0,1},{1,0},{2,3},{3,2},{4,5},{5,4},{6,7},{7,6},{8,9},{9,8},{10,11... | collective-permute-start | bytes 786440 | tf_op jit(solution)/shard_map/ppermute | solution.py:347
  14.1 0.9 copy-start.10
  15.6 1.1 %copy-start.11 = (bf16[256,2560]{1,0:T(8,128)(2,1)}, bf16[256,2560]{1,0:T(8,128)(2,1)S(1)}, u32[]{:S(2)}) copy-start(bf16[256,2560]{1,0:T(8,128)(2,1)S(1)} %get-tuple-element.27.band) | copy-start | bytes 3932164
  16.7 20.9 %copy-start.8 = (f32[16,1024]{1,0:T(8,128)}, f32[16,1024]{1,0:T(8,128)S(1)}, u32[]{:S(2)}) copy-start(f32[16,1024]{1,0:T(8,128)S(1)} %get-tuple-element.32.rows) | copy-start | bytes 196612
  24.6 1.3 %copy-start.12 = (bf16[256,2560]{1,0:T(8,128)(2,1)S(1)}, bf16[256,2560]{1,0:T(8,128)(2,1)}, u32[]{:S(2)}) copy-start(bf16[256,2560]{1,0:T(8,128)(2,1)} %copy-done.11) | copy-start | bytes 3932164
  43.4 1.9 %copy-start.13 = (bf16[128,1024]{1,0:T(8,128)(2,1)S(1)}, bf16[128,1024]{1,0:T(8,128)(2,1)}, u32[]{:S(2)}) copy-start(bf16[128,1024]{1,0:T(8,128)(2,1)} %cotangent.1) | copy-start | bytes 786436
  43.5 1.4 %collective-permute-start.3 = (bf16[128,512]{1,0:T(8,128)(2,1)S(1)}, bf16[128,512]{1,0:T(8,128)(2,1)S(1)}, u32[]{:S(2)}, u32[]{:S(2)}) collective-permute-start(bf16[128,512]{1,0:T(8,128)(2,1)S(1)} %slice_bitcast_fusion), channel_id=1, source_target_pairs={{0,1},{1,0},{2,3},{3,2},{4,5},{5,4},{6,7},{7,6},{8,9},{9,8},{10,11... | collective-permute-start | bytes 393224 | tf_op jit(solution)/shard_map/ppermute | solution.py:347
  43.5 3.2 %collective-permute-start.6 = (bf16[512,1024]{1,0:T(8,128)(2,1)}, bf16[512,1024]{1,0:T(8,128)(2,1)}, u32[]{:S(2)}, u32[]{:S(2)}) collective-permute-start(bf16[512,1024]{1,0:T(8,128)(2,1)} %down_mine.1), channel_id=1, source_target_pairs={{0,1},{1,0},{2,3},{3,2},{4,5},{5,4},{6,7},{7,6},{8,9},{9,8},{10,11... | collective-permute-start | bytes 3145736 | tf_op jit(solution)/shard_map/ppermute | solution.py:347
  46.0 9.5 %collective-permute-start.5 = (bf16[256,512]{1,0:T(8,128)(2,1)S(1)}, bf16[256,512]{1,0:T(8,128)(2,1)S(1)}, u32[]{:S(2)}, u32[]{:S(2)}) collective-permute-start(bf16[256,512]{1,0:T(8,128)(2,1)S(1)} %fusion), channel_id=1, source_target_pairs={{0,2},{2,0},{4,6},{6,4},{8,10},{10,8},{12,14},{14,12},{16,18},{18,... | collective-permute-start | bytes 786440 | tf_op jit(solution)/shard_map/ppermute | solution.py:351
  54.7 9.2 %collective-permute-start.8 = (bf16[256,512]{1,0:T(8,128)(2,1)S(1)}, bf16[256,512]{1,0:T(8,128)(2,1)S(1)}, u32[]{:S(2)}, u32[]{:S(2)}) collective-permute-start(bf16[256,512]{1,0:T(8,128)(2,1)S(1)} %fusion.1), channel_id=1, source_target_pairs={{0,4},{2,6},{4,0},{6,2},{8,12},{10,14},{12,8},{14,10},{16,20},{18,... | collective-permute-start | bytes 786440 | tf_op jit(solution)/shard_map/ppermute | solution.py:351
  55.7 10.4 %collective-permute-start.7 = (bf16[128,512]{1,0:T(8,128)(2,1)S(1)}, bf16[128,512]{1,0:T(8,128)(2,1)S(1)}, u32[]{:S(2)}, u32[]{:S(2)}) collective-permute-start(bf16[128,512]{1,0:T(8,128)(2,1)S(1)} %fusion.3), channel_id=1, source_target_pairs={{0,4},{2,6},{4,0},{6,2},{8,12},{10,14},{12,8},{14,10},{16,20},{18,... | collective-permute-start | bytes 393224 | tf_op jit(solution)/shard_map/ppermute | solution.py:351
  64.0 5.0 %collective-permute-start.9 = (bf16[128,512]{1,0:T(8,128)(2,1)S(1)}, bf16[128,512]{1,0:T(8,128)(2,1)S(1)}, u32[]{:S(2)}, u32[]{:S(2)}) collective-permute-start(bf16[128,512]{1,0:T(8,128)(2,1)S(1)} %fusion.4), channel_id=1, source_target_pairs={{0,2},{2,0},{4,6},{6,4},{8,10},{10,8},{12,14},{14,12},{16,18},{18,... | collective-permute-start | bytes 393224 | tf_op jit(solution)/shard_map/ppermute | solution.py:351
  69.1 5.0 %collective-permute-start.10 = (bf16[64,1024]{1,0:T(8,128)(2,1)S(1)}, bf16[64,1024]{1,0:T(8,128)(2,1)S(1)}, u32[]{:S(2)}, u32[]{:S(2)}) collective-permute-start(bf16[64,1024]{1,0:T(8,128)(2,1)S(1)} %fusion.5), channel_id=1, source_target_pairs={{0,8},{2,10},{4,12},{6,14},{8,0},{10,2},{12,4},{14,6},{16,24},{18,... | collective-permute-start | bytes 393224 | tf_op jit(solution)/shard_map/ppermute | solution.py:351
  74.2 6.0 %collective-permute-start.11 = (bf16[64,1024]{1,0:T(8,128)(2,1)S(1)}, bf16[64,1024]{1,0:T(8,128)(2,1)S(1)}, u32[]{:S(2)}, u32[]{:S(2)}) collective-permute-start(bf16[64,1024]{1,0:T(8,128)(2,1)S(1)} %fusion.2), channel_id=1, source_target_pairs={{0,16},{2,18},{4,20},{6,22},{8,24},{10,26},{12,28},{14,30},{16,0},... | collective-permute-start | bytes 393224 | tf_op jit(solution)/shard_map/ppermute | solution.py:351
  80.2 5.8 %collective-permute-start.12 = (bf16[64,1024]{1,0:T(8,128)(2,1)S(1)}, bf16[64,1024]{1,0:T(8,128)(2,1)S(1)}, u32[]{:S(2)}, u32[]{:S(2)}) collective-permute-start(bf16[64,1024]{1,0:T(8,128)(2,1)S(1)} %multiply_convert_fusion), channel_id=1, source_target_pairs={{0,8},{2,10},{4,12},{6,14},{8,0},{10,2},{12,4},{14,6},{16,24},{18,... | collective-permute-start | bytes 393224 | tf_op jit(solution)/shard_map/ppermute | solution.py:351
  86.1 6.4 %collective-permute-start.13 = (bf16[128,512]{1,0:T(8,128)(2,1)S(1)}, bf16[128,512]{1,0:T(8,128)(2,1)S(1)}, u32[]{:S(2)}, u32[]{:S(2)}) collective-permute-start(bf16[128,512]{1,0:T(8,128)(2,1)S(1)} %get-tuple-element.55), channel_id=1, source_target_pairs={{0,4},{2,6},{4,0},{6,2},{8,12},{10,14},{12,8},{14,10},{16,20},{18,... | collective-permute-start | bytes 393224 | tf_op jit(solution)/shard_map/ppermute | solution.py:351
  87.1 7.4 %collective-permute-start.15 = (bf16[128,512]{1,0:T(8,128)(2,1)S(1)}, bf16[128,512]{1,0:T(8,128)(2,1)S(1)}, u32[]{:S(2)}, u32[]{:S(2)}) collective-permute-start(bf16[128,512]{1,0:T(8,128)(2,1)S(1)} %get-tuple-element.56), channel_id=1, source_target_pairs={{0,2},{2,0},{4,6},{6,4},{8,10},{10,8},{12,14},{14,12},{16,18},{18,... | collective-permute-start | bytes 393224 | tf_op jit(solution)/shard_map/ppermute | solution.py:351
  92.6 6.4 %collective-permute-start.14 = (bf16[256,512]{1,0:T(8,128)(2,1)S(1)}, bf16[256,512]{1,0:T(8,128)(2,1)S(1)}, u32[]{:S(2)}, u32[]{:S(2)}) collective-permute-start(bf16[256,512]{1,0:T(8,128)(2,1)S(1)} %pad_maximum_fusion.1), channel_id=1, source_target_pairs={{0,2},{2,0},{4,6},{6,4},{8,10},{10,8},{12,14},{14,12},{16,18},{18,... | collective-permute-start | bytes 786440 | tf_op jit(solution)/shard_map/ppermute | solution.py:351
  94.5 6.4 %collective-permute-start.16 = (bf16[256,512]{1,0:T(8,128)(2,1)S(1)}, bf16[256,512]{1,0:T(8,128)(2,1)S(1)}, u32[]{:S(2)}, u32[]{:S(2)}) collective-permute-start(bf16[256,512]{1,0:T(8,128)(2,1)S(1)} %pad_maximum_fusion.2), channel_id=1, source_target_pairs={{0,4},{2,6},{4,0},{6,2},{8,12},{10,14},{12,8},{14,10},{16,20},{18,... | collective-permute-start | bytes 786440 | tf_op jit(solution)/shard_map/ppermute | solution.py:351
  (8 other events, 5.9 us)

commit v4 on v3

--- a/solution.py
+++ b/solution.py
@@ -14,6 +14,8 @@
 SPAN = PANEL // 8
 BLOCK = 8
 ROWS = BLOCK * SPAN
+FRONT = 34
+BACK = 14
 BINS = 40
 GROUP = 10
 WINDOW = 2 * GROUP + 1
@@ -119,8 +121,8 @@
 
 def forward_kernel(
     incoming, band, taps_a, taps_b, point_a, point_b, rows, linear_mine, linear_other, up_mine, up_other,
-    hidden_out, kept_out, features_out, standard_out, value_out, gate_out, standard_two_out, scales_out, keep_out,
-    linear_s, up_s, pick_s, ext_s, x_s, first_s, spread_s, even_s, odd_s, flat_s, gated_s, sems,
+    give_0, give_1, give_2, give_3, features_out, value_out, gate_out, standard_two_out, scale_out, keep_out,
+    linear_s, up_s, pick_s, ext_s, x_s, first_s, spread_s, even_s, odd_s, flat_s, gated_s, kept_s, sems,
 ):
     step = pl.program_id(0)
     me = lax.axis_index("fsdp")
@@ -224,7 +226,6 @@
     centred = centre(features_out[...].astype(F32))
     scale_one = lax.rsqrt(jnp.mean(centred * centred, axis=1, keepdims=True) + EPSILON)
     standard = centred * scale_one
-    standard_out[...] = standard
     normed = (standard * rows[9:10, :]).astype(BF)
 
     @pl.when(step == 0)
@@ -251,24 +252,70 @@
     standard_two_out[...] = standard_two
     active = standard_two * rows[10:11, :]
     hidden = (active * jax.nn.sigmoid(active)).astype(BF)
-    hidden_out[...] = hidden
-    scales_out[:, 0:128] = jnp.broadcast_to(scale_one, (ROWS, 128))
-    scales_out[:, 128:256] = jnp.broadcast_to(scale_two, (ROWS, 128))
+    scale_out[...] = jnp.broadcast_to(scale_two, (ROWS, 128))
     kept = jnp.where(row_keep > 0, hidden, jnp.zeros_like(hidden))
     kept = dot(row_order(), kept).astype(BF)
-    kept_out[me] = kept[:, :half]
-    kept_out[1 - me] = kept[:, half:]
+    count = kept_s.shape[0]
+    for n in range(count):
+        kept_s[n] = kept[:, n * 128 : (n + 1) * 128]
+    plane = lax.axis_index("dp") % 4
+    for offset, give in enumerate((give_0, give_1, give_2, give_3)):
+        quarter = plane ^ offset
+        give[0] = kept_s[me * (count // 2) + quarter]
+        give[1] = kept_s[(1 - me) * (count // 2) + quarter]
+
+
+def near_kernel(*refs):
+    left = jnp.concatenate([ref[0] for ref in refs[0:4]], axis=0)
+    right = jnp.concatenate([ref[...] for ref in refs[4:8]], axis=0)
+    refs[8][...] = dot(left, right, DOWN)
+
+
+def far_kernel(groups, *refs):
+    first, gifts, theirs, planes, outs, total = refs[0], refs[1:5], refs[5], refs[6], refs[7:-1], refs[-1]
+    left = jnp.concatenate([ref[1] for ref in gifts], axis=0)
+    right = jnp.concatenate([theirs[...]] + [planes[n] for n in range(3)], axis=0)
+    total[...] = first[...] + dot(left, right, DOWN)
+    me = lax.axis_index("dp") // 4
+    size = total.shape[0] // (groups // 4)
+    for offset, out in enumerate(outs):
+        at = pl.multiple_of((me ^ offset) * size, size)
+        out[...] = total[pl.ds(at, size), :].astype(out.dtype)
+
+
+def layers_kernel(*refs):
+    pieces, left, right, total = refs[:-3], refs[-3], refs[-2], refs[-1]
+    me = lax.axis_index("dp") // 4
+    size = pieces[0].shape[0]
+    for offset, piece in enumerate(pieces):
+        at = pl.multiple_of((me ^ offset) * size, size)
+        total[pl.ds(at, size), :] = piece[...].astype(F32)
+    half = left.shape[1]
+    left[...] = total[:, :half].astype(BF)
+    right[...] = total[:, half:].astype(BF)
+
+
+def finish_kernel(*refs):
+    lefts, rights, out = refs[0:4], refs[4:8], refs[8]
+    plane = lax.axis_index("dp") % 4
+    size, half = lefts[0].shape
+    for offset in range(4):
+        at = pl.multiple_of((plane ^ offset) * size, size)
+        out[pl.ds(at, size), :half] = lefts[offset][...].astype(F32)
+        out[pl.ds(at, size), half:] = rights[offset][...].astype(F32)
 
 
 def backward_kernel(
-    hidden_in, features_in, standard_in, value_in, gate_in, standard_two_in, scales_in, keep_in, rows, cotangent,
-    down_mine, down_other, up_mine, up_other,
-    layer_out, grad_out,
+    features_in, value_in, gate_in, standard_two_in, scale_in, keep_in, rows, cotangent,
+    down_mine, down_other, up_mine, up_other, plane_1, plane_2, plane_3,
+    layer_out, grad_out, planes_out,
     down_s, up_s, depth_s, sems,
 ):
     step = pl.program_id(0)
     me = lax.axis_index("fsdp")
     copies = fetch(((down_mine, down_other, down_s), (up_mine, up_other, up_s)), sems, me)
+    for n, plane in enumerate((plane_1, plane_2, plane_3)):
+        copies.append(pltpu.make_async_copy(plane, planes_out.at[n], sems.at[4 + n]))
 
     @pl.when(step == 0)
     def _():
@@ -283,6 +330,11 @@
     active = standard_two * rows[10:11, :]
     swish = jax.nn.sigmoid(active)
     slope = (swish + active * swish * (1.0 - swish)) * rows[10:11, :]
+    hidden = (active * swish).astype(BF)
+    values = features_in[...].astype(F32)
+    centred = centre(values)
+    scale_one = lax.rsqrt(jnp.mean(centred * centred, axis=1, keepdims=True) + EPSILON)
+    standard = centred * scale_one
 
     @pl.when(step == 0)
     def _():
@@ -290,13 +342,12 @@
         copies[1].wait()
 
     half = down_s.shape[1]
-    mixed = dot(hidden_in[:, :half], down_s[0]) + dot(hidden_in[:, half:], down_s[1])
-    layer = jnp.where(row_keep > 0, features_in[...].astype(F32) + mixed, 0.0).astype(BF)
+    mixed = dot(hidden[:, :half], down_s[0]) + dot(hidden[:, half:], down_s[1])
+    layer = jnp.where(row_keep > 0, values + mixed, 0.0).astype(BF)
     layer_out[...] = dot(order, layer).astype(BF)
     back_hidden = jnp.concatenate([dot(back_bf, down_s[0], ACROSS), dot(back_bf, down_s[1], ACROSS)], axis=1)
     gain_up = back_hidden * slope
-    scale_one = scales_in[:, 0:1]
-    scale_two = scales_in[:, 128:129]
+    scale_two = scale_in[:, 0:1]
     back_depth = scale_two * (
         gain_up
         - jnp.mean(gain_up, axis=1, keepdims=True)
@@ -322,7 +373,6 @@
 
     back_normed = dot(back_value.astype(BF), up_s[0], ACROSS) + dot(back_gate, up_s[1], ACROSS)
     gain_in = back_normed * rows[9:10, :]
-    standard = standard_in[...]
     back_input = scale_one * (
         gain_in
         - jnp.mean(gain_in, axis=1, keepdims=True)
@@ -330,6 +380,11 @@
     )
     grad_out[...] = dot(order, (back_out + back_input).astype(BF)).astype(BF)
 
+    @pl.when(step == 0)
+    def _():
+        for copy in copies[4:]:
+            copy.wait()
+
 
 def whole(shape):
     return pl.BlockSpec(shape, lambda g: (0,) * len(shape))
@@ -347,51 +402,19 @@
     return lax.ppermute(block, "fsdp", [(0, 1), (1, 0)])
 
 
-def swap_bit(block, bit, groups):
-    return lax.ppermute(block, "dp", [(i, i ^ (1 << bit)) for i in range(groups)])
-
-
-def pick(block, index):
-    return lax.dynamic_index_in_dim(block, index, axis=0, keepdims=False)
-
-
-def halve(total, bit, groups, beside=()):
-    side = (lax.axis_index("dp") >> bit) & 1
-    pair = total.reshape(2, total.shape[0] // 2, total.shape[1])
-    given = swap_bit(pick(pair, 1 - side).astype(jnp.bfloat16), bit, groups)
-    if beside:
-        given, *beside = lax.optimization_barrier((given, *beside))
-    return pick(pair, side) + given.astype(jnp.float32), beside
-
-
-def double(block, bit, groups):
-    side = (lax.axis_index("dp") >> bit) & 1
-    given = swap_bit(block, bit, groups)
-    return jnp.concatenate(
-        [jnp.where(side == 0, block, given), jnp.where(side == 0, given, block)], axis=0
-    )
-
-
-def sum_over_dp(total, scale, groups, beside):
-    bits = groups.bit_length() - 1
-    half = total.shape[1] // 2
-    orders = ([0, 1], [1, 0])
-    parts = [total[:, :half], total[:, half:]]
-    parts[0], beside = halve(parts[0], orders[0][0], groups, beside)
-    parts[1], _ = halve(parts[1], orders[1][0], groups)
-    parts = [halve(part, order[1], groups)[0] for part, order in zip(parts, orders)]
-    joined = jnp.concatenate(parts, axis=1)
-    for bit in range(2, bits - 1):
-        joined, _ = halve(joined, bit, groups)
-    rounded = joined.astype(jnp.bfloat16)
-    given = swap_bit(rounded, bits - 1, groups)
-    block = ((rounded.astype(jnp.float32) + given.astype(jnp.float32)) * scale).astype(jnp.bfloat16)
-    for bit in reversed(range(2, bits - 1)):
-        block = double(block, bit, groups)
-    parts = [block[:, :half], block[:, half:]]
-    for step in reversed(range(2)):
-        parts = [double(part, order[step], groups) for part, order in zip(parts, orders)]
-    return jnp.concatenate(parts, axis=1).astype(jnp.float32), beside
+def swap_rank(block, offset, groups):
+    return lax.ppermute(block, "dp", [(i, i ^ offset) for i in range(groups)])
+
+
+def held_call(kernel, outs, scratch, name, *operands):
+    return pl.pallas_call(
+        kernel,
+        out_shape=outs,
+        scratch_shapes=scratch,
+        compiler_params=params(32),
+        cost_estimate=cost(1e6, 1e5),
+        name=name,
+    )(*operands)
 
 
 def local(
@@ -441,6 +464,7 @@
     linear_other = swap_cores(linear_weight)
     up_other = swap_cores(up_weight)
     down_other = swap_cores(down_weight)
+    cotangents = [cotangent] + [swap_rank(cotangent, offset, groups) for offset in range(1, 4)]
     cotangent_other = swap_cores(cotangent)
     band, taps_a, taps_b, point_one, point_two, rows = pl.pallas_call(
         weights_kernel,
@@ -460,7 +484,8 @@
     def by_rows(columns):
         return pl.BlockSpec((ROWS, columns), lambda g: (g, 0))
 
-    hidden, kept, features, standard, value, gate, standard_two, scales, keep = pl.pallas_call(
+    by_plane = pl.BlockSpec((members, ROWS, 128), lambda g: (0, g, 0))
+    *given, features, value, gate, standard_two, scale, keep = pl.pallas_call(
         forward_kernel,
         grid=(blocks,),
         in_specs=[
@@ -468,18 +493,16 @@
             whole(point_two.shape), whole(rows.shape), anywhere, anywhere, anywhere, anywhere,
         ],
         out_specs=[
-            by_rows(width), pl.BlockSpec((members, ROWS, half), lambda g: (0, g, 0)), by_rows(width), by_rows(width),
-            by_rows(width), by_rows(width), by_rows(width), by_rows(256), by_rows(128),
+            by_plane, by_plane, by_plane, by_plane, by_rows(width),
+            by_rows(width), by_rows(width), by_rows(width), by_rows(128), by_rows(128),
         ],
         out_shape=(
-            shape((rows_here, width), BF),
-            shape((members, rows_here, half), BF),
+            *[shape((members, rows_here, 128), BF)] * 4,
             shape((rows_here, width), BF),
             shape((rows_here, width), F32),
             shape((rows_here, width), F32),
             shape((rows_here, width), F32),
-            shape((rows_here, width), F32),
-            shape((rows_here, 256), F32),
+            shape((rows_here, 128), F32),
             shape((rows_here, 128), F32),
         ),
         scratch_shapes=[
@@ -494,39 +517,67 @@
             pltpu.VMEM((BINS // 2, ROWS + BLOCK, 256), F32),
             pltpu.VMEM((ROWS, BINS // 4 * 256), BF),
             pltpu.VMEM((ROWS + 8 * BLOCK, width), F32),
+            pltpu.VMEM((width // 128, ROWS, 128), BF),
             pltpu.SemaphoreType.DMA((4,)),
         ],
-        compiler_params=params(44),
+        compiler_params=params(FRONT + groups // 2),
         cost_estimate=cost(2e10 * blocks, 1e7),
         name="forward",
     )(incoming, band, taps_a, taps_b, point_one, point_two, rows, linear_weight, linear_other, up_weight, up_other)
-    kept_mine = kept[0]
-    kept_other = swap_cores(kept[1])
-    product = dot(kept_mine, cotangent, DOWN) + dot(kept_other, cotangent_other, DOWN)
-    scale = 1.0 / math.sqrt(rows_here * groups * members)
+    near = [swap_rank(block, offset, groups) for offset, block in enumerate(given) if offset]
     beside = pl.pallas_call(
         backward_kernel,
         grid=(blocks,),
         in_specs=[
-            by_rows(width), by_rows(width), by_rows(width), by_rows(width), by_rows(width), by_rows(width), by_rows(256),
-            by_rows(128), whole(rows.shape), by_rows(width), anywhere, anywhere, anywhere, anywhere,
+            by_rows(width), by_rows(width), by_rows(width), by_rows(width), by_rows(128), by_rows(128),
+            whole(rows.shape), by_rows(width), *[anywhere] * 7,
         ],
-        out_specs=[by_rows(width), by_rows(width)],
-        out_shape=(shape((rows_here, width), BF), shape((rows_here, width), BF)),
+        out_specs=[by_rows(width), by_rows(width), anywhere],
+        out_shape=(
+            shape((rows_here, width), BF), shape((rows_here, width), BF), shape((3, rows_here, width), BF),
+        ),
         scratch_shapes=[
             pltpu.VMEM((2,) + down_weight.shape, BF),
             pltpu.VMEM((2,) + up_weight.shape, BF),
             pltpu.VMEM((ROWS + 8 * BLOCK, width), F32),
-            pltpu.SemaphoreType.DMA((4,)),
+            pltpu.SemaphoreType.DMA((7,)),
         ],
-        compiler_params=params(60),
+        compiler_params=params(BACK),
         cost_estimate=cost(1e6, 1e5),
         name="backward",
     )(
-        hidden, features, standard, value, gate, standard_two, scales, keep, rows, cotangent,
-        down_weight, down_other, up_weight, up_other,
-    )
-    grad_down, (layer_out, grad_input) = sum_over_dp(product, scale, groups, beside)
+        features, value, gate, standard_two, scale, keep, rows, cotangent,
+        down_weight, down_other, up_weight, up_other, *cotangents[1:],
+    )
+    *near, layer_out, grad_input, planes = lax.optimization_barrier((*near, *beside))
+    near = [given[0], *near]
+    far = [swap_cores(block) for block in near]
+    planes_other = swap_cores(planes)
+    layers = groups // 4
+    block = width // members // 4
+    size = block // layers
+    half_sum = held_call(near_kernel, shape((block, width), F32), [], "near", *near, *cotangents)
+    own, *others = held_call(
+        functools.partial(far_kernel, groups),
+        [shape((size, width), F32)] + [shape((size, width), BF)] * (layers - 1),
+        [pltpu.VMEM((block, width), F32)],
+        "far",
+        half_sum, *far, cotangent_other, planes_other,
+    )
+    for offset, other in enumerate(others):
+        own = own + swap_rank(other, 4 * (offset + 1), groups).astype(F32)
+    own = (own * (1.0 / math.sqrt(rows_here * groups * members))).astype(BF)
+    pieces = [own] + [swap_rank(own, 4 * offset, groups) for offset in range(1, layers)]
+    left, right = held_call(
+        layers_kernel, [shape((block, width // 2), BF)] * 2, [pltpu.VMEM((block, width), F32)], "layers", *pieces
+    )
+    left_x, right_y = swap_rank(left, 1, groups), swap_rank(right, 2, groups)
+    left_y, right_x = swap_rank(left, 2, groups), swap_rank(right, 1, groups)
+    left_xy, right_xy = swap_rank(left_x, 2, groups), swap_rank(right_y, 1, groups)
+    grad_down = held_call(
+        finish_kernel, shape((half, width), F32), [], "finish",
+        left, left_x, left_y, left_xy, right, right_x, right_y, right_xy,
+    )
     return (layer_out, grad_input, grad_down)
 
 

time: 103 us -> 88.5 us (0.86)
  waiting for transfers between devices: 39.2 us -> 20.7 us
  starting transfers between devices: 26.9 us -> 33.2 us
  Pallas kernels: 23 us -> 25.2 us
  other arithmetic: 2.21 us -> 0.04 us
  local copies, waits for them, and re-layouts: 9.52 us -> 8.15 us
    ppermute x11 -> x18, waiting for transfers between devices: 29.3 us -> 15.1 us  [swap_rank(): return lax.ppermute(block, 'dp', [(i, i ^ offset) for i in range(groups)])]
    ppermute x11 -> x18, starting transfers between devices: 16.9 us -> 22.9 us  [swap_rank(): return lax.ppermute(block, 'dp', [(i, i ^ offset) for i in range(groups)])]
    all_to_all x1, waiting for transfers between devices: 7.92 us -> 4.06 us  [local(): lax.all_to_all(outgoing, 'dp', split_axis=0, concat_axis=0, tiled=True)]
    pallas_call x0 -> x4, Pallas kernels: none -> 3.26 us  [held_call(): pl.pallas_call(kernel, out_shape=outs, scratch_shapes=scratch, compiler_p...]
    pallas_call x1, Pallas kernels: 7.92 us -> 5.77 us  [local(): pl.pallas_call(backward_kernel, grid=(blocks,), in_specs=[by_rows(width),...]
    convert_element_type x3 -> x1, other arithmetic: 1.66 us -> 0.04 us  [local(): own = (own * (1.0 / math.sqrt(rows_here * groups * members))).astype(BF)]
    pallas_call x1, Pallas kernels: 11.6 us -> 12.7 us  [local(): pl.pallas_call(forward_kernel, grid=(blocks,), in_specs=[whole(incoming.s...]
    unnamed x28 -> x22, local copies, waits for them, and re-layouts: 9.15 us -> 8.15 us
  transfers between devices with their start and end apart: 18 -> 29, of which waited for: 12 -> 9; matrix products, arithmetic and copies ran while one was open for 2% -> 0% of each run, Pallas kernels for 20% -> 23%
where the time goes in v4:
time: 88.5 us; the launch traced here: 88.1 us
  starting transfers between devices  33.2 us (38%)
  Pallas kernels  25.2 us (28%)
  waiting for transfers between devices  20.7 us (23%)
  local copies, waits for them, and re-layouts  8.15 us (9%)
    ppermute x18, starting transfers between devices, swap_rank(): return lax.ppermute(block, 'dp', [(i, i ^ offset) for i in range(groups)])  22.9 us
    ppermute x18, waiting for transfers between devices, swap_rank(): return lax.ppermute(block, 'dp', [(i, i ^ offset) for i in range(groups)])  15.1 us
    pallas_call x1, Pallas kernels, local(): pl.pallas_call(forward_kernel, grid=(blocks,), in_specs=[whole(incoming.s...  12.7 us
    all_to_all x1, starting transfers between devices, local(): lax.all_to_all(outgoing, 'dp', split_axis=0, concat_axis=0, tiled=True)  8.36 us
    unnamed x22, local copies, waits for them, and re-layouts  8.15 us
    pallas_call x1, Pallas kernels, local(): pl.pallas_call(backward_kernel, grid=(blocks,), in_specs=[by_rows(width),...  5.77 us
    all_to_all x1, waiting for transfers between devices, local(): lax.all_to_all(outgoing, 'dp', split_axis=0, concat_axis=0, tiled=True)  4.06 us
    pallas_call x4, Pallas kernels, held_call(): pl.pallas_call(kernel, out_shape=outs, scratch_shapes=scratch, compiler_p...  3.26 us
  transfers between devices with their start and end apart: 29, of which 9 were waited for; matrix products, arithmetic and copies ran while one was open for 0% of the time, Pallas kernels for 23%

profile of v4, /device:TPU:0, one launch (start us, length us, event | category | flops | bytes accessed | tf_op | source)
XLA Modules:
  0.0 88.1 jit_solution(2824972435591092195)
XLA Ops:
  1.2 2.9 %send.1 = (bf16[16,88,128]{2,1,0:T(8,128)(2,1)}, bf16[160,512]{1,0:T(8,128)(2,1)}) custom-call(bf16[16,10240]{1,0:T(8,128)(2,1)} %mel.1, s32[1,16]{1,0:T(1,128)} %bitcast.2, s32[1,16]{1,0:T(1,128)} %bitcast.3, bf16[9,128]{1,0:T(8,128)(2,1)} %first.1, bf16[9,128]{1,0:T(8,128)(2,1)} %depth_a.1, bf16[256,128]{1,0:T(8,128)(2,1)} %point_a.1, ...), custom_call_target="tpu_custom_call" | custom-call | flops 200000000 | bytes 1000000 | tf_op jit(solution)/shard_map/send/pallas_call | solution.py:448
  4.1 8.4 %all-to-all-start = ((bf16[16,88,128]{2,1,0:T(8,128)(2,1)}), bf16[16,88,128]{2,1,0:T(8,128)(2,1)}, u32[]{:S(2)}, u32[]{:S(2)}) async-start(bf16[16,88,128]{2,1,0:T(8,128)(2,1)} %get-tuple-element.36), calls=%async_computation | async-start | bytes 720896 | tf_op jit(solution)/shard_map/all_to_all | solution.py:462
  12.6 1.9 %collective-permute-start.7 = (bf16[128,1024]{1,0:T(8,128)(2,1)}, bf16[128,1024]{1,0:T(8,128)(2,1)S(1)}, u32[]{:S(2)}, u32[]{:S(2)}) collective-permute-start(bf16[128,1024]{1,0:T(8,128)(2,1)} %refs_4_.1), channel_id=1, source_target_pairs={{0,2},{2,0},{4,6},{6,4},{8,10},{10,8},{12,14},{14,12},{16,18},{18,... | collective-permute-start | bytes 786440 | tf_op jit(solution)/shard_map/ppermute | solution.py:406
  14.5 1.5 %collective-permute-start.8 = (bf16[128,1024]{1,0:T(8,128)(2,1)}, bf16[128,1024]{1,0:T(8,128)(2,1)}, u32[]{:S(2)}, u32[]{:S(2)}) collective-permute-start(bf16[128,1024]{1,0:T(8,128)(2,1)} %refs_4_.1), channel_id=1, source_target_pairs={{0,4},{2,6},{4,0},{6,2},{8,12},{10,14},{12,8},{14,10},{16,20},{18,... | collective-permute-start | bytes 786440 | tf_op jit(solution)/shard_map/ppermute | solution.py:406
  20.8 4.1 %all-to-all-done.incoming = bf16[16,88,128]{2,1,0:T(8,128)(2,1)} async-done(((bf16[16,88,128]{2,1,0:T(8,128)(2,1)}), bf16[16,88,128]{2,1,0:T(8,128)(2,1)}, u32[]{:S(2)}, u32[]{:S(2)}) %all-to-all-start) | async-done | bytes 360480 | tf_op jit(solution)/shard_map/all_to_all | solution.py:462
  24.8 1.7 %copy-done.3 = bf16[2560,512]{1,0:T(8,128)(2,1)S(1)} copy-done((bf16[2560,512]{1,0:T(8,128)(2,1)S(1)}, bf16[2560,512]{1,0:T(8,128)(2,1)}, u32[]{:S(2)}) %copy-start.3) | copy-done | bytes 2621464
  26.6 1.3 %copy-done.6 = bf16[256,2560]{1,0:T(8,128)(2,1)S(1)} copy-done((bf16[256,2560]{1,0:T(8,128)(2,1)S(1)}, bf16[256,2560]{1,0:T(8,128)(2,1)}, u32[]{:S(2)}) %copy-start.6) | copy-done | bytes 1310744
  29.7 12.7 %forward.1 = (bf16[2,128,128]{2,1,0:T(8,128)(2,1)S(1)}, bf16[2,128,128]{2,1,0:T(8,128)(2,1)S(1)}, bf16[2,128,128]{2,1,0:T(8,128)(2,1)S(1)}, bf16[2,128,128]{2,1,...) custom-call(bf16[16,88,128]{2,1,0:T(8,128)(2,1)} %all-to-all-done.in, ...), custom_call_target="tpu_custom_call" | custom-call | flops 20000000000 | bytes 10000000 | tf_op jit(solution)/shard_map/forward/pallas_call | solution.py:488
  44.0 2.0 %collective-permute-start.5 = (bf16[2,128,128]{2,1,0:T(8,128)(2,1)S(1)}, bf16[2,128,128]{2,1,0:T(8,128)(2,1)S(1)}, u32[]{:S(2)}, u32[]{:S(2)}) collective-permute-start(bf16[2,128,128]{2,1,0:T(8,128)(2,1)S(1)} %get-tuple-element.46), channel_id=1, source_target_pairs={{0,6},{2,4},{4,2},{6,0},{8,14},{10,12},{12,10},{14,8},{16,22},{18,... | collective-permute-start | bytes 196616 | tf_op jit(solution)/shard_map/ppermute | solution.py:406
  46.0 5.8 %backward.1 = (bf16[128,1024]{1,0:T(8,128)(2,1)}, bf16[128,1024]{1,0:T(8,128)(2,1)}, bf16[3,128,1024]{2,1,0:T(8,128)(2,1)S(1)}) custom-call(bf16[128,1024]{1,0:T(8,128)(2,1)S(1)} %get-tuple-element.47.features_in, f32[128,1024]{1,0:T(8,128)S(1)} %get-tuple-element.48.value_in, f32[128,1024]{1,0:T(8,128)S(1)} %get-tuple-element.49.gate_in, ...), custom_call_target="tpu_custom_call" | custom-call | flops 1000000 | bytes 100000 | tf_op jit(solution)/shard_map/backward/pallas_call | solution.py:528
  53.0 1.6 %collective-permute-done.14.refs_5_ = bf16[128,1024]{1,0:T(8,128)(2,1)S(1)} collective-permute-done((bf16[128,1024]{1,0:T(8,128)(2,1)S(1)}, bf16[128,1024]{1,0:T(8,128)(2,1)S(1)}, u32[]{:S(2)}, u32[]{:S(2)}) %collective-permute-start.14) | collective-permute-done | bytes 262176 | tf_op jit(solution)/shard_map/ppermute | solution.py:402
  54.7 1.4 %near.1.refs_0_ = f32[128,1024]{1,0:T(8,128)S(1)} custom-call(bf16[2,128,128]{2,1,0:T(8,128)(2,1)S(1)} %get-tuple-element.58.refs_0_, bf16[2,128,128]{2,1,0:T(8,128)(2,1)S(1)} %collective-permute-done.3.refs_1_, bf16[2,128,128]{2,1,0:T(8,128)(2,1)S(1)} %collective-permute-done.4.refs_2_, bf16[2,128,128]{2,1,0:T(8,128)(2,1)S(1)} %collective-permute-done.5.refs_3_, ...), custom_call_target="tpu_custom_call" | custom-call | flops 1000000 | bytes 100000 | tf_op jit(solution)/shard_map/near/pallas_call | solution.py:410
  56.5 1.1 %collective-permute-start.16 = (bf16[32,1024]{1,0:T(8,128)(2,1)S(1)}, bf16[32,1024]{1,0:T(8,128)(2,1)S(1)}, u32[]{:S(2)}, u32[]{:S(2)}) collective-permute-start(bf16[32,1024]{1,0:T(8,128)(2,1)S(1)} %get-tuple-element.64), channel_id=1, source_target_pairs={{0,8},{2,10},{4,12},{6,14},{8,0},{10,2},{12,4},{14,6},{16,24},{18,... | collective-permute-start | bytes 196616 | tf_op jit(solution)/shard_map/ppermute | solution.py:406
  58.5 2.4 %collective-permute-start.18 = (bf16[32,1024]{1,0:T(8,128)(2,1)S(1)}, bf16[32,1024]{1,0:T(8,128)(2,1)S(1)}, u32[]{:S(2)}, u32[]{:S(2)}) collective-permute-start(bf16[32,1024]{1,0:T(8,128)(2,1)S(1)} %get-tuple-element.66), channel_id=1, source_target_pairs={{0,24},{2,26},{4,28},{6,30},{8,16},{10,18},{12,20},{14,22},{16,8},... | collective-permute-start | bytes 196616 | tf_op jit(solution)/shard_map/ppermute | solution.py:406
  60.9 4.9 %collective-permute-done.17 = bf16[32,1024]{1,0:T(8,128)(2,1)S(1)} collective-permute-done((bf16[32,1024]{1,0:T(8,128)(2,1)S(1)}, bf16[32,1024]{1,0:T(8,128)(2,1)S(1)}, u32[]{:S(2)}, u32[]{:S(2)}) %collective-permute-start.17) | collective-permute-done | bytes 65568 | tf_op jit(solution)/shard_map/ppermute | solution.py:406
  65.9 1.5 %collective-permute-start.19 = (bf16[32,1024]{1,0:T(8,128)(2,1)S(1)}, bf16[32,1024]{1,0:T(8,128)(2,1)S(1)}, u32[]{:S(2)}, u32[]{:S(2)}) collective-permute-start(bf16[32,1024]{1,0:T(8,128)(2,1)S(1)} %multiply_convert_fusion.refs_0_), channel_id=1, source_target_pairs={{0,8},{2,10},{4,12},{6,14},{8,0},{10,2},{12,4},{14,6},{16,24},{18,... | collective-permute-start | bytes 196616 | tf_op jit(solution)/shard_map/ppermute | solution.py:406
  67.7 2.6 %collective-permute-start.21 = (bf16[32,1024]{1,0:T(8,128)(2,1)S(1)}, bf16[32,1024]{1,0:T(8,128)(2,1)S(1)}, u32[]{:S(2)}, u32[]{:S(2)}) collective-permute-start(bf16[32,1024]{1,0:T(8,128)(2,1)S(1)} %multiply_convert_fusion.refs_0_), channel_id=1, source_target_pairs={{0,24},{2,26},{4,28},{6,30},{8,16},{10,18},{12,20},{14,22},{16,8},... | collective-permute-start | bytes 196616 | tf_op jit(solution)/shard_map/ppermute | solution.py:406
  70.4 4.6 %collective-permute-done.20.refs_2_ = bf16[32,1024]{1,0:T(8,128)(2,1)S(1)} collective-permute-done((bf16[32,1024]{1,0:T(8,128)(2,1)S(1)}, bf16[32,1024]{1,0:T(8,128)(2,1)S(1)}, u32[]{:S(2)}, u32[]{:S(2)}) %collective-permute-start.20) | collective-permute-done | bytes 65568 | tf_op jit(solution)/shard_map/ppermute | solution.py:406
  76.7 1.1 %collective-permute-start.23 = (bf16[128,512]{1,0:T(8,128)(2,1)S(1)}, bf16[128,512]{1,0:T(8,128)(2,1)S(1)}, u32[]{:S(2)}, u32[]{:S(2)}) collective-permute-start(bf16[128,512]{1,0:T(8,128)(2,1)S(1)} %get-tuple-element.67.refs_0_), channel_id=1, source_target_pairs={{0,4},{2,6},{4,0},{6,2},{8,12},{10,14},{12,8},{14,10},{16,20},{18,... | collective-permute-start | bytes 393224 | tf_op jit(solution)/shard_map/ppermute | solution.py:406
  77.7 1.5 %collective-permute-start.25 = (bf16[128,512]{1,0:T(8,128)(2,1)S(1)}, bf16[128,512]{1,0:T(8,128)(2,1)S(1)}, u32[]{:S(2)}, u32[]{:S(2)}) collective-permute-start(bf16[128,512]{1,0:T(8,128)(2,1)S(1)} %get-tuple-element.68.refs_4_), channel_id=1, source_target_pairs={{0,2},{2,0},{4,6},{6,4},{8,10},{10,8},{12,14},{14,12},{16,18},{18,... | collective-permute-start | bytes 393224 | tf_op jit(solution)/shard_map/ppermute | solution.py:406
  79.2 1.5 %collective-permute-done.22.refs_1_ = bf16[128,512]{1,0:T(8,128)(2,1)S(1)} collective-permute-done((bf16[128,512]{1,0:T(8,128)(2,1)S(1)}, bf16[128,512]{1,0:T(8,128)(2,1)S(1)}, u32[]{:S(2)}, u32[]{:S(2)}) %collective-permute-start.22) | collective-permute-done | bytes 131104 | tf_op jit(solution)/shard_map/ppermute | solution.py:406
  81.7 1.6 %collective-permute-start.27 = (bf16[128,512]{1,0:T(8,128)(2,1)S(1)}, bf16[128,512]{1,0:T(8,128)(2,1)S(1)}, u32[]{:S(2)}, u32[]{:S(2)}) collective-permute-start(bf16[128,512]{1,0:T(8,128)(2,1)S(1)} %collective-permute-done.26.refs_6_), channel_id=1, source_target_pairs={{0,2},{2,0},{4,6},{6,4},{8,10},{10,8},{12,14},{14,12},{16,18},{18,... | collective-permute-start | bytes 393224 | tf_op jit(solution)/shard_map/ppermute | solution.py:406
  83.5 2.2 %collective-permute-done.24.refs_3_ = bf16[128,512]{1,0:T(8,128)(2,1)S(1)} collective-permute-done((bf16[128,512]{1,0:T(8,128)(2,1)S(1)}, bf16[128,512]{1,0:T(8,128)(2,1)S(1)}, u32[]{:S(2)}, u32[]{:S(2)}) %collective-permute-start.24) | collective-permute-done | bytes 131104 | tf_op jit(solution)/shard_map/ppermute | solution.py:406
  86.6 1.5 %finish.1 = f32[512,1024]{1,0:T(8,128)} custom-call(bf16[128,512]{1,0:T(8,128)(2,1)S(1)} %get-tuple-element.67.refs_0_, bf16[128,512]{1,0:T(8,128)(2,1)S(1)} %collective-permute-done.22.refs_1_, bf16[128,512]{1,0:T(8,128)(2,1)S(1)} %collective-permute-done.23.refs_2_, bf16[128,512]{1,0:T(8,128)(2,1)S(1)} %collective-permute-done.24.refs_3_, ...), custom_call_target="tpu_custom_call" | custom-call | flops 1000000 | bytes 100000 | tf_op jit(solution)/shard_map/finish/pallas_call | solution.py:410
  (65 shorter events, 15.5 us)
Async XLA Ops:
  0.6 24.2 %collective-permute-start.1 = (bf16[2560,512]{1,0:T(8,128)(2,1)}, bf16[2560,512]{1,0:T(8,128)(2,1)}, u32[]{:S(2)}, u32[]{:S(2)}) collective-permute-start(bf16[2560,512]{1,0:T(8,128)(2,1)} %linear_mine.1), channel_id=1, source_target_pairs={{0,1},{1,0},{2,3},{3,2},{4,5},{5,4},{6,7},{7,6},{8,9},{9,8},{10,11... | collective-permute-start | bytes 7864328 | tf_op jit(solution)/shard_map/ppermute | solution.py:402
  1.2 19.6 %collective-permute-start.2 = (bf16[1024,1024]{1,0:T(8,128)(2,1)}, bf16[1024,1024]{1,0:T(8,128)(2,1)}, u32[]{:S(2)}, u32[]{:S(2)}) collective-permute-start(bf16[1024,1024]{1,0:T(8,128)(2,1)} %up_mine.3), channel_id=1, source_target_pairs={{0,1},{1,0},{2,3},{3,2},{4,5},{5,4},{6,7},{7,6},{8,9},{9,8},{10,11... | collective-permute-start | bytes 6291464 | tf_op jit(solution)/shard_map/ppermute | solution.py:402
  4.1 20.7 %all-to-all-start = ((bf16[16,88,128]{2,1,0:T(8,128)(2,1)}), bf16[16,88,128]{2,1,0:T(8,128)(2,1)}, u32[]{:S(2)}, u32[]{:S(2)}) async-start(bf16[16,88,128]{2,1,0:T(8,128)(2,1)} %get-tuple-element.36), calls=%async_computation | async-start | bytes 720896 | tf_op jit(solution)/shard_map/all_to_all | solution.py:462
  12.6 30.5 %collective-permute-start.7 = (bf16[128,1024]{1,0:T(8,128)(2,1)}, bf16[128,1024]{1,0:T(8,128)(2,1)S(1)}, u32[]{:S(2)}, u32[]{:S(2)}) collective-permute-start(bf16[128,1024]{1,0:T(8,128)(2,1)} %refs_4_.1), channel_id=1, source_target_pairs={{0,2},{2,0},{4,6},{6,4},{8,10},{10,8},{12,14},{14,12},{16,18},{18,... | collective-permute-start | bytes 786440 | tf_op jit(solution)/shard_map/ppermute | solution.py:406
  14.5 29.5 %collective-permute-start.8 = (bf16[128,1024]{1,0:T(8,128)(2,1)}, bf16[128,1024]{1,0:T(8,128)(2,1)}, u32[]{:S(2)}, u32[]{:S(2)}) collective-permute-start(bf16[128,1024]{1,0:T(8,128)(2,1)} %refs_4_.1), channel_id=1, source_target_pairs={{0,4},{2,6},{4,0},{6,2},{8,12},{10,14},{12,8},{14,10},{16,20},{18,... | collective-permute-start | bytes 786440 | tf_op jit(solution)/shard_map/ppermute | solution.py:406
  15.9 30.1 %collective-permute-start.9 = (bf16[128,1024]{1,0:T(8,128)(2,1)}, bf16[128,1024]{1,0:T(8,128)(2,1)}, u32[]{:S(2)}, u32[]{:S(2)}) collective-permute-start(bf16[128,1024]{1,0:T(8,128)(2,1)} %refs_4_.1), channel_id=1, source_target_pairs={{0,6},{2,4},{4,2},{6,0},{8,14},{10,12},{12,10},{14,8},{16,22},{18,... | collective-permute-start | bytes 786440 | tf_op jit(solution)/shard_map/ppermute | solution.py:406
  20.8 25.2 %collective-permute-start.6 = (bf16[512,1024]{1,0:T(8,128)(2,1)}, bf16[512,1024]{1,0:T(8,128)(2,1)S(1)}, u32[]{:S(2)}, u32[]{:S(2)}) collective-permute-start(bf16[512,1024]{1,0:T(8,128)(2,1)} %down_mine.1), channel_id=1, source_target_pairs={{0,1},{1,0},{2,3},{3,2},{4,5},{5,4},{6,7},{7,6},{8,9},{9,8},{10,11... | collective-permute-start | bytes 3145736 | tf_op jit(solution)/shard_map/ppermute | solution.py:402
  42.4 9.4 %collective-permute-start.3 = (bf16[2,128,128]{2,1,0:T(8,128)(2,1)S(1)}, bf16[2,128,128]{2,1,0:T(8,128)(2,1)S(1)}, u32[]{:S(2)}, u32[]{:S(2)}) collective-permute-start(bf16[2,128,128]{2,1,0:T(8,128)(2,1)S(1)} %get-tuple-element.44), channel_id=1, source_target_pairs={{0,2},{2,0},{4,6},{6,4},{8,10},{10,8},{12,14},{14,12},{16,18},{18,... | collective-permute-start | bytes 196616 | tf_op jit(solution)/shard_map/ppermute | solution.py:406
  43.1 8.7 %collective-permute-start.4 = (bf16[2,128,128]{2,1,0:T(8,128)(2,1)S(1)}, bf16[2,128,128]{2,1,0:T(8,128)(2,1)S(1)}, u32[]{:S(2)}, u32[]{:S(2)}) collective-permute-start(bf16[2,128,128]{2,1,0:T(8,128)(2,1)S(1)} %get-tuple-element.45), channel_id=1, source_target_pairs={{0,4},{2,6},{4,0},{6,2},{8,12},{10,14},{12,8},{14,10},{16,20},{18,... | collective-permute-start | bytes 196616 | tf_op jit(solution)/shard_map/ppermute | solution.py:406
  44.0 7.8 %collective-permute-start.5 = (bf16[2,128,128]{2,1,0:T(8,128)(2,1)S(1)}, bf16[2,128,128]{2,1,0:T(8,128)(2,1)S(1)}, u32[]{:S(2)}, u32[]{:S(2)}) collective-permute-start(bf16[2,128,128]{2,1,0:T(8,128)(2,1)S(1)} %get-tuple-element.46), channel_id=1, source_target_pairs={{0,6},{2,4},{4,2},{6,0},{8,14},{10,12},{12,10},{14,8},{16,22},{18,... | collective-permute-start | bytes 196616 | tf_op jit(solution)/shard_map/ppermute | solution.py:406
  51.8 4.3 %collective-permute-start.15 = (bf16[3,128,1024]{2,1,0:T(8,128)(2,1)S(1)}, bf16[3,128,1024]{2,1,0:T(8,128)(2,1)S(1)}, u32[]{:S(2)}, u32[]{:S(2)}) collective-permute-start(bf16[3,128,1024]{2,1,0:T(8,128)(2,1)S(1)} %get-tuple-element.62), channel_id=1, source_target_pairs={{0,1},{1,0},{2,3},{3,2},{4,5},{5,4},{6,7},{7,6},{8,9},{9,8},{10,11... | collective-permute-start | bytes 2359304 | tf_op jit(solution)/shard_map/ppermute | solution.py:402
  52.4 3.7 %collective-permute-start.10 = (bf16[2,128,128]{2,1,0:T(8,128)(2,1)S(1)}, bf16[2,128,128]{2,1,0:T(8,128)(2,1)S(1)}, u32[]{:S(2)}, u32[]{:S(2)}) collective-permute-start(bf16[2,128,128]{2,1,0:T(8,128)(2,1)S(1)} %get-tuple-element.58.refs_0_), channel_id=1, source_target_pairs={{0,1},{1,0},{2,3},{3,2},{4,5},{5,4},{6,7},{7,6},{8,9},{9,8},{10,11... | collective-permute-start | bytes 196616 | tf_op jit(solution)/shard_map/ppermute | solution.py:402
  56.5 4.5 %collective-permute-start.16 = (bf16[32,1024]{1,0:T(8,128)(2,1)S(1)}, bf16[32,1024]{1,0:T(8,128)(2,1)S(1)}, u32[]{:S(2)}, u32[]{:S(2)}) collective-permute-start(bf16[32,1024]{1,0:T(8,128)(2,1)S(1)} %get-tuple-element.64), channel_id=1, source_target_pairs={{0,8},{2,10},{4,12},{6,14},{8,0},{10,2},{12,4},{14,6},{16,24},{18,... | collective-permute-start | bytes 196616 | tf_op jit(solution)/shard_map/ppermute | solution.py:406
  57.6 8.3 %collective-permute-start.17 = (bf16[32,1024]{1,0:T(8,128)(2,1)S(1)}, bf16[32,1024]{1,0:T(8,128)(2,1)S(1)}, u32[]{:S(2)}, u32[]{:S(2)}) collective-permute-start(bf16[32,1024]{1,0:T(8,128)(2,1)S(1)} %get-tuple-element.65), channel_id=1, source_target_pairs={{0,16},{2,18},{4,20},{6,22},{8,24},{10,26},{12,28},{14,30},{16,0},... | collective-permute-start | bytes 196616 | tf_op jit(solution)/shard_map/ppermute | solution.py:406
  58.5 7.3 %collective-permute-start.18 = (bf16[32,1024]{1,0:T(8,128)(2,1)S(1)}, bf16[32,1024]{1,0:T(8,128)(2,1)S(1)}, u32[]{:S(2)}, u32[]{:S(2)}) collective-permute-start(bf16[32,1024]{1,0:T(8,128)(2,1)S(1)} %get-tuple-element.66), channel_id=1, source_target_pairs={{0,24},{2,26},{4,28},{6,30},{8,16},{10,18},{12,20},{14,22},{16,8},... | collective-permute-start | bytes 196616 | tf_op jit(solution)/shard_map/ppermute | solution.py:406
  65.9 4.5 %collective-permute-start.19 = (bf16[32,1024]{1,0:T(8,128)(2,1)S(1)}, bf16[32,1024]{1,0:T(8,128)(2,1)S(1)}, u32[]{:S(2)}, u32[]{:S(2)}) collective-permute-start(bf16[32,1024]{1,0:T(8,128)(2,1)S(1)} %multiply_convert_fusion.refs_0_), channel_id=1, source_target_pairs={{0,8},{2,10},{4,12},{6,14},{8,0},{10,2},{12,4},{14,6},{16,24},{18,... | collective-permute-start | bytes 196616 | tf_op jit(solution)/shard_map/ppermute | solution.py:406
  67.5 7.5 %collective-permute-start.20 = (bf16[32,1024]{1,0:T(8,128)(2,1)S(1)}, bf16[32,1024]{1,0:T(8,128)(2,1)S(1)}, u32[]{:S(2)}, u32[]{:S(2)}) collective-permute-start(bf16[32,1024]{1,0:T(8,128)(2,1)S(1)} %multiply_convert_fusion.refs_0_), channel_id=1, source_target_pairs={{0,16},{2,18},{4,20},{6,22},{8,24},{10,26},{12,28},{14,30},{16,0},... | collective-permute-start | bytes 196616 | tf_op jit(solution)/shard_map/ppermute | solution.py:406
  67.7 7.3 %collective-permute-start.21 = (bf16[32,1024]{1,0:T(8,128)(2,1)S(1)}, bf16[32,1024]{1,0:T(8,128)(2,1)S(1)}, u32[]{:S(2)}, u32[]{:S(2)}) collective-permute-start(bf16[32,1024]{1,0:T(8,128)(2,1)S(1)} %multiply_convert_fusion.refs_0_), channel_id=1, source_target_pairs={{0,24},{2,26},{4,28},{6,30},{8,16},{10,18},{12,20},{14,22},{16,8},... | collective-permute-start | bytes 196616 | tf_op jit(solution)/shard_map/ppermute | solution.py:406
  75.1 5.6 %collective-permute-start.22 = (bf16[128,512]{1,0:T(8,128)(2,1)S(1)}, bf16[128,512]{1,0:T(8,128)(2,1)S(1)}, u32[]{:S(2)}, u32[]{:S(2)}) collective-permute-start(bf16[128,512]{1,0:T(8,128)(2,1)S(1)} %get-tuple-element.67.refs_0_), channel_id=1, source_target_pairs={{0,2},{2,0},{4,6},{6,4},{8,10},{10,8},{12,14},{14,12},{16,18},{18,... | collective-permute-start | bytes 393224 | tf_op jit(solution)/shard_map/ppermute | solution.py:406
  75.7 6.0 %collective-permute-start.26 = (bf16[128,512]{1,0:T(8,128)(2,1)S(1)}, bf16[128,512]{1,0:T(8,128)(2,1)S(1)}, u32[]{:S(2)}, u32[]{:S(2)}) collective-permute-start(bf16[128,512]{1,0:T(8,128)(2,1)S(1)} %get-tuple-element.68.refs_4_), channel_id=1, source_target_pairs={{0,4},{2,6},{4,0},{6,2},{8,12},{10,14},{12,8},{14,10},{16,20},{18,... | collective-permute-start | bytes 393224 | tf_op jit(solution)/shard_map/ppermute | solution.py:406
  76.7 6.8 %collective-permute-start.23 = (bf16[128,512]{1,0:T(8,128)(2,1)S(1)}, bf16[128,512]{1,0:T(8,128)(2,1)S(1)}, u32[]{:S(2)}, u32[]{:S(2)}) collective-permute-start(bf16[128,512]{1,0:T(8,128)(2,1)S(1)} %get-tuple-element.67.refs_0_), channel_id=1, source_target_pairs={{0,4},{2,6},{4,0},{6,2},{8,12},{10,14},{12,8},{14,10},{16,20},{18,... | collective-permute-start | bytes 393224 | tf_op jit(solution)/shard_map/ppermute | solution.py:406
  77.7 5.8 %collective-permute-start.25 = (bf16[128,512]{1,0:T(8,128)(2,1)S(1)}, bf16[128,512]{1,0:T(8,128)(2,1)S(1)}, u32[]{:S(2)}, u32[]{:S(2)}) collective-permute-start(bf16[128,512]{1,0:T(8,128)(2,1)S(1)} %get-tuple-element.68.refs_4_), channel_id=1, source_target_pairs={{0,2},{2,0},{4,6},{6,4},{8,10},{10,8},{12,14},{14,12},{16,18},{18,... | collective-permute-start | bytes 393224 | tf_op jit(solution)/shard_map/ppermute | solution.py:406
  80.7 5.0 %collective-permute-start.24 = (bf16[128,512]{1,0:T(8,128)(2,1)S(1)}, bf16[128,512]{1,0:T(8,128)(2,1)S(1)}, u32[]{:S(2)}, u32[]{:S(2)}) collective-permute-start(bf16[128,512]{1,0:T(8,128)(2,1)S(1)} %collective-permute-done.22.refs_1_), channel_id=1, source_target_pairs={{0,4},{2,6},{4,0},{6,2},{8,12},{10,14},{12,8},{14,10},{16,20},{18,... | collective-permute-start | bytes 393224 | tf_op jit(solution)/shard_map/ppermute | solution.py:406
  81.7 5.0 %collective-permute-start.27 = (bf16[128,512]{1,0:T(8,128)(2,1)S(1)}, bf16[128,512]{1,0:T(8,128)(2,1)S(1)}, u32[]{:S(2)}, u32[]{:S(2)}) collective-permute-start(bf16[128,512]{1,0:T(8,128)(2,1)S(1)} %collective-permute-done.26.refs_6_), channel_id=1, source_target_pairs={{0,2},{2,0},{4,6},{6,4},{8,10},{10,8},{12,14},{14,12},{16,18},{18,... | collective-permute-start | bytes 393224 | tf_op jit(solution)/shard_map/ppermute | solution.py:406
  (16 other events, 79.3 us)

commit v5 on v4

--- a/solution.py
+++ b/solution.py
@@ -14,8 +14,8 @@
 SPAN = PANEL // 8
 BLOCK = 8
 ROWS = BLOCK * SPAN
-FRONT = 34
-BACK = 14
+FRONT = 60
+BACK = 61
 BINS = 40
 GROUP = 10
 WINDOW = 2 * GROUP + 1
@@ -83,12 +83,8 @@
     packed[32:160, 384:512] = point_b_s[128:256, :]
 
 
-def weights_kernel(mine, other, band, taps_a, taps_b, point_a, point_b, rows):
-    me = lax.axis_index("fsdp")
-    near = mine[...].astype(F32)
-    far = other[...].astype(F32)
-    low = jnp.where(me == 0, near, far)
-    high = jnp.where(me == 0, far, near)
+def unpack_weights(low, high, band, taps_a, taps_b, point_a, point_b, rows):
+    low, high = low[...].astype(F32), high[...].astype(F32)
     rows[:, 0:512] = low[0:16]
     rows[:, 512:1024] = high[0:16]
     first = jnp.concatenate([low[16:32, 0:128], high[16:32, 0:128]], axis=1).astype(BF)
@@ -120,18 +116,39 @@
 
 
 def forward_kernel(
-    incoming, band, taps_a, taps_b, point_a, point_b, rows, linear_mine, linear_other, up_mine, up_other,
-    give_0, give_1, give_2, give_3, features_out, value_out, gate_out, standard_two_out, scale_out, keep_out,
-    linear_s, up_s, pick_s, ext_s, x_s, first_s, spread_s, even_s, odd_s, flat_s, gated_s, kept_s, sems,
+    incoming_in, packed_mine, packed_other, linear_mine, linear_other, up_mine, up_other,
+    give_0, give_1, give_2, give_3, features_o, value_o, gate_o, standard_two_o, scale_o, keep_o, rows_o,
+    incoming, features_out, value_out, gate_out, standard_two_out, scale_out, keep_out, rows, packed_s, band, taps_a, taps_b, point_a, point_b, linear_s, up_s, pick_s, ext_s, x_s, first_s, spread_s, even_s, odd_s, flat_s, gated_s, kept_s, sems, out_sems,
 ):
     step = pl.program_id(0)
     me = lax.axis_index("fsdp")
-    copies = fetch(((linear_mine, linear_other, linear_s), (up_mine, up_other, up_s)), sems, me)
-
-    @pl.when(step == 0)
-    def _():
-        for copy in copies:
+    copies = fetch(
+        ((packed_mine, packed_other, packed_s), (linear_mine, linear_other, linear_s), (up_mine, up_other, up_s)), sems, me
+    )
+
+    copies.append(pltpu.make_async_copy(incoming_in, incoming, sems.at[len(copies)]))
+    here = pl.ds(step * ROWS, ROWS)
+    held = (features_out, value_out, gate_out, standard_two_out, scale_out, keep_out)
+    saves = [
+        pltpu.make_async_copy(source, out.at[here], out_sems.at[n])
+        for n, (source, out) in enumerate(zip(held, (features_o, value_o, gate_o, standard_two_o, scale_o, keep_o)))
+    ]
+    save_rows = pltpu.make_async_copy(rows, rows_o, out_sems.at[len(saves)])
+
+    @pl.when(step == 0)
+    def _():
+        for copy in copies[:2] + copies[6:]:
             copy.start()
+        copies[0].wait()
+        copies[1].wait()
+        unpack_weights(packed_s.at[0], packed_s.at[1], band, taps_a, taps_b, point_a, point_b, rows)
+
+    @pl.when(step == 0)
+    def _():
+        copies[6].wait()
+        for copy in copies[2:6]:
+            copy.start()
+        save_rows.start()
 
     sources = incoming.shape[0]
     lanes = incoming.shape[1] - 8
@@ -217,12 +234,14 @@
 
     @pl.when(step == 0)
     def _():
-        copies[0].wait()
-        copies[1].wait()
+        copies[2].wait()
+        copies[3].wait()
 
     half = linear_s.shape[2]
     for side in range(2):
         features_out[:, side * half : (side + 1) * half] = dot(flat_s[...], linear_s[side]).astype(BF)
+    saves[0].start()
+    saves[5].start()
     centred = centre(features_out[...].astype(F32))
     scale_one = lax.rsqrt(jnp.mean(centred * centred, axis=1, keepdims=True) + EPSILON)
     standard = centred * scale_one
@@ -230,14 +249,16 @@
 
     @pl.when(step == 0)
     def _():
-        copies[2].wait()
-        copies[3].wait()
+        copies[4].wait()
+        copies[5].wait()
 
     row_keep = keep_out[:, 0:1]
     value = dot(normed, up_s[0])
     value_out[...] = value
     gate = jax.nn.sigmoid(dot(normed, up_s[1]))
     gate_out[...] = gate
+    saves[1].start()
+    saves[2].start()
     reach = 4 * BLOCK
     gated_s[0:reach, :] = jnp.zeros((reach, gated_s.shape[1]), F32)
     gated_s[reach + ROWS :, :] = jnp.zeros((reach, gated_s.shape[1]), F32)
@@ -250,9 +271,11 @@
     scale_two = lax.rsqrt(jnp.mean(centred * centred, axis=1, keepdims=True) + EPSILON)
     standard_two = centred * scale_two
     standard_two_out[...] = standard_two
+    scale_out[...] = jnp.broadcast_to(scale_two, (ROWS, 128))
+    saves[3].start()
+    saves[4].start()
     active = standard_two * rows[10:11, :]
     hidden = (active * jax.nn.sigmoid(active)).astype(BF)
-    scale_out[...] = jnp.broadcast_to(scale_two, (ROWS, 128))
     kept = jnp.where(row_keep > 0, hidden, jnp.zeros_like(hidden))
     kept = dot(row_order(), kept).astype(BF)
     count = kept_s.shape[0]
@@ -263,6 +286,17 @@
         quarter = plane ^ offset
         give[0] = kept_s[me * (count // 2) + quarter]
         give[1] = kept_s[(1 - me) * (count // 2) + quarter]
+    for save in saves:
+        save.wait()
+
+    @pl.when(step == 0)
+    def _():
+        save_rows.wait()
+
+
+def pack_kernel(*refs):
+    for n in range(4):
+        refs[4][n] = refs[n][1]
 
 
 def near_kernel(*refs):
@@ -272,9 +306,9 @@
 
 
 def far_kernel(groups, *refs):
-    first, gifts, theirs, planes, outs, total = refs[0], refs[1:5], refs[5], refs[6], refs[7:-1], refs[-1]
-    left = jnp.concatenate([ref[1] for ref in gifts], axis=0)
-    right = jnp.concatenate([theirs[...]] + [planes[n] for n in range(3)], axis=0)
+    first, gifts, theirs, outs, total = refs[0], refs[1], refs[2:6], refs[6:-1], refs[-1]
+    left = jnp.concatenate([gifts[n] for n in range(4)], axis=0)
+    right = jnp.concatenate([ref[...] for ref in theirs], axis=0)
     total[...] = first[...] + dot(left, right, DOWN)
     me = lax.axis_index("dp") // 4
     size = total.shape[0] // (groups // 4)
@@ -305,17 +339,17 @@
         out[pl.ds(at, size), half:] = rights[offset][...].astype(F32)
 
 
-def backward_kernel(
-    features_in, value_in, gate_in, standard_two_in, scale_in, keep_in, rows, cotangent,
-    down_mine, down_other, up_mine, up_other, plane_1, plane_2, plane_3,
-    layer_out, grad_out, planes_out,
-    down_s, up_s, depth_s, sems,
+def back_rows(order, cotangent, row_keep):
+    return jnp.where(row_keep > 0, dot(order, cotangent[...], DOWN), 0.0)
+
+
+def down_kernel(
+    features_in, standard_two_in, scale_in, keep_in, rows, cotangent, down_mine, down_other,
+    layer_out, depth_out,
+    down_s, sems,
 ):
     step = pl.program_id(0)
-    me = lax.axis_index("fsdp")
-    copies = fetch(((down_mine, down_other, down_s), (up_mine, up_other, up_s)), sems, me)
-    for n, plane in enumerate((plane_1, plane_2, plane_3)):
-        copies.append(pltpu.make_async_copy(plane, planes_out.at[n], sems.at[4 + n]))
+    copies = fetch(((down_mine, down_other, down_s),), sems, lax.axis_index("fsdp"))
 
     @pl.when(step == 0)
     def _():
@@ -324,52 +358,66 @@
 
     order = row_order()
     row_keep = keep_in[:, 0:1]
-    back_out = jnp.where(row_keep > 0, dot(order, cotangent[...], DOWN), 0.0)
-    back_bf = back_out.astype(BF)
+    back_out = back_rows(order, cotangent, row_keep).astype(BF)
     standard_two = standard_two_in[...]
     active = standard_two * rows[10:11, :]
     swish = jax.nn.sigmoid(active)
     slope = (swish + active * swish * (1.0 - swish)) * rows[10:11, :]
     hidden = (active * swish).astype(BF)
-    values = features_in[...].astype(F32)
-    centred = centre(values)
-    scale_one = lax.rsqrt(jnp.mean(centred * centred, axis=1, keepdims=True) + EPSILON)
-    standard = centred * scale_one
-
-    @pl.when(step == 0)
-    def _():
-        copies[0].wait()
-        copies[1].wait()
+
+    @pl.when(step == 0)
+    def _():
+        for copy in copies:
+            copy.wait()
 
     half = down_s.shape[1]
-    mixed = dot(hidden[:, :half], down_s[0]) + dot(hidden[:, half:], down_s[1])
-    layer = jnp.where(row_keep > 0, values + mixed, 0.0).astype(BF)
-    layer_out[...] = dot(order, layer).astype(BF)
-    back_hidden = jnp.concatenate([dot(back_bf, down_s[0], ACROSS), dot(back_bf, down_s[1], ACROSS)], axis=1)
+    back_hidden = jnp.concatenate([dot(back_out, down_s[0], ACROSS), dot(back_out, down_s[1], ACROSS)], axis=1)
     gain_up = back_hidden * slope
-    scale_two = scale_in[:, 0:1]
-    back_depth = scale_two * (
+    depth_out[...] = scale_in[:, 0:1] * (
         gain_up
         - jnp.mean(gain_up, axis=1, keepdims=True)
         - standard_two * jnp.mean(gain_up * standard_two, axis=1, keepdims=True)
     )
+    mixed = dot(hidden[:, :half], down_s[0]) + dot(hidden[:, half:], down_s[1])
+    layer = jnp.where(row_keep > 0, features_in[...].astype(F32) + mixed, 0.0).astype(BF)
+    layer_out[...] = dot(order, layer).astype(BF)
+
+
+def up_kernel(
+    depth_in, features_in, value_in, gate_in, keep_in, rows, cotangent, up_mine, up_other,
+    grad_out,
+    up_s, depth_s, sems,
+):
+    step = pl.program_id(0)
+    copies = fetch(((up_mine, up_other, up_s),), sems, lax.axis_index("fsdp"))
+
+    @pl.when(step == 0)
+    def _():
+        for copy in copies:
+            copy.start()
+
+    order = row_order()
+    row_keep = keep_in[:, 0:1]
+    back_out = back_rows(order, cotangent, row_keep)
+    centred = centre(features_in[...].astype(F32))
+    scale_one = lax.rsqrt(jnp.mean(centred * centred, axis=1, keepdims=True) + EPSILON)
+    standard = centred * scale_one
     reach = 4 * BLOCK
     depth_s[0:reach, :] = jnp.zeros((reach, depth_s.shape[1]), F32)
     depth_s[reach + ROWS :, :] = jnp.zeros((reach, depth_s.shape[1]), F32)
-    depth_s[reach : reach + ROWS, :] = back_depth
+    depth_s[reach : reach + ROWS, :] = depth_in[...]
     total = None
     for k in range(9):
         term = depth_s[(8 - k) * BLOCK : (8 - k) * BLOCK + ROWS, :] * rows[k : k + 1, :]
         total = term if total is None else total + term
-    back_gated = row_keep * total
     gate = gate_in[...]
-    back_value = back_gated * gate
+    back_value = row_keep * total * gate
     back_gate = (back_value * value_in[...] * (1.0 - gate)).astype(BF)
 
     @pl.when(step == 0)
     def _():
-        copies[2].wait()
-        copies[3].wait()
+        for copy in copies:
+            copy.wait()
 
     back_normed = dot(back_value.astype(BF), up_s[0], ACROSS) + dot(back_gate, up_s[1], ACROSS)
     gain_in = back_normed * rows[9:10, :]
@@ -379,11 +427,6 @@
         - standard * jnp.mean(gain_in * standard, axis=1, keepdims=True)
     )
     grad_out[...] = dot(order, (back_out + back_input).astype(BF)).astype(BF)
-
-    @pl.when(step == 0)
-    def _():
-        for copy in copies[4:]:
-            copy.wait()
 
 
 def whole(shape):
@@ -466,35 +509,18 @@
     down_other = swap_cores(down_weight)
     cotangents = [cotangent] + [swap_rank(cotangent, offset, groups) for offset in range(1, 4)]
     cotangent_other = swap_cores(cotangent)
-    band, taps_a, taps_b, point_one, point_two, rows = pl.pallas_call(
-        weights_kernel,
-        out_shape=(
-            shape((256, GROUP * 256), BF),
-            shape((16, 256), F32),
-            shape((16, 256), F32),
-            shape((256, 256), BF),
-            shape((256, 256), BF),
-            shape((16, width), F32),
-        ),
-        compiler_params=params(16),
-        cost_estimate=cost(2e8, 2e6),
-        name="weights",
-    )(packed, packed_other)
-
     def by_rows(columns):
         return pl.BlockSpec((ROWS, columns), lambda g: (g, 0))
 
     by_plane = pl.BlockSpec((members, ROWS, 128), lambda g: (0, g, 0))
-    *given, features, value, gate, standard_two, scale, keep = pl.pallas_call(
+    *given, features, value, gate, standard_two, scale, keep, rows = pl.pallas_call(
         forward_kernel,
         grid=(blocks,),
         in_specs=[
-            whole(incoming.shape), whole(band.shape), whole(taps_a.shape), whole(taps_b.shape), whole(point_one.shape),
-            whole(point_two.shape), whole(rows.shape), anywhere, anywhere, anywhere, anywhere,
+            *[anywhere] * 7,
         ],
         out_specs=[
-            by_plane, by_plane, by_plane, by_plane, by_rows(width),
-            by_rows(width), by_rows(width), by_rows(width), by_rows(128), by_rows(128),
+            *[by_plane] * 4, *[anywhere] * 7,
         ],
         out_shape=(
             *[shape((members, rows_here, 128), BF)] * 4,
@@ -504,8 +530,23 @@
             shape((rows_here, width), F32),
             shape((rows_here, 128), F32),
             shape((rows_here, 128), F32),
+            shape((16, width), F32),
         ),
         scratch_shapes=[
+            pltpu.VMEM(incoming.shape, BF),
+            pltpu.VMEM((ROWS, width), BF),
+            pltpu.VMEM((ROWS, width), F32),
+            pltpu.VMEM((ROWS, width), F32),
+            pltpu.VMEM((ROWS, width), F32),
+            pltpu.VMEM((ROWS, 128), F32),
+            pltpu.VMEM((ROWS, 128), F32),
+            pltpu.VMEM((16, width), F32),
+            pltpu.VMEM((2,) + packed.shape, BF),
+            pltpu.VMEM((256, GROUP * 256), BF),
+            pltpu.VMEM((16, 256), F32),
+            pltpu.VMEM((16, 256), F32),
+            pltpu.VMEM((256, 256), BF),
+            pltpu.VMEM((256, 256), BF),
             pltpu.VMEM((2,) + linear_weight.shape, BF),
             pltpu.VMEM((2,) + up_weight.shape, BF),
             pltpu.VMEM((ROWS * width_in // SPAN // 128, groups * width_in // 128), F32),
@@ -518,41 +559,17 @@
             pltpu.VMEM((ROWS, BINS // 4 * 256), BF),
             pltpu.VMEM((ROWS + 8 * BLOCK, width), F32),
             pltpu.VMEM((width // 128, ROWS, 128), BF),
-            pltpu.SemaphoreType.DMA((4,)),
+            pltpu.SemaphoreType.DMA((7,)),
+            pltpu.SemaphoreType.DMA((7,)),
         ],
-        compiler_params=params(FRONT + groups // 2),
+        compiler_params=params(FRONT),
         cost_estimate=cost(2e10 * blocks, 1e7),
         name="forward",
-    )(incoming, band, taps_a, taps_b, point_one, point_two, rows, linear_weight, linear_other, up_weight, up_other)
-    near = [swap_rank(block, offset, groups) for offset, block in enumerate(given) if offset]
-    beside = pl.pallas_call(
-        backward_kernel,
-        grid=(blocks,),
-        in_specs=[
-            by_rows(width), by_rows(width), by_rows(width), by_rows(width), by_rows(128), by_rows(128),
-            whole(rows.shape), by_rows(width), *[anywhere] * 7,
-        ],
-        out_specs=[by_rows(width), by_rows(width), anywhere],
-        out_shape=(
-            shape((rows_here, width), BF), shape((rows_here, width), BF), shape((3, rows_here, width), BF),
-        ),
-        scratch_shapes=[
-            pltpu.VMEM((2,) + down_weight.shape, BF),
-            pltpu.VMEM((2,) + up_weight.shape, BF),
-            pltpu.VMEM((ROWS + 8 * BLOCK, width), F32),
-            pltpu.SemaphoreType.DMA((7,)),
-        ],
-        compiler_params=params(BACK),
-        cost_estimate=cost(1e6, 1e5),
-        name="backward",
-    )(
-        features, value, gate, standard_two, scale, keep, rows, cotangent,
-        down_weight, down_other, up_weight, up_other, *cotangents[1:],
-    )
-    *near, layer_out, grad_input, planes = lax.optimization_barrier((*near, *beside))
-    near = [given[0], *near]
-    far = [swap_cores(block) for block in near]
-    planes_other = swap_cores(planes)
+    )(incoming, packed, packed_other, linear_weight, linear_other, up_weight, up_other)
+    near = [given[0]] + [swap_rank(given[offset], offset, groups) for offset in range(1, 4)]
+    far = swap_cores(held_call(pack_kernel, shape((4, rows_here, 128), BF), [], "pack", *near))
+    given[0], *cotangents[1:] = lax.optimization_barrier((given[0], *cotangents[1:]))
+    cotangents_other = [cotangent_other] + [swap_cores(block) for block in cotangents[1:]]
     layers = groups // 4
     block = width // members // 4
     size = block // layers
@@ -562,12 +579,42 @@
         [shape((size, width), F32)] + [shape((size, width), BF)] * (layers - 1),
         [pltpu.VMEM((block, width), F32)],
         "far",
-        half_sum, *far, cotangent_other, planes_other,
-    )
-    for offset, other in enumerate(others):
-        own = own + swap_rank(other, 4 * (offset + 1), groups).astype(F32)
+        half_sum, far, *cotangents_other,
+    )
+    moved = [swap_rank(other, 4 * (offset + 1), groups) for offset, other in enumerate(others)]
+    full, thin = by_rows(width), by_rows(128)
+    layer_out, depth = pl.pallas_call(
+        down_kernel,
+        grid=(blocks,),
+        in_specs=[full, full, thin, thin, whole(rows.shape), full, anywhere, anywhere],
+        out_specs=[full, full],
+        out_shape=(shape((rows_here, width), BF), shape((rows_here, width), F32)),
+        scratch_shapes=[pltpu.VMEM((2,) + down_weight.shape, BF), pltpu.SemaphoreType.DMA((2,))],
+        compiler_params=params(BACK),
+        cost_estimate=cost(1e6, 1e5),
+        name="down",
+    )(features, standard_two, scale, keep, rows, cotangent, down_weight, down_other)
+    *moved, layer_out, depth = lax.optimization_barrier((*moved, layer_out, depth))
+    for part in moved:
+        own = own + part.astype(F32)
     own = (own * (1.0 / math.sqrt(rows_here * groups * members))).astype(BF)
     pieces = [own] + [swap_rank(own, 4 * offset, groups) for offset in range(1, layers)]
+    grad_input = pl.pallas_call(
+        up_kernel,
+        grid=(blocks,),
+        in_specs=[full, full, full, full, thin, whole(rows.shape), full, anywhere, anywhere],
+        out_specs=full,
+        out_shape=shape((rows_here, width), BF),
+        scratch_shapes=[
+            pltpu.VMEM((2,) + up_weight.shape, BF),
+            pltpu.VMEM((ROWS + 8 * BLOCK, width), F32),
+            pltpu.SemaphoreType.DMA((2,)),
+        ],
+        compiler_params=params(BACK),
+        cost_estimate=cost(1e6, 1e5),
+        name="up",
+    )(depth, features, value, gate, keep, rows, cotangent, up_weight, up_other)
+    *pieces, grad_input = lax.optimization_barrier((*pieces, grad_input))
     left, right = held_call(
         layers_kernel, [shape((block, width // 2), BF)] * 2, [pltpu.VMEM((block, width), F32)], "layers", *pieces
     )

time: 88.5 us -> 86.4 us (0.976)
  Pallas kernels: 25.2 us -> 31.3 us
  local copies, waits for them, and re-layouts: 8.15 us -> 2.56 us
  waiting for transfers between devices: 20.7 us -> 18.4 us
    pallas_call x3, Pallas kernels: 19.1 us -> 26.2 us  [the longest x1 15 us: local(): pl.pallas_call(forward_kernel, grid=(blocks,), in_specs=[*[anywhere] * 7]...]
    unnamed x22 -> x10, local copies, waits for them, and re-layouts: 8.15 us -> 2.56 us
    ppermute x18, waiting for transfers between devices: 15.1 us -> 10.5 us  [swap_rank(): return lax.ppermute(block, 'dp', [(i, i ^ offset) for i in range(groups)])]
    all_to_all x1, waiting for transfers between devices: 4.06 us -> 7.3 us  [local(): lax.all_to_all(outgoing, 'dp', split_axis=0, concat_axis=0, tiled=True)]
    pallas_call x4 -> x5, Pallas kernels: 3.26 us -> 2.24 us  [held_call(): pl.pallas_call(kernel, out_shape=outs, scratch_shapes=scratch, compiler_p...]
    ppermute x10 -> x9, waiting for transfers between devices: 1.58 us -> 0.68 us  [swap_cores(): return lax.ppermute(block, 'fsdp', [(0, 1), (1, 0)])]
    ppermute x10 -> x9, starting transfers between devices: 1.97 us -> 1.76 us  [swap_cores(): return lax.ppermute(block, 'fsdp', [(0, 1), (1, 0)])]
  transfers between devices with their start and end apart: 29 -> 28, of which waited for: 9 -> 10; matrix products, arithmetic and copies ran while one was open for 0% -> 0% of each run, Pallas kernels for 23% -> 31%
where the time goes in v5:
time: 86.4 us; the launch traced here: 86 us
  starting transfers between devices  32.8 us (38%)
  Pallas kernels  31.3 us (36%)
  waiting for transfers between devices  18.4 us (21%)
  local copies, waits for them, and re-layouts  2.56 us (3%)
    ppermute x18, starting transfers between devices, swap_rank(): return lax.ppermute(block, 'dp', [(i, i ^ offset) for i in range(groups)])  22.7 us
    pallas_call x1, Pallas kernels, local(): pl.pallas_call(forward_kernel, grid=(blocks,), in_specs=[*[anywhere] * 7]...  15 us
    ppermute x18, waiting for transfers between devices, swap_rank(): return lax.ppermute(block, 'dp', [(i, i ^ offset) for i in range(groups)])  10.5 us
    all_to_all x1, starting transfers between devices, local(): lax.all_to_all(outgoing, 'dp', split_axis=0, concat_axis=0, tiled=True)  8.3 us
    all_to_all x1, waiting for transfers between devices, local(): lax.all_to_all(outgoing, 'dp', split_axis=0, concat_axis=0, tiled=True)  7.3 us
    pallas_call x1, Pallas kernels, local(): pl.pallas_call(up_kernel, grid=(blocks,), in_specs=[full, full, full, ful...  6.34 us
    pallas_call x1, Pallas kernels, local(): pl.pallas_call(down_kernel, grid=(blocks,), in_specs=[full, full, thin, t...  4.88 us
    pallas_call x1, Pallas kernels, local(): pl.pallas_call(send_kernel, in_specs=[anywhere, held, held] + [anywhere]...  2.85 us
  transfers between devices with their start and end apart: 28, of which 10 were waited for; matrix products, arithmetic and copies ran while one was open for 0% of the time, Pallas kernels for 31%

profile of v5, /device:TPU:0, one launch (start us, length us, event | category | flops | bytes accessed | tf_op | source)
XLA Modules:
  0.0 86.0 jit_solution(1324903049717714012)
XLA Ops:
  1.2 2.8 %send.1 = (bf16[16,88,128]{2,1,0:T(8,128)(2,1)}, bf16[160,512]{1,0:T(8,128)(2,1)}) custom-call(bf16[16,10240]{1,0:T(8,128)(2,1)} %mel.1, s32[1,16]{1,0:T(1,128)} %bitcast.2, s32[1,16]{1,0:T(1,128)} %bitcast.3, bf16[9,128]{1,0:T(8,128)(2,1)} %first.1, bf16[9,128]{1,0:T(8,128)(2,1)} %depth_a.1, bf16[256,128]{1,0:T(8,128)(2,1)} %point_a.1, ...), custom_call_target="tpu_custom_call" | custom-call | flops 200000000 | bytes 1000000 | tf_op jit(solution)/shard_map/send/pallas_call | solution.py:491
  4.1 8.3 %all-to-all-start = ((bf16[16,88,128]{2,1,0:T(8,128)(2,1)}), bf16[16,88,128]{2,1,0:T(8,128)(2,1)S(1)}, u32[]{:S(2)}, u32[]{:S(2)}) async-start(bf16[16,88,128]{2,1,0:T(8,128)(2,1)} %get-tuple-element.37), calls=%async_computation | async-start | bytes 720896 | tf_op jit(solution)/shard_map/all_to_all | solution.py:505
  12.5 2.0 %collective-permute-start.6 = (bf16[128,1024]{1,0:T(8,128)(2,1)}, bf16[128,1024]{1,0:T(8,128)(2,1)S(1)}, u32[]{:S(2)}, u32[]{:S(2)}) collective-permute-start(bf16[128,1024]{1,0:T(8,128)(2,1)} %cotangent.3), channel_id=1, source_target_pairs={{0,2},{2,0},{4,6},{6,4},{8,10},{10,8},{12,14},{14,12},{16,18},{18,... | collective-permute-start | bytes 786440 | tf_op jit(solution)/shard_map/ppermute | solution.py:449
  14.5 1.5 %collective-permute-start.7 = (bf16[128,1024]{1,0:T(8,128)(2,1)}, bf16[128,1024]{1,0:T(8,128)(2,1)S(1)}, u32[]{:S(2)}, u32[]{:S(2)}) collective-permute-start(bf16[128,1024]{1,0:T(8,128)(2,1)} %cotangent.3), channel_id=1, source_target_pairs={{0,4},{2,6},{4,0},{6,2},{8,12},{10,14},{12,8},{14,10},{16,20},{18,... | collective-permute-start | bytes 786440 | tf_op jit(solution)/shard_map/ppermute | solution.py:449
  17.4 7.3 %all-to-all-done.incoming_in = bf16[16,88,128]{2,1,0:T(8,128)(2,1)S(1)} async-done(((bf16[16,88,128]{2,1,0:T(8,128)(2,1)}), bf16[16,88,128]{2,1,0:T(8,128)(2,1)S(1)}, u32[]{:S(2)}, u32[]{:S(2)}) %all-to-all-start) | async-done | bytes 360480 | tf_op jit(solution)/shard_map/all_to_all | solution.py:505
  25.5 15.0 %forward.1 = (bf16[2,128,128]{2,1,0:T(8,128)(2,1)}, bf16[2,128,128]{2,1,0:T(8,128)(2,1)}, bf16[2,128,128]{2,1,0:T(8,128)(2,1)}, bf16[2,128,128]{2,1,0:T(8,128)(2...) custom-call(bf16[16,88,128]{2,1,0:T(8,128)(2,1)} %copy-done.3, ...), custom_call_target="tpu_custom_call" | custom-call | flops 20000000000 | bytes 10000000 | tf_op jit(solution)/shard_map/forward/pallas_call | solution.py:516
  42.0 2.0 %collective-permute-start.5 = (bf16[2,128,128]{2,1,0:T(8,128)(2,1)}, bf16[2,128,128]{2,1,0:T(8,128)(2,1)S(1)}, u32[]{:S(2)}, u32[]{:S(2)}) collective-permute-start(bf16[2,128,128]{2,1,0:T(8,128)(2,1)} %get-tuple-element.42), channel_id=1, source_target_pairs={{0,6},{2,4},{4,2},{6,0},{8,14},{10,12},{12,10},{14,8},{16,22},{18,... | collective-permute-start | bytes 196616 | tf_op jit(solution)/shard_map/ppermute | solution.py:449
  44.1 1.0 %collective-permute-done.3.refs_1_ = bf16[2,128,128]{2,1,0:T(8,128)(2,1)S(1)} collective-permute-done((bf16[2,128,128]{2,1,0:T(8,128)(2,1)}, bf16[2,128,128]{2,1,0:T(8,128)(2,1)S(1)}, u32[]{:S(2)}, u32[]{:S(2)}) %collective-permute-start.3) | collective-permute-done | bytes 65568 | tf_op jit(solution)/shard_map/ppermute | solution.py:449
  45.6 1.8 %collective-permute-done.5.refs_3_ = bf16[2,128,128]{2,1,0:T(8,128)(2,1)S(1)} collective-permute-done((bf16[2,128,128]{2,1,0:T(8,128)(2,1)}, bf16[2,128,128]{2,1,0:T(8,128)(2,1)S(1)}, u32[]{:S(2)}, u32[]{:S(2)}) %collective-permute-start.5) | collective-permute-done | bytes 65568 | tf_op jit(solution)/shard_map/ppermute | solution.py:449
  50.2 1.1 %collective-permute-start.14 = (bf16[32,1024]{1,0:T(8,128)(2,1)S(1)}, bf16[32,1024]{1,0:T(8,128)(2,1)S(1)}, u32[]{:S(2)}, u32[]{:S(2)}) collective-permute-start(bf16[32,1024]{1,0:T(8,128)(2,1)S(1)} %get-tuple-element.46), channel_id=1, source_target_pairs={{0,8},{2,10},{4,12},{6,14},{8,0},{10,2},{12,4},{14,6},{16,24},{18,... | collective-permute-start | bytes 196616 | tf_op jit(solution)/shard_map/ppermute | solution.py:449
  51.3 1.4 %collective-permute-start.15 = (bf16[32,1024]{1,0:T(8,128)(2,1)S(1)}, bf16[32,1024]{1,0:T(8,128)(2,1)S(1)}, u32[]{:S(2)}, u32[]{:S(2)}) collective-permute-start(bf16[32,1024]{1,0:T(8,128)(2,1)S(1)} %get-tuple-element.47), channel_id=1, source_target_pairs={{0,16},{2,18},{4,20},{6,22},{8,24},{10,26},{12,28},{14,30},{16,0},... | collective-permute-start | bytes 196616 | tf_op jit(solution)/shard_map/ppermute | solution.py:449
  52.7 2.0 %collective-permute-start.16 = (bf16[32,1024]{1,0:T(8,128)(2,1)S(1)}, bf16[32,1024]{1,0:T(8,128)(2,1)S(1)}, u32[]{:S(2)}, u32[]{:S(2)}) collective-permute-start(bf16[32,1024]{1,0:T(8,128)(2,1)S(1)} %get-tuple-element.48), channel_id=1, source_target_pairs={{0,24},{2,26},{4,28},{6,30},{8,16},{10,18},{12,20},{14,22},{16,8},... | collective-permute-start | bytes 196616 | tf_op jit(solution)/shard_map/ppermute | solution.py:449
  55.7 4.9 %down.1 = (bf16[128,1024]{1,0:T(8,128)(2,1)}, f32[128,1024]{1,0:T(8,128)}) custom-call(bf16[128,1024]{1,0:T(8,128)(2,1)} %get-tuple-element.49.features_in, f32[128,1024]{1,0:T(8,128)} %get-tuple-element.50.standard_two_in, f32[128,128]{1,0:T(8,128)} %get-tuple-element.51.scale_in, f32[128,128]{1,0:T(8,128)} %get-tuple-element.52.keep_in, ...), custom_call_target="tpu_custom_call" | custom-call | flops 1000000 | bytes 100000 | tf_op jit(solution)/shard_map/down/pallas_call | solution.py:586
  61.2 1.9 %collective-permute-start.19 = (bf16[32,1024]{1,0:T(8,128)(2,1)S(1)}, bf16[32,1024]{1,0:T(8,128)(2,1)S(1)}, u32[]{:S(2)}, u32[]{:S(2)}) collective-permute-start(bf16[32,1024]{1,0:T(8,128)(2,1)S(1)} %multiply_convert_fusion.refs_0_), channel_id=1, source_target_pairs={{0,16},{2,18},{4,20},{6,22},{8,24},{10,26},{12,28},{14,30},{16,0},... | collective-permute-start | bytes 196616 | tf_op jit(solution)/shard_map/ppermute | solution.py:449
  63.1 2.0 %collective-permute-start.20 = (bf16[32,1024]{1,0:T(8,128)(2,1)S(1)}, bf16[32,1024]{1,0:T(8,128)(2,1)S(1)}, u32[]{:S(2)}, u32[]{:S(2)}) collective-permute-start(bf16[32,1024]{1,0:T(8,128)(2,1)S(1)} %multiply_convert_fusion.refs_0_), channel_id=1, source_target_pairs={{0,24},{2,26},{4,28},{6,30},{8,16},{10,18},{12,20},{14,22},{16,8},... | collective-permute-start | bytes 196616 | tf_op jit(solution)/shard_map/ppermute | solution.py:449
  65.1 6.3 %up.1 = bf16[128,1024]{1,0:T(8,128)(2,1)} custom-call(f32[128,1024]{1,0:T(8,128)} %get-tuple-element.61.depth_in, bf16[128,1024]{1,0:T(8,128)(2,1)} %get-tuple-element.49.features_in, f32[128,1024]{1,0:T(8,128)} %get-tuple-element.62.value_in, f32[128,1024]{1,0:T(8,128)} %get-tuple-element.63.gate_in, f32[128,128]{1,0:T(8,128)} %get-tuple-element.52.keep_in, ...), custom_call_target="tpu_custom_call" | custom-call | flops 1000000 | bytes 100000 | tf_op jit(solution)/shard_map/up/pallas_call | solution.py:602
  71.6 1.5 %collective-permute-start.21 = (bf16[128,512]{1,0:T(8,128)(2,1)S(1)}, bf16[128,512]{1,0:T(8,128)(2,1)S(1)}, u32[]{:S(2)}, u32[]{:S(2)}) collective-permute-start(bf16[128,512]{1,0:T(8,128)(2,1)S(1)} %get-tuple-element.69.refs_0_), channel_id=1, source_target_pairs={{0,2},{2,0},{4,6},{6,4},{8,10},{10,8},{12,14},{14,12},{16,18},{18,... | collective-permute-start | bytes 393224 | tf_op jit(solution)/shard_map/ppermute | solution.py:449
  73.1 1.1 %collective-permute-start.25 = (bf16[128,512]{1,0:T(8,128)(2,1)S(1)}, bf16[128,512]{1,0:T(8,128)(2,1)S(1)}, u32[]{:S(2)}, u32[]{:S(2)}) collective-permute-start(bf16[128,512]{1,0:T(8,128)(2,1)S(1)} %get-tuple-element.70.refs_4_), channel_id=1, source_target_pairs={{0,4},{2,6},{4,0},{6,2},{8,12},{10,14},{12,8},{14,10},{16,20},{18,... | collective-permute-start | bytes 393224 | tf_op jit(solution)/shard_map/ppermute | solution.py:449
  75.7 2.0 %collective-permute-done.21.refs_1_ = bf16[128,512]{1,0:T(8,128)(2,1)S(1)} collective-permute-done((bf16[128,512]{1,0:T(8,128)(2,1)S(1)}, bf16[128,512]{1,0:T(8,128)(2,1)S(1)}, u32[]{:S(2)}, u32[]{:S(2)}) %collective-permute-start.21) | collective-permute-done | bytes 131104 | tf_op jit(solution)/shard_map/ppermute | solution.py:449
  77.7 1.1 %collective-permute-start.23 = (bf16[128,512]{1,0:T(8,128)(2,1)S(1)}, bf16[128,512]{1,0:T(8,128)(2,1)S(1)}, u32[]{:S(2)}, u32[]{:S(2)}) collective-permute-start(bf16[128,512]{1,0:T(8,128)(2,1)S(1)} %collective-permute-done.21.refs_1_), channel_id=1, source_target_pairs={{0,4},{2,6},{4,0},{6,2},{8,12},{10,14},{12,8},{14,10},{16,20},{18,... | collective-permute-start | bytes 393224 | tf_op jit(solution)/shard_map/ppermute | solution.py:449
  80.1 1.0 %collective-permute-done.22.refs_2_ = bf16[128,512]{1,0:T(8,128)(2,1)S(1)} collective-permute-done((bf16[128,512]{1,0:T(8,128)(2,1)S(1)}, bf16[128,512]{1,0:T(8,128)(2,1)S(1)}, u32[]{:S(2)}, u32[]{:S(2)}) %collective-permute-start.22) | collective-permute-done | bytes 131104 | tf_op jit(solution)/shard_map/ppermute | solution.py:449
  81.1 1.5 %collective-permute-done.23.refs_3_ = bf16[128,512]{1,0:T(8,128)(2,1)S(1)} collective-permute-done((bf16[128,512]{1,0:T(8,128)(2,1)S(1)}, bf16[128,512]{1,0:T(8,128)(2,1)S(1)}, u32[]{:S(2)}, u32[]{:S(2)}) %collective-permute-start.23) | collective-permute-done | bytes 131104 | tf_op jit(solution)/shard_map/ppermute | solution.py:449
  82.6 1.9 %collective-permute-done.26.refs_7_ = bf16[128,512]{1,0:T(8,128)(2,1)S(1)} collective-permute-done((bf16[128,512]{1,0:T(8,128)(2,1)S(1)}, bf16[128,512]{1,0:T(8,128)(2,1)S(1)}, u32[]{:S(2)}, u32[]{:S(2)}) %collective-permute-start.26) | collective-permute-done | bytes 131104 | tf_op jit(solution)/shard_map/ppermute | solution.py:449
  84.5 1.5 %finish.1 = f32[512,1024]{1,0:T(8,128)} custom-call(bf16[128,512]{1,0:T(8,128)(2,1)S(1)} %get-tuple-element.69.refs_0_, bf16[128,512]{1,0:T(8,128)(2,1)S(1)} %collective-permute-done.21.refs_1_, bf16[128,512]{1,0:T(8,128)(2,1)S(1)} %collective-permute-done.22.refs_2_, bf16[128,512]{1,0:T(8,128)(2,1)S(1)} %collective-permute-done.23.refs_3_, ...), custom_call_target="tpu_custom_call" | custom-call | flops 1000000 | bytes 100000 | tf_op jit(solution)/shard_map/finish/pallas_call | solution.py:453
  (52 shorter events, 12.2 us)
Async XLA Ops:
  0.6 16.3 %collective-permute-start.1 = (bf16[2560,512]{1,0:T(8,128)(2,1)}, bf16[2560,512]{1,0:T(8,128)(2,1)}, u32[]{:S(2)}, u32[]{:S(2)}) collective-permute-start(bf16[2560,512]{1,0:T(8,128)(2,1)} %linear_mine.1), channel_id=1, source_target_pairs={{0,1},{1,0},{2,3},{3,2},{4,5},{5,4},{6,7},{7,6},{8,9},{9,8},{10,11... | collective-permute-start | bytes 7864328 | tf_op jit(solution)/shard_map/ppermute | solution.py:445
  1.2 15.8 %collective-permute-start.2 = (bf16[1024,1024]{1,0:T(8,128)(2,1)}, bf16[1024,1024]{1,0:T(8,128)(2,1)}, u32[]{:S(2)}, u32[]{:S(2)}) collective-permute-start(bf16[1024,1024]{1,0:T(8,128)(2,1)} %up_mine.3), channel_id=1, source_target_pairs={{0,1},{1,0},{2,3},{3,2},{4,5},{5,4},{6,7},{7,6},{8,9},{9,8},{10,11... | collective-permute-start | bytes 6291464 | tf_op jit(solution)/shard_map/ppermute | solution.py:445
  4.1 20.6 %all-to-all-start = ((bf16[16,88,128]{2,1,0:T(8,128)(2,1)}), bf16[16,88,128]{2,1,0:T(8,128)(2,1)S(1)}, u32[]{:S(2)}, u32[]{:S(2)}) async-start(bf16[16,88,128]{2,1,0:T(8,128)(2,1)} %get-tuple-element.37), calls=%async_computation | async-start | bytes 720896 | tf_op jit(solution)/shard_map/all_to_all | solution.py:505
  12.5 28.0 %collective-permute-start.6 = (bf16[128,1024]{1,0:T(8,128)(2,1)}, bf16[128,1024]{1,0:T(8,128)(2,1)S(1)}, u32[]{:S(2)}, u32[]{:S(2)}) collective-permute-start(bf16[128,1024]{1,0:T(8,128)(2,1)} %cotangent.3), channel_id=1, source_target_pairs={{0,2},{2,0},{4,6},{6,4},{8,10},{10,8},{12,14},{14,12},{16,18},{18,... | collective-permute-start | bytes 786440 | tf_op jit(solution)/shard_map/ppermute | solution.py:449
  14.5 26.7 %collective-permute-start.7 = (bf16[128,1024]{1,0:T(8,128)(2,1)}, bf16[128,1024]{1,0:T(8,128)(2,1)S(1)}, u32[]{:S(2)}, u32[]{:S(2)}) collective-permute-start(bf16[128,1024]{1,0:T(8,128)(2,1)} %cotangent.3), channel_id=1, source_target_pairs={{0,4},{2,6},{4,0},{6,2},{8,12},{10,14},{12,8},{14,10},{16,20},{18,... | collective-permute-start | bytes 786440 | tf_op jit(solution)/shard_map/ppermute | solution.py:449
  15.9 26.1 %collective-permute-start.8 = (bf16[128,1024]{1,0:T(8,128)(2,1)}, bf16[128,1024]{1,0:T(8,128)(2,1)S(1)}, u32[]{:S(2)}, u32[]{:S(2)}) collective-permute-start(bf16[128,1024]{1,0:T(8,128)(2,1)} %cotangent.3), channel_id=1, source_target_pairs={{0,6},{2,4},{4,2},{6,0},{8,14},{10,12},{12,10},{14,8},{16,22},{18,... | collective-permute-start | bytes 786440 | tf_op jit(solution)/shard_map/ppermute | solution.py:449
  16.9 31.4 %collective-permute-start.10 = (bf16[128,1024]{1,0:T(8,128)(2,1)}, bf16[128,1024]{1,0:T(8,128)(2,1)S(1)}, u32[]{:S(2)}, u32[]{:S(2)}) collective-permute-start(bf16[128,1024]{1,0:T(8,128)(2,1)} %cotangent.3), channel_id=1, source_target_pairs={{0,1},{1,0},{2,3},{3,2},{4,5},{5,4},{6,7},{7,6},{8,9},{9,8},{10,11... | collective-permute-start | bytes 786440 | tf_op jit(solution)/shard_map/ppermute | solution.py:445
  16.9 37.8 %collective-permute-start.17 = (bf16[512,1024]{1,0:T(8,128)(2,1)}, bf16[512,1024]{1,0:T(8,128)(2,1)S(1)}, u32[]{:S(2)}, u32[]{:S(2)}) collective-permute-start(bf16[512,1024]{1,0:T(8,128)(2,1)} %down_mine.1), channel_id=1, source_target_pairs={{0,1},{1,0},{2,3},{3,2},{4,5},{5,4},{6,7},{7,6},{8,9},{9,8},{10,11... | collective-permute-start | bytes 3145736 | tf_op jit(solution)/shard_map/ppermute | solution.py:445
  40.5 4.5 %collective-permute-start.3 = (bf16[2,128,128]{2,1,0:T(8,128)(2,1)}, bf16[2,128,128]{2,1,0:T(8,128)(2,1)S(1)}, u32[]{:S(2)}, u32[]{:S(2)}) collective-permute-start(bf16[2,128,128]{2,1,0:T(8,128)(2,1)} %get-tuple-element.40), channel_id=1, source_target_pairs={{0,2},{2,0},{4,6},{6,4},{8,10},{10,8},{12,14},{14,12},{16,18},{18,... | collective-permute-start | bytes 196616 | tf_op jit(solution)/shard_map/ppermute | solution.py:449
  41.1 4.5 %collective-permute-start.4 = (bf16[2,128,128]{2,1,0:T(8,128)(2,1)}, bf16[2,128,128]{2,1,0:T(8,128)(2,1)S(1)}, u32[]{:S(2)}, u32[]{:S(2)}) collective-permute-start(bf16[2,128,128]{2,1,0:T(8,128)(2,1)} %get-tuple-element.41), channel_id=1, source_target_pairs={{0,4},{2,6},{4,0},{6,2},{8,12},{10,14},{12,8},{14,10},{16,20},{18,... | collective-permute-start | bytes 196616 | tf_op jit(solution)/shard_map/ppermute | solution.py:449
  42.0 5.4 %collective-permute-start.5 = (bf16[2,128,128]{2,1,0:T(8,128)(2,1)}, bf16[2,128,128]{2,1,0:T(8,128)(2,1)S(1)}, u32[]{:S(2)}, u32[]{:S(2)}) collective-permute-start(bf16[2,128,128]{2,1,0:T(8,128)(2,1)} %get-tuple-element.42), channel_id=1, source_target_pairs={{0,6},{2,4},{4,2},{6,0},{8,14},{10,12},{12,10},{14,8},{16,22},{18,... | collective-permute-start | bytes 196616 | tf_op jit(solution)/shard_map/ppermute | solution.py:449
  45.0 4.8 %collective-permute-start.11 = (bf16[128,1024]{1,0:T(8,128)(2,1)S(1)}, bf16[128,1024]{1,0:T(8,128)(2,1)S(1)}, u32[]{:S(2)}, u32[]{:S(2)}) collective-permute-start(bf16[128,1024]{1,0:T(8,128)(2,1)S(1)} %collective-permute-done.6.refs_5_), channel_id=1, source_target_pairs={{0,1},{1,0},{2,3},{3,2},{4,5},{5,4},{6,7},{7,6},{8,9},{9,8},{10,11... | collective-permute-start | bytes 786440 | tf_op jit(solution)/shard_map/ppermute | solution.py:445
  50.2 10.3 %collective-permute-start.14 = (bf16[32,1024]{1,0:T(8,128)(2,1)S(1)}, bf16[32,1024]{1,0:T(8,128)(2,1)S(1)}, u32[]{:S(2)}, u32[]{:S(2)}) collective-permute-start(bf16[32,1024]{1,0:T(8,128)(2,1)S(1)} %get-tuple-element.46), channel_id=1, source_target_pairs={{0,8},{2,10},{4,12},{6,14},{8,0},{10,2},{12,4},{14,6},{16,24},{18,... | collective-permute-start | bytes 196616 | tf_op jit(solution)/shard_map/ppermute | solution.py:449
  51.3 9.2 %collective-permute-start.15 = (bf16[32,1024]{1,0:T(8,128)(2,1)S(1)}, bf16[32,1024]{1,0:T(8,128)(2,1)S(1)}, u32[]{:S(2)}, u32[]{:S(2)}) collective-permute-start(bf16[32,1024]{1,0:T(8,128)(2,1)S(1)} %get-tuple-element.47), channel_id=1, source_target_pairs={{0,16},{2,18},{4,20},{6,22},{8,24},{10,26},{12,28},{14,30},{16,0},... | collective-permute-start | bytes 196616 | tf_op jit(solution)/shard_map/ppermute | solution.py:449
  52.7 7.9 %collective-permute-start.16 = (bf16[32,1024]{1,0:T(8,128)(2,1)S(1)}, bf16[32,1024]{1,0:T(8,128)(2,1)S(1)}, u32[]{:S(2)}, u32[]{:S(2)}) collective-permute-start(bf16[32,1024]{1,0:T(8,128)(2,1)S(1)} %get-tuple-element.48), channel_id=1, source_target_pairs={{0,24},{2,26},{4,28},{6,30},{8,16},{10,18},{12,20},{14,22},{16,8},... | collective-permute-start | bytes 196616 | tf_op jit(solution)/shard_map/ppermute | solution.py:449
  60.6 10.8 %collective-permute-start.18 = (bf16[32,1024]{1,0:T(8,128)(2,1)S(1)}, bf16[32,1024]{1,0:T(8,128)(2,1)S(1)}, u32[]{:S(2)}, u32[]{:S(2)}) collective-permute-start(bf16[32,1024]{1,0:T(8,128)(2,1)S(1)} %multiply_convert_fusion.refs_0_), channel_id=1, source_target_pairs={{0,8},{2,10},{4,12},{6,14},{8,0},{10,2},{12,4},{14,6},{16,24},{18,... | collective-permute-start | bytes 196616 | tf_op jit(solution)/shard_map/ppermute | solution.py:449
  61.2 10.3 %collective-permute-start.19 = (bf16[32,1024]{1,0:T(8,128)(2,1)S(1)}, bf16[32,1024]{1,0:T(8,128)(2,1)S(1)}, u32[]{:S(2)}, u32[]{:S(2)}) collective-permute-start(bf16[32,1024]{1,0:T(8,128)(2,1)S(1)} %multiply_convert_fusion.refs_0_), channel_id=1, source_target_pairs={{0,16},{2,18},{4,20},{6,22},{8,24},{10,26},{12,28},{14,30},{16,0},... | collective-permute-start | bytes 196616 | tf_op jit(solution)/shard_map/ppermute | solution.py:449
  63.1 8.4 %collective-permute-start.20 = (bf16[32,1024]{1,0:T(8,128)(2,1)S(1)}, bf16[32,1024]{1,0:T(8,128)(2,1)S(1)}, u32[]{:S(2)}, u32[]{:S(2)}) collective-permute-start(bf16[32,1024]{1,0:T(8,128)(2,1)S(1)} %multiply_convert_fusion.refs_0_), channel_id=1, source_target_pairs={{0,24},{2,26},{4,28},{6,30},{8,16},{10,18},{12,20},{14,22},{16,8},... | collective-permute-start | bytes 196616 | tf_op jit(solution)/shard_map/ppermute | solution.py:449
  71.6 6.1 %collective-permute-start.21 = (bf16[128,512]{1,0:T(8,128)(2,1)S(1)}, bf16[128,512]{1,0:T(8,128)(2,1)S(1)}, u32[]{:S(2)}, u32[]{:S(2)}) collective-permute-start(bf16[128,512]{1,0:T(8,128)(2,1)S(1)} %get-tuple-element.69.refs_0_), channel_id=1, source_target_pairs={{0,2},{2,0},{4,6},{6,4},{8,10},{10,8},{12,14},{14,12},{16,18},{18,... | collective-permute-start | bytes 393224 | tf_op jit(solution)/shard_map/ppermute | solution.py:449
  73.1 6.4 %collective-permute-start.25 = (bf16[128,512]{1,0:T(8,128)(2,1)S(1)}, bf16[128,512]{1,0:T(8,128)(2,1)S(1)}, u32[]{:S(2)}, u32[]{:S(2)}) collective-permute-start(bf16[128,512]{1,0:T(8,128)(2,1)S(1)} %get-tuple-element.70.refs_4_), channel_id=1, source_target_pairs={{0,4},{2,6},{4,0},{6,2},{8,12},{10,14},{12,8},{14,10},{16,20},{18,... | collective-permute-start | bytes 393224 | tf_op jit(solution)/shard_map/ppermute | solution.py:449
  74.2 6.9 %collective-permute-start.22 = (bf16[128,512]{1,0:T(8,128)(2,1)S(1)}, bf16[128,512]{1,0:T(8,128)(2,1)S(1)}, u32[]{:S(2)}, u32[]{:S(2)}) collective-permute-start(bf16[128,512]{1,0:T(8,128)(2,1)S(1)} %get-tuple-element.69.refs_0_), channel_id=1, source_target_pairs={{0,4},{2,6},{4,0},{6,2},{8,12},{10,14},{12,8},{14,10},{16,20},{18,... | collective-permute-start | bytes 393224 | tf_op jit(solution)/shard_map/ppermute | solution.py:449
  75.1 6.0 %collective-permute-start.24 = (bf16[128,512]{1,0:T(8,128)(2,1)S(1)}, bf16[128,512]{1,0:T(8,128)(2,1)S(1)}, u32[]{:S(2)}, u32[]{:S(2)}) collective-permute-start(bf16[128,512]{1,0:T(8,128)(2,1)S(1)} %get-tuple-element.70.refs_4_), channel_id=1, source_target_pairs={{0,2},{2,0},{4,6},{6,4},{8,10},{10,8},{12,14},{14,12},{16,18},{18,... | collective-permute-start | bytes 393224 | tf_op jit(solution)/shard_map/ppermute | solution.py:449
  77.7 5.0 %collective-permute-start.23 = (bf16[128,512]{1,0:T(8,128)(2,1)S(1)}, bf16[128,512]{1,0:T(8,128)(2,1)S(1)}, u32[]{:S(2)}, u32[]{:S(2)}) collective-permute-start(bf16[128,512]{1,0:T(8,128)(2,1)S(1)} %collective-permute-done.21.refs_1_), channel_id=1, source_target_pairs={{0,4},{2,6},{4,0},{6,2},{8,12},{10,14},{12,8},{14,10},{16,20},{18,... | collective-permute-start | bytes 393224 | tf_op jit(solution)/shard_map/ppermute | solution.py:449
  79.5 5.0 %collective-permute-start.26 = (bf16[128,512]{1,0:T(8,128)(2,1)S(1)}, bf16[128,512]{1,0:T(8,128)(2,1)S(1)}, u32[]{:S(2)}, u32[]{:S(2)}) collective-permute-start(bf16[128,512]{1,0:T(8,128)(2,1)S(1)} %collective-permute-done.25.refs_6_), channel_id=1, source_target_pairs={{0,2},{2,0},{4,6},{6,4},{8,10},{10,8},{12,14},{14,12},{16,18},{18,... | collective-permute-start | bytes 393224 | tf_op jit(solution)/shard_map/ppermute | solution.py:449
  (9 other events, 59.6 us)

commit v6 on v5

--- a/solution.py
+++ b/solution.py
@@ -14,8 +14,8 @@
 SPAN = PANEL // 8
 BLOCK = 8
 ROWS = BLOCK * SPAN
-FRONT = 60
-BACK = 61
+FRONT = 62
+BACK = 62
 BINS = 40
 GROUP = 10
 WINDOW = 2 * GROUP + 1
@@ -183,9 +183,9 @@
             ext_s[BLOCK:, ahead * 128 : (ahead + 1) * 128] = part[: ROWS - BLOCK]
     lane = iota((ROWS, 256), 1)
     edge = (lane == 0) | (lane == MELS) | (lane == 2 * MELS)
-    for q in range(5):
+    for q in range(4):
         for b in range(4):
-            start = LEAD + (2 * q - 3) * MELS + 2 * GROUP * b - 1
+            start = LEAD + (2 * q - 1) * MELS + 2 * GROUP * b - 1
             tile = start // 128 * 128
             shift = start - tile
             span = 256 if shift + 2 * MELS + WINDOW <= 256 else 384
@@ -195,19 +195,24 @@
                 part = jnp.where(edge, 0.0, part)
             x_s[b, q * ROWS : (q + 1) * ROWS, :] = part.astype(BF)
 
+    views = (3 * ROWS, 0, ROWS, 2 * ROWS, 3 * ROWS + BLOCK)
     first_s[0] = jnp.zeros(first_s.shape[1:], F32)
+    for f in range(GROUP):
+        first_s[1 + f, 3 * ROWS : 3 * ROWS + BLOCK, :] = jnp.zeros((BLOCK, 256), F32)
     odd_s[:, 0:BLOCK, :] = jnp.zeros((odd_s.shape[0], BLOCK, 256), F32)
 
     def section(b, carry):
         source = x_s[b]
         for f in range(GROUP):
-            first_s[1 + f] = jnp.maximum(dot(source, band[:, f * 256 : (f + 1) * 256]), 0.0)
+            sums = jnp.maximum(dot(source, band[:, f * 256 : (f + 1) * 256]), 0.0)
+            first_s[1 + f, : 3 * ROWS, :] = sums[: 3 * ROWS]
+            first_s[1 + f, 3 * ROWS + BLOCK :, :] = sums[3 * ROWS :]
         for g in range(GROUP // 2):
             for s in range(2):
                 total = None
                 for j in range(3):
                     for i in range(3):
-                        at = (2 * s + i) * ROWS
+                        at = views[2 * s + i]
                         term = first_s[2 * g + j, at : at + ROWS, :] * taps_a[3 * i + j : 3 * i + j + 1, :]
                         total = term if total is None else total + term
                 spread_s[(2 * g + s) * ROWS : (2 * g + s + 1) * ROWS, :] = total.astype(BF)
@@ -330,96 +335,110 @@
 
 
 def finish_kernel(*refs):
-    lefts, rights, out = refs[0:4], refs[4:8], refs[8]
+    pieces, out, held, sems = refs[0:8], refs[8], refs[9], refs[10]
     plane = lax.axis_index("dp") % 4
-    size, half = lefts[0].shape
-    for offset in range(4):
-        at = pl.multiple_of((plane ^ offset) * size, size)
-        out[pl.ds(at, size), :half] = lefts[offset][...].astype(F32)
-        out[pl.ds(at, size), half:] = rights[offset][...].astype(F32)
+    size, half = pieces[0].shape
+    copies = []
+    for n, piece in enumerate(pieces):
+        side = slice(n // 4 * half, (n // 4 + 1) * half)
+        held[n] = piece[...].astype(F32)
+        at = pl.multiple_of((plane ^ (n % 4)) * size, size)
+        copies.append(pltpu.make_async_copy(held.at[n], out.at[pl.ds(at, size), side], sems.at[n]))
+        copies[-1].start()
+    for copy in copies:
+        copy.wait()
 
 
 def back_rows(order, cotangent, row_keep):
     return jnp.where(row_keep > 0, dot(order, cotangent[...], DOWN), 0.0)
 
 
-def down_kernel(
-    features_in, standard_two_in, scale_in, keep_in, rows, cotangent, down_mine, down_other,
-    layer_out, depth_out,
-    down_s, sems,
-):
+def bring(body, inputs, outputs, *refs):
+    sources, mine, other = refs[:inputs], refs[inputs], refs[inputs + 1]
+    outs = refs[inputs + 2 : inputs + 2 + outputs]
+    refs = refs[inputs + 2 + outputs :]
+    held, weight, sems, extra = refs[:inputs], refs[inputs], refs[inputs + 1], refs[inputs + 2 :]
     step = pl.program_id(0)
-    copies = fetch(((down_mine, down_other, down_s),), sems, lax.axis_index("fsdp"))
+    copies = []
+    for n, (source, buffer) in enumerate(zip(sources, held)):
+        if source.shape[0] != 16:
+            source = source.at[pl.ds(step * ROWS, ROWS)]
+        copies.append(pltpu.make_async_copy(source, buffer, sems.at[n]))
+    me = lax.axis_index("fsdp")
+    weights = [
+        pltpu.make_async_copy(mine, weight.at[me], sems.at[inputs]),
+        pltpu.make_async_copy(other, weight.at[1 - me], sems.at[inputs + 1]),
+    ]
+    for copy in copies:
+        copy.start()
 
     @pl.when(step == 0)
     def _():
-        for copy in copies:
+        for copy in weights:
             copy.start()
 
+    for copy in copies:
+        copy.wait()
+
+    def wait_weight():
+        @pl.when(step == 0)
+        def _():
+            for copy in weights:
+                copy.wait()
+
+    body(wait_weight, weight, *held, *outs, *extra)
+
+
+def layer_kernel(wait_weight, down_s, features_in, standard_two_in, keep_in, rows, layer_out):
+    active = standard_two_in[...] * rows[10:11, :]
+    hidden = (active * jax.nn.sigmoid(active)).astype(BF)
     order = row_order()
+    wait_weight()
+    half = down_s.shape[1]
+    mixed = dot(hidden[:, :half], down_s[0]) + dot(hidden[:, half:], down_s[1])
+    layer = jnp.where(keep_in[:, 0:1] > 0, features_in[...].astype(F32) + mixed, 0.0).astype(BF)
+    layer_out[...] = dot(order, layer).astype(BF)
+
+
+def depth_kernel_back(
+    wait_weight, down_s, standard_two_in, value_in, gate_in, scale_in, keep_in, rows, cotangent, value_out, gate_out, depth_s,
+):
     row_keep = keep_in[:, 0:1]
-    back_out = back_rows(order, cotangent, row_keep).astype(BF)
+    back_out = back_rows(row_order(), cotangent, row_keep).astype(BF)
     standard_two = standard_two_in[...]
     active = standard_two * rows[10:11, :]
     swish = jax.nn.sigmoid(active)
     slope = (swish + active * swish * (1.0 - swish)) * rows[10:11, :]
-    hidden = (active * swish).astype(BF)
-
-    @pl.when(step == 0)
-    def _():
-        for copy in copies:
-            copy.wait()
-
-    half = down_s.shape[1]
+    wait_weight()
     back_hidden = jnp.concatenate([dot(back_out, down_s[0], ACROSS), dot(back_out, down_s[1], ACROSS)], axis=1)
     gain_up = back_hidden * slope
-    depth_out[...] = scale_in[:, 0:1] * (
+    reach = 4 * BLOCK
+    depth_s[0:reach, :] = jnp.zeros((reach, depth_s.shape[1]), F32)
+    depth_s[reach + ROWS :, :] = jnp.zeros((reach, depth_s.shape[1]), F32)
+    depth_s[reach : reach + ROWS, :] = scale_in[:, 0:1] * (
         gain_up
         - jnp.mean(gain_up, axis=1, keepdims=True)
         - standard_two * jnp.mean(gain_up * standard_two, axis=1, keepdims=True)
     )
-    mixed = dot(hidden[:, :half], down_s[0]) + dot(hidden[:, half:], down_s[1])
-    layer = jnp.where(row_keep > 0, features_in[...].astype(F32) + mixed, 0.0).astype(BF)
-    layer_out[...] = dot(order, layer).astype(BF)
-
-
-def up_kernel(
-    depth_in, features_in, value_in, gate_in, keep_in, rows, cotangent, up_mine, up_other,
-    grad_out,
-    up_s, depth_s, sems,
-):
-    step = pl.program_id(0)
-    copies = fetch(((up_mine, up_other, up_s),), sems, lax.axis_index("fsdp"))
-
-    @pl.when(step == 0)
-    def _():
-        for copy in copies:
-            copy.start()
-
+    total = None
+    for k in range(9):
+        term = depth_s[(8 - k) * BLOCK : (8 - k) * BLOCK + ROWS, :] * rows[k : k + 1, :]
+        total = term if total is None else total + term
+    gate = gate_in[...]
+    back_value = row_keep * total * gate
+    value_out[...] = back_value.astype(BF)
+    gate_out[...] = (back_value * value_in[...] * (1.0 - gate)).astype(BF)
+
+
+def up_kernel(wait_weight, up_s, back_value, back_gate, features_in, keep_in, rows, cotangent, grad_out):
     order = row_order()
     row_keep = keep_in[:, 0:1]
     back_out = back_rows(order, cotangent, row_keep)
     centred = centre(features_in[...].astype(F32))
     scale_one = lax.rsqrt(jnp.mean(centred * centred, axis=1, keepdims=True) + EPSILON)
     standard = centred * scale_one
-    reach = 4 * BLOCK
-    depth_s[0:reach, :] = jnp.zeros((reach, depth_s.shape[1]), F32)
-    depth_s[reach + ROWS :, :] = jnp.zeros((reach, depth_s.shape[1]), F32)
-    depth_s[reach : reach + ROWS, :] = depth_in[...]
-    total = None
-    for k in range(9):
-        term = depth_s[(8 - k) * BLOCK : (8 - k) * BLOCK + ROWS, :] * rows[k : k + 1, :]
-        total = term if total is None else total + term
-    gate = gate_in[...]
-    back_value = row_keep * total * gate
-    back_gate = (back_value * value_in[...] * (1.0 - gate)).astype(BF)
-
-    @pl.when(step == 0)
-    def _():
-        for copy in copies:
-            copy.wait()
-
-    back_normed = dot(back_value.astype(BF), up_s[0], ACROSS) + dot(back_gate, up_s[1], ACROSS)
+    wait_weight()
+    back_normed = dot(back_value[...], up_s[0], ACROSS) + dot(back_gate[...], up_s[1], ACROSS)
     gain_in = back_normed * rows[9:10, :]
     back_input = scale_one * (
         gain_in
@@ -449,9 +468,10 @@
     return lax.ppermute(block, "dp", [(i, i ^ offset) for i in range(groups)])
 
 
-def held_call(kernel, outs, scratch, name, *operands):
+def held_call(kernel, outs, scratch, name, *operands, **specs):
     return pl.pallas_call(
         kernel,
+        **specs,
         out_shape=outs,
         scratch_shapes=scratch,
         compiler_params=params(32),
@@ -551,8 +571,8 @@
             pltpu.VMEM((2,) + up_weight.shape, BF),
             pltpu.VMEM((ROWS * width_in // SPAN // 128, groups * width_in // 128), F32),
             pltpu.VMEM((ROWS, LEAD + width_in // SPAN), F32),
-            pltpu.VMEM((4, 5 * ROWS, 256), BF),
-            pltpu.VMEM((GROUP + 1, 5 * ROWS, 256), F32),
+            pltpu.VMEM((4, 4 * ROWS, 256), BF),
+            pltpu.VMEM((GROUP + 1, 4 * ROWS + BLOCK, 256), F32),
             pltpu.VMEM((GROUP * ROWS, 256), BF),
             pltpu.VMEM((BINS // 2, ROWS, 256), F32),
             pltpu.VMEM((BINS // 2, ROWS + BLOCK, 256), F32),
@@ -566,10 +586,34 @@
         cost_estimate=cost(2e10 * blocks, 1e7),
         name="forward",
     )(incoming, packed, packed_other, linear_weight, linear_other, up_weight, up_other)
-    near = [given[0]] + [swap_rank(given[offset], offset, groups) for offset in range(1, 4)]
+    first, *cotangents[1:3] = lax.optimization_barrier((given[0], *cotangents[1:3]))
+    cotangents_other = [cotangent_other] + [swap_cores(block) for block in cotangents[1:3]]
+    near = [swap_rank(given[offset], offset, groups) for offset in range(1, 4)]
+    full = by_rows(width)
+
+    def back_call(body, name, sources, mine, other, outs, extra=()):
+        return pl.pallas_call(
+            functools.partial(bring, body, len(sources), outs),
+            grid=(blocks,),
+            in_specs=[anywhere] * (len(sources) + 2),
+            out_specs=[full] * outs,
+            out_shape=[shape((rows_here, width), BF)] * outs,
+            scratch_shapes=[
+                *[pltpu.VMEM((min(array.shape[0], ROWS), array.shape[1]), array.dtype) for array in sources],
+                pltpu.VMEM((2,) + mine.shape, BF),
+                pltpu.SemaphoreType.DMA((len(sources) + 2,)),
+                *extra,
+            ],
+            compiler_params=params(BACK),
+            cost_estimate=cost(1e6, 1e5),
+            name=name,
+        )(*sources, mine, other)
+
+    (layer_out,) = back_call(layer_kernel, "layer", (features, standard_two, keep, rows), down_weight, down_other, 1)
+    *near, layer_out, cotangents[3] = lax.optimization_barrier((*near, layer_out, cotangents[3]))
+    near = [first, *near]
     far = swap_cores(held_call(pack_kernel, shape((4, rows_here, 128), BF), [], "pack", *near))
-    given[0], *cotangents[1:] = lax.optimization_barrier((given[0], *cotangents[1:]))
-    cotangents_other = [cotangent_other] + [swap_cores(block) for block in cotangents[1:]]
+    cotangents_other.append(swap_cores(cotangents[3]))
     layers = groups // 4
     block = width // members // 4
     size = block // layers
@@ -582,38 +626,18 @@
         half_sum, far, *cotangents_other,
     )
     moved = [swap_rank(other, 4 * (offset + 1), groups) for offset, other in enumerate(others)]
-    full, thin = by_rows(width), by_rows(128)
-    layer_out, depth = pl.pallas_call(
-        down_kernel,
-        grid=(blocks,),
-        in_specs=[full, full, thin, thin, whole(rows.shape), full, anywhere, anywhere],
-        out_specs=[full, full],
-        out_shape=(shape((rows_here, width), BF), shape((rows_here, width), F32)),
-        scratch_shapes=[pltpu.VMEM((2,) + down_weight.shape, BF), pltpu.SemaphoreType.DMA((2,))],
-        compiler_params=params(BACK),
-        cost_estimate=cost(1e6, 1e5),
-        name="down",
-    )(features, standard_two, scale, keep, rows, cotangent, down_weight, down_other)
-    *moved, layer_out, depth = lax.optimization_barrier((*moved, layer_out, depth))
+    value_back, gate_back = back_call(
+        depth_kernel_back, "depth", (standard_two, value, gate, scale, keep, rows, cotangent), down_weight, down_other, 2,
+        [pltpu.VMEM((ROWS + 8 * BLOCK, width), F32)],
+    )
+    *moved, value_back, gate_back = lax.optimization_barrier((*moved, value_back, gate_back))
     for part in moved:
         own = own + part.astype(F32)
     own = (own * (1.0 / math.sqrt(rows_here * groups * members))).astype(BF)
     pieces = [own] + [swap_rank(own, 4 * offset, groups) for offset in range(1, layers)]
-    grad_input = pl.pallas_call(
-        up_kernel,
-        grid=(blocks,),
-        in_specs=[full, full, full, full, thin, whole(rows.shape), full, anywhere, anywhere],
-        out_specs=full,
-        out_shape=shape((rows_here, width), BF),
-        scratch_shapes=[
-            pltpu.VMEM((2,) + up_weight.shape, BF),
-            pltpu.VMEM((ROWS + 8 * BLOCK, width), F32),
-            pltpu.SemaphoreType.DMA((2,)),
-        ],
-        compiler_params=params(BACK),
-        cost_estimate=cost(1e6, 1e5),
-        name="up",
-    )(depth, features, value, gate, keep, rows, cotangent, up_weight, up_other)
+    (grad_input,) = back_call(
+        up_kernel, "up", (value_back, gate_back, features, keep, rows, cotangent), up_weight, up_other, 1
+    )
     *pieces, grad_input = lax.optimization_barrier((*pieces, grad_input))
     left, right = held_call(
         layers_kernel, [shape((block, width // 2), BF)] * 2, [pltpu.VMEM((block, width), F32)], "layers", *pieces
@@ -622,8 +646,9 @@
     left_y, right_x = swap_rank(left, 2, groups), swap_rank(right, 1, groups)
     left_xy, right_xy = swap_rank(left_x, 2, groups), swap_rank(right_y, 1, groups)
     grad_down = held_call(
-        finish_kernel, shape((half, width), F32), [], "finish",
-        left, left_x, left_y, left_xy, right, right_x, right_y, right_xy,
+        finish_kernel, shape((half, width), F32),
+        [pltpu.VMEM((8, block, width // 2), F32), pltpu.SemaphoreType.DMA((8,))], "finish",
+        left, left_x, left_y, left_xy, right, right_x, right_y, right_xy, out_specs=anywhere,
     )
     return (layer_out, grad_input, grad_down)
 

time: 86.4 us -> 82.6 us (0.956)
  waiting for transfers between devices: 18.4 us -> 15.3 us
  local copies, waits for them, and re-layouts: 2.56 us -> 0.73 us
  Pallas kernels: 31.3 us -> 32.3 us
    ppermute x18, waiting for transfers between devices: 10.5 us -> 5.37 us  [swap_rank(): return lax.ppermute(block, 'dp', [(i, i ^ offset) for i in range(groups)])]
    unnamed x10 -> x8, local copies, waits for them, and re-layouts: 2.56 us -> 0.73 us
    pallas_call x7 -> x8, Pallas kernels: 13.5 us -> 15.1 us  [the longest x3 12.9 us: back_call(): pl.pallas_call(functools.partial(bring, body, len(sources), outs), grid=(...]
    all_to_all x1, waiting for transfers between devices: 7.3 us -> 8.8 us  [local(): lax.all_to_all(outgoing, 'dp', split_axis=0, concat_axis=0, tiled=True)]
  transfers between devices with their start and end apart: 28 -> 28, of which waited for: 10 -> 7; matrix products, arithmetic and copies ran while one was open for 0% -> 0% of each run, Pallas kernels for 31% -> 34%
where the time goes in v6:
time: 82.6 us; the launch traced here: 82.3 us
  starting transfers between devices  32.9 us (40%)
  Pallas kernels  32.3 us (39%)
  waiting for transfers between devices  15.3 us (19%)
  between operations  0.98 us (1%)
    ppermute x18, starting transfers between devices, swap_rank(): return lax.ppermute(block, 'dp', [(i, i ^ offset) for i in range(groups)])  22.7 us
    pallas_call x1, Pallas kernels, local(): pl.pallas_call(forward_kernel, grid=(blocks,), in_specs=[*[anywhere] * 7]...  14.4 us
    pallas_call x3, Pallas kernels, back_call(): pl.pallas_call(functools.partial(bring, body, len(sources), outs), grid=(...  12.9 us
    all_to_all x1, waiting for transfers between devices, local(): lax.all_to_all(outgoing, 'dp', split_axis=0, concat_axis=0, tiled=True)  8.8 us
    all_to_all x1, starting transfers between devices, local(): lax.all_to_all(outgoing, 'dp', split_axis=0, concat_axis=0, tiled=True)  8.3 us
    ppermute x18, waiting for transfers between devices, swap_rank(): return lax.ppermute(block, 'dp', [(i, i ^ offset) for i in range(groups)])  5.37 us
    pallas_call x1, Pallas kernels, local(): pl.pallas_call(send_kernel, in_specs=[anywhere, held, held] + [anywhere]...  2.85 us
    pallas_call x5, Pallas kernels, held_call(): pl.pallas_call(kernel, **specs, out_shape=outs, scratch_shapes=scratch, c...  2.16 us
  transfers between devices with their start and end apart: 28, of which 7 were waited for; matrix products, arithmetic and copies ran while one was open for 0% of the time, Pallas kernels for 34%

profile of v6, /device:TPU:0, one launch (start us, length us, event | category | flops | bytes accessed | tf_op | source)
XLA Modules:
  0.0 82.3 jit_solution(2353973097265308465)
XLA Ops:
  1.2 2.8 %send.1 = (bf16[16,88,128]{2,1,0:T(8,128)(2,1)}, bf16[160,512]{1,0:T(8,128)(2,1)}) custom-call(bf16[16,10240]{1,0:T(8,128)(2,1)} %mel.1, s32[1,16]{1,0:T(1,128)} %bitcast.2, s32[1,16]{1,0:T(1,128)} %bitcast.3, bf16[9,128]{1,0:T(8,128)(2,1)} %first.1, bf16[9,128]{1,0:T(8,128)(2,1)} %depth_a.1, bf16[256,128]{1,0:T(8,128)(2,1)} %point_a.1, ...), custom_call_target="tpu_custom_call" | custom-call | flops 200000000 | bytes 1000000 | tf_op jit(solution)/shard_map/send/pallas_call | solution.py:511
  4.1 8.3 %all-to-all-start = ((bf16[16,88,128]{2,1,0:T(8,128)(2,1)}), bf16[16,88,128]{2,1,0:T(8,128)(2,1)S(1)}, u32[]{:S(2)}, u32[]{:S(2)}) async-start(bf16[16,88,128]{2,1,0:T(8,128)(2,1)} %get-tuple-element.42), calls=%async_computation | async-start | bytes 720896 | tf_op jit(solution)/shard_map/all_to_all | solution.py:525
  12.5 2.9 %collective-permute-start.7 = (bf16[128,1024]{1,0:T(8,128)(2,1)}, bf16[128,1024]{1,0:T(8,128)(2,1)S(1)}, u32[]{:S(2)}, u32[]{:S(2)}) collective-permute-start(bf16[128,1024]{1,0:T(8,128)(2,1)} %refs_5_.1), channel_id=1, source_target_pairs={{0,6},{2,4},{4,2},{6,0},{8,14},{10,12},{12,10},{14,8},{16,22},{18,... | collective-permute-start | bytes 786440 | tf_op jit(solution)/shard_map/ppermute | solution.py:468
  16.1 8.8 %all-to-all-done.incoming_in = bf16[16,88,128]{2,1,0:T(8,128)(2,1)S(1)} async-done(((bf16[16,88,128]{2,1,0:T(8,128)(2,1)}), bf16[16,88,128]{2,1,0:T(8,128)(2,1)S(1)}, u32[]{:S(2)}, u32[]{:S(2)}) %all-to-all-start) | async-done | bytes 360480 | tf_op jit(solution)/shard_map/all_to_all | solution.py:525
  25.6 14.4 %forward.1 = (bf16[2,128,128]{2,1,0:T(8,128)(2,1)}, bf16[2,128,128]{2,1,0:T(8,128)(2,1)}, bf16[2,128,128]{2,1,0:T(8,128)(2,1)}, bf16[2,128,128]{2,1,0:T(8,128)(2...) custom-call(bf16[16,88,128]{2,1,0:T(8,128)(2,1)} %copy-done.2, ...), custom_call_target="tpu_custom_call" | custom-call | flops 20000000000 | bytes 10000000 | tf_op jit(solution)/shard_map/forward/pallas_call | solution.py:536
  41.3 2.2 %collective-permute-start.5 = (bf16[2,128,128]{2,1,0:T(8,128)(2,1)}, bf16[2,128,128]{2,1,0:T(8,128)(2,1)S(1)}, u32[]{:S(2)}, u32[]{:S(2)}) collective-permute-start(bf16[2,128,128]{2,1,0:T(8,128)(2,1)} %get-tuple-element.46), channel_id=1, source_target_pairs={{0,6},{2,4},{4,2},{6,0},{8,14},{10,12},{12,10},{14,8},{16,22},{18,... | collective-permute-start | bytes 196616 | tf_op jit(solution)/shard_map/ppermute | solution.py:468
  43.5 3.2 %layer.1 = bf16[128,1024]{1,0:T(8,128)(2,1)} custom-call(bf16[128,1024]{1,0:T(8,128)(2,1)} %get-tuple-element.47.refs_0_.refs_2_, f32[128,1024]{1,0:T(8,128)} %get-tuple-element.48.refs_1_.refs_0_, f32[128,128]{1,0:T(8,128)} %get-tuple-element.49.refs_2_.refs_4_.refs_3_, f32[16,1024]{1,0:T(8,128)} %get-tuple-element.50.refs_3_.refs_5_.refs_4_, ...), custom_call_target="tpu_custom_call" | custom-call | flops 1000000 | bytes 100000 | tf_op jit(solution)/shard_map/layer/pallas_call | solution.py:595
  48.4 1.1 %collective-permute-done.10.refs_1_ = bf16[4,128,128]{2,1,0:T(8,128)(2,1)S(1)} collective-permute-done((bf16[4,128,128]{2,1,0:T(8,128)(2,1)S(1)}, bf16[4,128,128]{2,1,0:T(8,128)(2,1)S(1)}, u32[]{:S(2)}, u32[]{:S(2)}) %collective-permute-start.10) | collective-permute-done | bytes 131104 | tf_op jit(solution)/shard_map/ppermute | solution.py:464
  49.8 1.0 %collective-permute-start.15 = (bf16[32,1024]{1,0:T(8,128)(2,1)S(1)}, bf16[32,1024]{1,0:T(8,128)(2,1)S(1)}, u32[]{:S(2)}, u32[]{:S(2)}) collective-permute-start(bf16[32,1024]{1,0:T(8,128)(2,1)S(1)} %get-tuple-element.61), channel_id=1, source_target_pairs={{0,8},{2,10},{4,12},{6,14},{8,0},{10,2},{12,4},{14,6},{16,24},{18,... | collective-permute-start | bytes 196616 | tf_op jit(solution)/shard_map/ppermute | solution.py:468
  50.9 0.9 %collective-permute-start.16 = (bf16[32,1024]{1,0:T(8,128)(2,1)S(1)}, bf16[32,1024]{1,0:T(8,128)(2,1)S(1)}, u32[]{:S(2)}, u32[]{:S(2)}) collective-permute-start(bf16[32,1024]{1,0:T(8,128)(2,1)S(1)} %get-tuple-element.62), channel_id=1, source_target_pairs={{0,16},{2,18},{4,20},{6,22},{8,24},{10,26},{12,28},{14,30},{16,0},... | collective-permute-start | bytes 196616 | tf_op jit(solution)/shard_map/ppermute | solution.py:468
  51.8 2.5 %collective-permute-start.17 = (bf16[32,1024]{1,0:T(8,128)(2,1)S(1)}, bf16[32,1024]{1,0:T(8,128)(2,1)S(1)}, u32[]{:S(2)}, u32[]{:S(2)}) collective-permute-start(bf16[32,1024]{1,0:T(8,128)(2,1)S(1)} %get-tuple-element.63), channel_id=1, source_target_pairs={{0,24},{2,26},{4,28},{6,30},{8,16},{10,18},{12,20},{14,22},{16,8},... | collective-permute-start | bytes 196616 | tf_op jit(solution)/shard_map/ppermute | solution.py:468
  54.3 4.5 %depth.1 = (bf16[128,1024]{1,0:T(8,128)(2,1)}, bf16[128,1024]{1,0:T(8,128)(2,1)}) custom-call(f32[128,1024]{1,0:T(8,128)} %get-tuple-element.48.refs_1_.refs_0_, f32[128,1024]{1,0:T(8,128)} %get-tuple-element.64.refs_1_, f32[128,1024]{1,0:T(8,128)} %get-tuple-element.65.refs_2_, f32[128,128]{1,0:T(8,128)} %get-tuple-element.66.refs_3_, ...), custom_call_target="tpu_custom_call" | custom-call | flops 1000000 | bytes 100000 | tf_op jit(solution)/shard_map/depth/pallas_call | solution.py:595
  59.3 1.4 %collective-permute-start.18 = (bf16[32,1024]{1,0:T(8,128)(2,1)S(1)}, bf16[32,1024]{1,0:T(8,128)(2,1)S(1)}, u32[]{:S(2)}, u32[]{:S(2)}) collective-permute-start(bf16[32,1024]{1,0:T(8,128)(2,1)S(1)} %multiply_convert_fusion.refs_0_), channel_id=1, source_target_pairs={{0,8},{2,10},{4,12},{6,14},{8,0},{10,2},{12,4},{14,6},{16,24},{18,... | collective-permute-start | bytes 196616 | tf_op jit(solution)/shard_map/ppermute | solution.py:468
  61.1 2.6 %collective-permute-start.20 = (bf16[32,1024]{1,0:T(8,128)(2,1)S(1)}, bf16[32,1024]{1,0:T(8,128)(2,1)S(1)}, u32[]{:S(2)}, u32[]{:S(2)}) collective-permute-start(bf16[32,1024]{1,0:T(8,128)(2,1)S(1)} %multiply_convert_fusion.refs_0_), channel_id=1, source_target_pairs={{0,24},{2,26},{4,28},{6,30},{8,16},{10,18},{12,20},{14,22},{16,8},... | collective-permute-start | bytes 196616 | tf_op jit(solution)/shard_map/ppermute | solution.py:468
  63.7 5.2 %up.1 = bf16[128,1024]{1,0:T(8,128)(2,1)} custom-call(bf16[128,1024]{1,0:T(8,128)(2,1)} %get-tuple-element.72.refs_0_, bf16[128,1024]{1,0:T(8,128)(2,1)} %get-tuple-element.73.refs_1_, bf16[128,1024]{1,0:T(8,128)(2,1)} %get-tuple-element.47.refs_0_.refs_2_, f32[128,128]{1,0:T(8,128)} %get-tuple-element.49.refs_2_.refs_4_.refs_3_, ...), custom_call_target="tpu_custom_call" | custom-call | flops 1000000 | bytes 100000 | tf_op jit(solution)/shard_map/up/pallas_call | solution.py:595
  69.8 0.9 %collective-permute-start.25 = (bf16[128,512]{1,0:T(8,128)(2,1)S(1)}, bf16[128,512]{1,0:T(8,128)(2,1)S(1)}, u32[]{:S(2)}, u32[]{:S(2)}) collective-permute-start(bf16[128,512]{1,0:T(8,128)(2,1)S(1)} %get-tuple-element.80.refs_4_), channel_id=1, source_target_pairs={{0,4},{2,6},{4,0},{6,2},{8,12},{10,14},{12,8},{14,10},{16,20},{18,... | collective-permute-start | bytes 393224 | tf_op jit(solution)/shard_map/ppermute | solution.py:468
  70.8 1.1 %collective-permute-start.22 = (bf16[128,512]{1,0:T(8,128)(2,1)S(1)}, bf16[128,512]{1,0:T(8,128)(2,1)S(1)}, u32[]{:S(2)}, u32[]{:S(2)}) collective-permute-start(bf16[128,512]{1,0:T(8,128)(2,1)S(1)} %get-tuple-element.79.refs_0_), channel_id=1, source_target_pairs={{0,4},{2,6},{4,0},{6,2},{8,12},{10,14},{12,8},{14,10},{16,20},{18,... | collective-permute-start | bytes 393224 | tf_op jit(solution)/shard_map/ppermute | solution.py:468
  71.8 1.3 %collective-permute-start.24 = (bf16[128,512]{1,0:T(8,128)(2,1)S(1)}, bf16[128,512]{1,0:T(8,128)(2,1)S(1)}, u32[]{:S(2)}, u32[]{:S(2)}) collective-permute-start(bf16[128,512]{1,0:T(8,128)(2,1)S(1)} %get-tuple-element.80.refs_4_), channel_id=1, source_target_pairs={{0,2},{2,0},{4,6},{6,4},{8,10},{10,8},{12,14},{14,12},{16,18},{18,... | collective-permute-start | bytes 393224 | tf_op jit(solution)/shard_map/ppermute | solution.py:468
  73.2 1.7 %collective-permute-done.21.refs_1_ = bf16[128,512]{1,0:T(8,128)(2,1)S(1)} collective-permute-done((bf16[128,512]{1,0:T(8,128)(2,1)S(1)}, bf16[128,512]{1,0:T(8,128)(2,1)S(1)}, u32[]{:S(2)}, u32[]{:S(2)}) %collective-permute-start.21) | collective-permute-done | bytes 131104 | tf_op jit(solution)/shard_map/ppermute | solution.py:468
  74.9 0.8 collective-permute-start.23
  75.7 1.8 %collective-permute-start.26 = (bf16[128,512]{1,0:T(8,128)(2,1)S(1)}, bf16[128,512]{1,0:T(8,128)(2,1)S(1)}, u32[]{:S(2)}, u32[]{:S(2)}) collective-permute-start(bf16[128,512]{1,0:T(8,128)(2,1)S(1)} %collective-permute-done.25.refs_6_), channel_id=1, source_target_pairs={{0,2},{2,0},{4,6},{6,4},{8,10},{10,8},{12,14},{14,12},{16,18},{18,... | collective-permute-start | bytes 393224 | tf_op jit(solution)/shard_map/ppermute | solution.py:468
  77.6 2.3 %collective-permute-done.23.refs_3_ = bf16[128,512]{1,0:T(8,128)(2,1)S(1)} collective-permute-done((bf16[128,512]{1,0:T(8,128)(2,1)S(1)}, bf16[128,512]{1,0:T(8,128)(2,1)S(1)}, u32[]{:S(2)}, u32[]{:S(2)}) %collective-permute-start.23) | collective-permute-done | bytes 131104 | tf_op jit(solution)/shard_map/ppermute | solution.py:468
  79.9 0.8 collective-permute-done.26.refs_7_
  80.7 1.4 %finish.1 = f32[512,1024]{1,0:T(8,128)} custom-call(bf16[128,512]{1,0:T(8,128)(2,1)S(1)} %get-tuple-element.79.refs_0_, bf16[128,512]{1,0:T(8,128)(2,1)S(1)} %collective-permute-done.21.refs_1_, bf16[128,512]{1,0:T(8,128)(2,1)S(1)} %collective-permute-done.22.refs_2_, bf16[128,512]{1,0:T(8,128)(2,1)S(1)} %collective-permute-done.23.refs_3_, ...), custom_call_target="tpu_custom_call" | custom-call | flops 1000000 | bytes 100000 | tf_op jit(solution)/shard_map/finish/pallas_call | solution.py:472
  (51 shorter events, 7.1 us)
Async XLA Ops:
  0.6 24.2 %collective-permute-start.1 = (bf16[2560,512]{1,0:T(8,128)(2,1)}, bf16[2560,512]{1,0:T(8,128)(2,1)}, u32[]{:S(2)}, u32[]{:S(2)}) collective-permute-start(bf16[2560,512]{1,0:T(8,128)(2,1)} %linear_mine.1), channel_id=1, source_target_pairs={{0,1},{1,0},{2,3},{3,2},{4,5},{5,4},{6,7},{7,6},{8,9},{9,8},{10,11... | collective-permute-start | bytes 7864328 | tf_op jit(solution)/shard_map/ppermute | solution.py:464
  1.2 14.9 %collective-permute-start.2 = (bf16[1024,1024]{1,0:T(8,128)(2,1)}, bf16[1024,1024]{1,0:T(8,128)(2,1)}, u32[]{:S(2)}, u32[]{:S(2)}) collective-permute-start(bf16[1024,1024]{1,0:T(8,128)(2,1)} %refs_6_.3), channel_id=1, source_target_pairs={{0,1},{1,0},{2,3},{3,2},{4,5},{5,4},{6,7},{7,6},{8,9},{9,8},{10,11... | collective-permute-start | bytes 6291464 | tf_op jit(solution)/shard_map/ppermute | solution.py:464
  4.1 20.8 %all-to-all-start = ((bf16[16,88,128]{2,1,0:T(8,128)(2,1)}), bf16[16,88,128]{2,1,0:T(8,128)(2,1)S(1)}, u32[]{:S(2)}, u32[]{:S(2)}) async-start(bf16[16,88,128]{2,1,0:T(8,128)(2,1)} %get-tuple-element.42), calls=%async_computation | async-start | bytes 720896 | tf_op jit(solution)/shard_map/all_to_all | solution.py:525
  12.4 3.5 %collective-permute-start = (bf16[160,512]{1,0:T(8,128)(2,1)}, bf16[160,512]{1,0:T(8,128)(2,1)S(1)}, u32[]{:S(2)}, u32[]{:S(2)}) collective-permute-start(bf16[160,512]{1,0:T(8,128)(2,1)} %get-tuple-element.43.packed_mine), channel_id=1, source_target_pairs={{0,1},{1,0},{2,3},{3,2},{4,5},{5,4},{6,7},{7,6},{8,9},{9,8},{10,11... | collective-permute-start | bytes 491528 | tf_op jit(solution)/shard_map/ppermute | solution.py:464
  12.5 34.3 %collective-permute-start.7 = (bf16[128,1024]{1,0:T(8,128)(2,1)}, bf16[128,1024]{1,0:T(8,128)(2,1)S(1)}, u32[]{:S(2)}, u32[]{:S(2)}) collective-permute-start(bf16[128,1024]{1,0:T(8,128)(2,1)} %refs_5_.1), channel_id=1, source_target_pairs={{0,6},{2,4},{4,2},{6,0},{8,14},{10,12},{12,10},{14,8},{16,22},{18,... | collective-permute-start | bytes 786440 | tf_op jit(solution)/shard_map/ppermute | solution.py:468
  15.4 25.4 %collective-permute-start.8 = (bf16[128,1024]{1,0:T(8,128)(2,1)}, bf16[128,1024]{1,0:T(8,128)(2,1)S(1)}, u32[]{:S(2)}, u32[]{:S(2)}) collective-permute-start(bf16[128,1024]{1,0:T(8,128)(2,1)} %refs_5_.1), channel_id=1, source_target_pairs={{0,2},{2,0},{4,6},{6,4},{8,10},{10,8},{12,14},{14,12},{16,18},{18,... | collective-permute-start | bytes 786440 | tf_op jit(solution)/shard_map/ppermute | solution.py:468
  15.9 25.3 %collective-permute-start.9 = (bf16[128,1024]{1,0:T(8,128)(2,1)}, bf16[128,1024]{1,0:T(8,128)(2,1)S(1)}, u32[]{:S(2)}, u32[]{:S(2)}) collective-permute-start(bf16[128,1024]{1,0:T(8,128)(2,1)} %refs_5_.1), channel_id=1, source_target_pairs={{0,4},{2,6},{4,0},{6,2},{8,12},{10,14},{12,8},{14,10},{16,20},{18,... | collective-permute-start | bytes 786440 | tf_op jit(solution)/shard_map/ppermute | solution.py:468
  16.1 27.5 %collective-permute-start.6 = (bf16[512,1024]{1,0:T(8,128)(2,1)}, bf16[512,1024]{1,0:T(8,128)(2,1)}, u32[]{:S(2)}, u32[]{:S(2)}) collective-permute-start(bf16[512,1024]{1,0:T(8,128)(2,1)} %refs_7_.1), channel_id=1, source_target_pairs={{0,1},{1,0},{2,3},{3,2},{4,5},{5,4},{6,7},{7,6},{8,9},{9,8},{10,11... | collective-permute-start | bytes 3145736 | tf_op jit(solution)/shard_map/ppermute | solution.py:464
  40.0 7.4 %collective-permute-start.3 = (bf16[2,128,128]{2,1,0:T(8,128)(2,1)}, bf16[2,128,128]{2,1,0:T(8,128)(2,1)S(1)}, u32[]{:S(2)}, u32[]{:S(2)}) collective-permute-start(bf16[2,128,128]{2,1,0:T(8,128)(2,1)} %get-tuple-element.44), channel_id=1, source_target_pairs={{0,2},{2,0},{4,6},{6,4},{8,10},{10,8},{12,14},{14,12},{16,18},{18,... | collective-permute-start | bytes 196616 | tf_op jit(solution)/shard_map/ppermute | solution.py:468
  40.7 6.7 %collective-permute-start.4 = (bf16[2,128,128]{2,1,0:T(8,128)(2,1)}, bf16[2,128,128]{2,1,0:T(8,128)(2,1)S(1)}, u32[]{:S(2)}, u32[]{:S(2)}) collective-permute-start(bf16[2,128,128]{2,1,0:T(8,128)(2,1)} %get-tuple-element.45), channel_id=1, source_target_pairs={{0,4},{2,6},{4,0},{6,2},{8,12},{10,14},{12,8},{14,10},{16,20},{18,... | collective-permute-start | bytes 196616 | tf_op jit(solution)/shard_map/ppermute | solution.py:468
  41.3 6.1 %collective-permute-start.5 = (bf16[2,128,128]{2,1,0:T(8,128)(2,1)}, bf16[2,128,128]{2,1,0:T(8,128)(2,1)S(1)}, u32[]{:S(2)}, u32[]{:S(2)}) collective-permute-start(bf16[2,128,128]{2,1,0:T(8,128)(2,1)} %get-tuple-element.46), channel_id=1, source_target_pairs={{0,6},{2,4},{4,2},{6,0},{8,14},{10,12},{12,10},{14,8},{16,22},{18,... | collective-permute-start | bytes 196616 | tf_op jit(solution)/shard_map/ppermute | solution.py:468
  43.5 4.8 %collective-permute-start.11 = (bf16[128,1024]{1,0:T(8,128)(2,1)S(1)}, bf16[128,1024]{1,0:T(8,128)(2,1)S(1)}, u32[]{:S(2)}, u32[]{:S(2)}) collective-permute-start(bf16[128,1024]{1,0:T(8,128)(2,1)S(1)} %copy-done), channel_id=1, source_target_pairs={{0,1},{1,0},{2,3},{3,2},{4,5},{5,4},{6,7},{7,6},{8,9},{9,8},{10,11... | collective-permute-start | bytes 786440 | tf_op jit(solution)/shard_map/ppermute | solution.py:464
  49.8 9.0 %collective-permute-start.15 = (bf16[32,1024]{1,0:T(8,128)(2,1)S(1)}, bf16[32,1024]{1,0:T(8,128)(2,1)S(1)}, u32[]{:S(2)}, u32[]{:S(2)}) collective-permute-start(bf16[32,1024]{1,0:T(8,128)(2,1)S(1)} %get-tuple-element.61), channel_id=1, source_target_pairs={{0,8},{2,10},{4,12},{6,14},{8,0},{10,2},{12,4},{14,6},{16,24},{18,... | collective-permute-start | bytes 196616 | tf_op jit(solution)/shard_map/ppermute | solution.py:468
  50.9 8.4 %collective-permute-start.16 = (bf16[32,1024]{1,0:T(8,128)(2,1)S(1)}, bf16[32,1024]{1,0:T(8,128)(2,1)S(1)}, u32[]{:S(2)}, u32[]{:S(2)}) collective-permute-start(bf16[32,1024]{1,0:T(8,128)(2,1)S(1)} %get-tuple-element.62), channel_id=1, source_target_pairs={{0,16},{2,18},{4,20},{6,22},{8,24},{10,26},{12,28},{14,30},{16,0},... | collective-permute-start | bytes 196616 | tf_op jit(solution)/shard_map/ppermute | solution.py:468
  51.8 7.5 %collective-permute-start.17 = (bf16[32,1024]{1,0:T(8,128)(2,1)S(1)}, bf16[32,1024]{1,0:T(8,128)(2,1)S(1)}, u32[]{:S(2)}, u32[]{:S(2)}) collective-permute-start(bf16[32,1024]{1,0:T(8,128)(2,1)S(1)} %get-tuple-element.63), channel_id=1, source_target_pairs={{0,24},{2,26},{4,28},{6,30},{8,16},{10,18},{12,20},{14,22},{16,8},... | collective-permute-start | bytes 196616 | tf_op jit(solution)/shard_map/ppermute | solution.py:468
  59.3 9.7 %collective-permute-start.18 = (bf16[32,1024]{1,0:T(8,128)(2,1)S(1)}, bf16[32,1024]{1,0:T(8,128)(2,1)S(1)}, u32[]{:S(2)}, u32[]{:S(2)}) collective-permute-start(bf16[32,1024]{1,0:T(8,128)(2,1)S(1)} %multiply_convert_fusion.refs_0_), channel_id=1, source_target_pairs={{0,8},{2,10},{4,12},{6,14},{8,0},{10,2},{12,4},{14,6},{16,24},{18,... | collective-permute-start | bytes 196616 | tf_op jit(solution)/shard_map/ppermute | solution.py:468
  60.7 8.3 %collective-permute-start.19 = (bf16[32,1024]{1,0:T(8,128)(2,1)S(1)}, bf16[32,1024]{1,0:T(8,128)(2,1)S(1)}, u32[]{:S(2)}, u32[]{:S(2)}) collective-permute-start(bf16[32,1024]{1,0:T(8,128)(2,1)S(1)} %multiply_convert_fusion.refs_0_), channel_id=1, source_target_pairs={{0,16},{2,18},{4,20},{6,22},{8,24},{10,26},{12,28},{14,30},{16,0},... | collective-permute-start | bytes 196616 | tf_op jit(solution)/shard_map/ppermute | solution.py:468
  61.1 7.9 %collective-permute-start.20 = (bf16[32,1024]{1,0:T(8,128)(2,1)S(1)}, bf16[32,1024]{1,0:T(8,128)(2,1)S(1)}, u32[]{:S(2)}, u32[]{:S(2)}) collective-permute-start(bf16[32,1024]{1,0:T(8,128)(2,1)S(1)} %multiply_convert_fusion.refs_0_), channel_id=1, source_target_pairs={{0,24},{2,26},{4,28},{6,30},{8,16},{10,18},{12,20},{14,22},{16,8},... | collective-permute-start | bytes 196616 | tf_op jit(solution)/shard_map/ppermute | solution.py:468
  69.1 5.8 %collective-permute-start.21 = (bf16[128,512]{1,0:T(8,128)(2,1)S(1)}, bf16[128,512]{1,0:T(8,128)(2,1)S(1)}, u32[]{:S(2)}, u32[]{:S(2)}) collective-permute-start(bf16[128,512]{1,0:T(8,128)(2,1)S(1)} %get-tuple-element.79.refs_0_), channel_id=1, source_target_pairs={{0,2},{2,0},{4,6},{6,4},{8,10},{10,8},{12,14},{14,12},{16,18},{18,... | collective-permute-start | bytes 393224 | tf_op jit(solution)/shard_map/ppermute | solution.py:468
  69.8 5.9 %collective-permute-start.25 = (bf16[128,512]{1,0:T(8,128)(2,1)S(1)}, bf16[128,512]{1,0:T(8,128)(2,1)S(1)}, u32[]{:S(2)}, u32[]{:S(2)}) collective-permute-start(bf16[128,512]{1,0:T(8,128)(2,1)S(1)} %get-tuple-element.80.refs_4_), channel_id=1, source_target_pairs={{0,4},{2,6},{4,0},{6,2},{8,12},{10,14},{12,8},{14,10},{16,20},{18,... | collective-permute-start | bytes 393224 | tf_op jit(solution)/shard_map/ppermute | solution.py:468
  70.8 6.8 %collective-permute-start.22 = (bf16[128,512]{1,0:T(8,128)(2,1)S(1)}, bf16[128,512]{1,0:T(8,128)(2,1)S(1)}, u32[]{:S(2)}, u32[]{:S(2)}) collective-permute-start(bf16[128,512]{1,0:T(8,128)(2,1)S(1)} %get-tuple-element.79.refs_0_), channel_id=1, source_target_pairs={{0,4},{2,6},{4,0},{6,2},{8,12},{10,14},{12,8},{14,10},{16,20},{18,... | collective-permute-start | bytes 393224 | tf_op jit(solution)/shard_map/ppermute | solution.py:468
  71.8 5.8 %collective-permute-start.24 = (bf16[128,512]{1,0:T(8,128)(2,1)S(1)}, bf16[128,512]{1,0:T(8,128)(2,1)S(1)}, u32[]{:S(2)}, u32[]{:S(2)}) collective-permute-start(bf16[128,512]{1,0:T(8,128)(2,1)S(1)} %get-tuple-element.80.refs_4_), channel_id=1, source_target_pairs={{0,2},{2,0},{4,6},{6,4},{8,10},{10,8},{12,14},{14,12},{16,18},{18,... | collective-permute-start | bytes 393224 | tf_op jit(solution)/shard_map/ppermute | solution.py:468
  74.9 5.0 %collective-permute-start.23 = (bf16[128,512]{1,0:T(8,128)(2,1)S(1)}, bf16[128,512]{1,0:T(8,128)(2,1)S(1)}, u32[]{:S(2)}, u32[]{:S(2)}) collective-permute-start(bf16[128,512]{1,0:T(8,128)(2,1)S(1)} %collective-permute-done.21.refs_1_), channel_id=1, source_target_pairs={{0,4},{2,6},{4,0},{6,2},{8,12},{10,14},{12,8},{14,10},{16,20},{18,... | collective-permute-start | bytes 393224 | tf_op jit(solution)/shard_map/ppermute | solution.py:468
  75.7 5.0 %collective-permute-start.26 = (bf16[128,512]{1,0:T(8,128)(2,1)S(1)}, bf16[128,512]{1,0:T(8,128)(2,1)S(1)}, u32[]{:S(2)}, u32[]{:S(2)}) collective-permute-start(bf16[128,512]{1,0:T(8,128)(2,1)S(1)} %collective-permute-done.25.refs_6_), channel_id=1, source_target_pairs={{0,2},{2,0},{4,6},{6,4},{8,10},{10,8},{12,14},{14,12},{16,18},{18,... | collective-permute-start | bytes 393224 | tf_op jit(solution)/shard_map/ppermute | solution.py:468
  (8 other events, 57.0 us)

commit v7 on v6

--- a/solution.py
+++ b/solution.py
@@ -83,8 +83,10 @@
     packed[32:160, 384:512] = point_b_s[128:256, :]
 
 
-def unpack_weights(low, high, band, taps_a, taps_b, point_a, point_b, rows):
-    low, high = low[...].astype(F32), high[...].astype(F32)
+def weights_kernel(mine, other, band, taps_a, taps_b, point_a, point_b, rows):
+    me = lax.axis_index("fsdp")
+    near, far = mine[...].astype(F32), other[...].astype(F32)
+    low, high = jnp.where(me == 0, near, far), jnp.where(me == 0, far, near)
     rows[:, 0:512] = low[0:16]
     rows[:, 512:1024] = high[0:16]
     first = jnp.concatenate([low[16:32, 0:128], high[16:32, 0:128]], axis=1).astype(BF)
@@ -116,39 +118,32 @@
 
 
 def forward_kernel(
-    incoming_in, packed_mine, packed_other, linear_mine, linear_other, up_mine, up_other,
-    give_0, give_1, give_2, give_3, features_o, value_o, gate_o, standard_two_o, scale_o, keep_o, rows_o,
-    incoming, features_out, value_out, gate_out, standard_two_out, scale_out, keep_out, rows, packed_s, band, taps_a, taps_b, point_a, point_b, linear_s, up_s, pick_s, ext_s, x_s, first_s, spread_s, even_s, odd_s, flat_s, gated_s, kept_s, sems, out_sems,
+    incoming_in, band_in, taps_a_in, taps_b_in, point_a_in, point_b_in, rows_in, linear_mine, linear_other, up_mine, up_other,
+    give_0, give_1, give_2, give_3, features_o, value_o, gate_o, standard_two_o, scale_o, keep_o,
+    incoming, features_out, value_out, gate_out, standard_two_out, scale_out, keep_out, band, taps_a, taps_b, point_a, point_b, rows, linear_s, up_s, pick_s, ext_s, x_s, first_s, spread_s, even_s, odd_s, flat_s, gated_s, kept_s, sems, out_sems,
 ):
     step = pl.program_id(0)
     me = lax.axis_index("fsdp")
-    copies = fetch(
-        ((packed_mine, packed_other, packed_s), (linear_mine, linear_other, linear_s), (up_mine, up_other, up_s)), sems, me
-    )
-
-    copies.append(pltpu.make_async_copy(incoming_in, incoming, sems.at[len(copies)]))
+    copies = fetch(((linear_mine, linear_other, linear_s), (up_mine, up_other, up_s)), sems, me)
+    pairs = (
+        (incoming_in, incoming), (band_in, band), (taps_a_in, taps_a), (taps_b_in, taps_b), (point_a_in, point_a),
+        (point_b_in, point_b), (rows_in, rows),
+    )
+    small = [pltpu.make_async_copy(source, target, sems.at[4 + n]) for n, (source, target) in enumerate(pairs)]
     here = pl.ds(step * ROWS, ROWS)
     held = (features_out, value_out, gate_out, standard_two_out, scale_out, keep_out)
     saves = [
         pltpu.make_async_copy(source, out.at[here], out_sems.at[n])
         for n, (source, out) in enumerate(zip(held, (features_o, value_o, gate_o, standard_two_o, scale_o, keep_o)))
     ]
-    save_rows = pltpu.make_async_copy(rows, rows_o, out_sems.at[len(saves)])
 
     @pl.when(step == 0)
     def _():
-        for copy in copies[:2] + copies[6:]:
+        for copy in small:
             copy.start()
-        copies[0].wait()
-        copies[1].wait()
-        unpack_weights(packed_s.at[0], packed_s.at[1], band, taps_a, taps_b, point_a, point_b, rows)
-
-    @pl.when(step == 0)
-    def _():
-        copies[6].wait()
-        for copy in copies[2:6]:
+        small[0].wait()
+        for copy in copies:
             copy.start()
-        save_rows.start()
 
     sources = incoming.shape[0]
     lanes = incoming.shape[1] - 8
@@ -195,6 +190,11 @@
                 part = jnp.where(edge, 0.0, part)
             x_s[b, q * ROWS : (q + 1) * ROWS, :] = part.astype(BF)
 
+    @pl.when(step == 0)
+    def _():
+        for copy in small[1:]:
+            copy.wait()
+
     views = (3 * ROWS, 0, ROWS, 2 * ROWS, 3 * ROWS + BLOCK)
     first_s[0] = jnp.zeros(first_s.shape[1:], F32)
     for f in range(GROUP):
@@ -223,7 +223,7 @@
             odd_s[b * (GROUP // 2) + g, BLOCK:, :] = second[(2 * g + 1) * ROWS : (2 * g + 2) * ROWS]
         return carry
 
-    lax.fori_loop(0, BINS // GROUP, section, 0)
+    lax.fori_loop(0, BINS // GROUP, section, 0, unroll=2)
 
     for f in range(BINS // 4):
         total = None
@@ -239,8 +239,8 @@
 
     @pl.when(step == 0)
     def _():
-        copies[2].wait()
-        copies[3].wait()
+        copies[0].wait()
+        copies[1].wait()
 
     half = linear_s.shape[2]
     for side in range(2):
@@ -254,8 +254,8 @@
 
     @pl.when(step == 0)
     def _():
-        copies[4].wait()
-        copies[5].wait()
+        copies[2].wait()
+        copies[3].wait()
 
     row_keep = keep_out[:, 0:1]
     value = dot(normed, up_s[0])
@@ -293,10 +293,6 @@
         give[1] = kept_s[(1 - me) * (count // 2) + quarter]
     for save in saves:
         save.wait()
-
-    @pl.when(step == 0)
-    def _():
-        save_rows.wait()
 
 
 def pack_kernel(*refs):
@@ -524,6 +520,15 @@
     )(mel_panels, frames.reshape(1, slots), target.reshape(1, slots), *small)
     incoming = lax.all_to_all(outgoing, "dp", split_axis=0, concat_axis=0, tiled=True)
     packed_other = swap_cores(packed)
+    unpacked = held_call(
+        weights_kernel,
+        [
+            shape((256, GROUP * 256), BF), shape((16, 256), F32), shape((16, 256), F32), shape((256, 256), BF),
+            shape((256, 256), BF), shape((16, width), F32),
+        ],
+        [], "weights", packed, packed_other,
+    )
+    rows = unpacked[-1]
     linear_other = swap_cores(linear_weight)
     up_other = swap_cores(up_weight)
     down_other = swap_cores(down_weight)
@@ -533,14 +538,14 @@
         return pl.BlockSpec((ROWS, columns), lambda g: (g, 0))
 
     by_plane = pl.BlockSpec((members, ROWS, 128), lambda g: (0, g, 0))
-    *given, features, value, gate, standard_two, scale, keep, rows = pl.pallas_call(
+    *given, features, value, gate, standard_two, scale, keep = pl.pallas_call(
         forward_kernel,
         grid=(blocks,),
         in_specs=[
-            *[anywhere] * 7,
+            *[anywhere] * 11,
         ],
         out_specs=[
-            *[by_plane] * 4, *[anywhere] * 7,
+            *[by_plane] * 4, *[anywhere] * 6,
         ],
         out_shape=(
             *[shape((members, rows_here, 128), BF)] * 4,
@@ -550,7 +555,6 @@
             shape((rows_here, width), F32),
             shape((rows_here, 128), F32),
             shape((rows_here, 128), F32),
-            shape((16, width), F32),
         ),
         scratch_shapes=[
             pltpu.VMEM(incoming.shape, BF),
@@ -560,13 +564,12 @@
             pltpu.VMEM((ROWS, width), F32),
             pltpu.VMEM((ROWS, 128), F32),
             pltpu.VMEM((ROWS, 128), F32),
-            pltpu.VMEM((16, width), F32),
-            pltpu.VMEM((2,) + packed.shape, BF),
             pltpu.VMEM((256, GROUP * 256), BF),
             pltpu.VMEM((16, 256), F32),
             pltpu.VMEM((16, 256), F32),
             pltpu.VMEM((256, 256), BF),
             pltpu.VMEM((256, 256), BF),
+            pltpu.VMEM((16, width), F32),
             pltpu.VMEM((2,) + linear_weight.shape, BF),
             pltpu.VMEM((2,) + up_weight.shape, BF),
             pltpu.VMEM((ROWS * width_in // SPAN // 128, groups * width_in // 128), F32),
@@ -579,13 +582,13 @@
             pltpu.VMEM((ROWS, BINS // 4 * 256), BF),
             pltpu.VMEM((ROWS + 8 * BLOCK, width), F32),
             pltpu.VMEM((width // 128, ROWS, 128), BF),
-            pltpu.SemaphoreType.DMA((7,)),
-            pltpu.SemaphoreType.DMA((7,)),
+            pltpu.SemaphoreType.DMA((11,)),
+            pltpu.SemaphoreType.DMA((6,)),
         ],
         compiler_params=params(FRONT),
         cost_estimate=cost(2e10 * blocks, 1e7),
         name="forward",
-    )(incoming, packed, packed_other, linear_weight, linear_other, up_weight, up_other)
+    )(incoming, *unpacked, linear_weight, linear_other, up_weight, up_other)
     first, *cotangents[1:3] = lax.optimization_barrier((given[0], *cotangents[1:3]))
     cotangents_other = [cotangent_other] + [swap_cores(block) for block in cotangents[1:3]]
     near = [swap_rank(given[offset], offset, groups) for offset in range(1, 4)]

time: 82.6 us -> 82 us (level)
  waiting for transfers between devices: 15.3 us -> 9.61 us
  local copies, waits for them, and re-layouts: 0.73 us -> 5.85 us
    all_to_all x1, waiting for transfers between devices: 8.8 us -> 3.12 us  [local(): lax.all_to_all(outgoing, 'dp', split_axis=0, concat_axis=0, tiled=True)]
    unnamed x8 -> x20, local copies, waits for them, and re-layouts: 0.73 us -> 5.85 us
    pallas_call x5 -> x6, Pallas kernels: 2.16 us -> 2.75 us  [held_call(): pl.pallas_call(kernel, **specs, out_shape=outs, scratch_shapes=scratch, c...]
where the time goes in v7:
time: 82 us; the launch traced here: 81.7 us
  starting transfers between devices  32.9 us (40%)
  Pallas kernels  32.3 us (39%)
  waiting for transfers between devices  9.61 us (12%)
  local copies, waits for them, and re-layouts  5.85 us (7%)
  between operations  0.99 us (1%)
    ppermute x18, starting transfers between devices, swap_rank(): return lax.ppermute(block, 'dp', [(i, i ^ offset) for i in range(groups)])  22.7 us
    pallas_call x1, Pallas kernels, local(): pl.pallas_call(forward_kernel, grid=(blocks,), in_specs=[*[anywhere] * 11...  13.7 us
    pallas_call x3, Pallas kernels, back_call(): pl.pallas_call(functools.partial(bring, body, len(sources), outs), grid=(...  12.9 us
    all_to_all x1, starting transfers between devices, local(): lax.all_to_all(outgoing, 'dp', split_axis=0, concat_axis=0, tiled=True)  8.3 us
    unnamed x20, local copies, waits for them, and re-layouts  5.85 us
    ppermute x18, waiting for transfers between devices, swap_rank(): return lax.ppermute(block, 'dp', [(i, i ^ offset) for i in range(groups)])  5.4 us
    all_to_all x1, waiting for transfers between devices, local(): lax.all_to_all(outgoing, 'dp', split_axis=0, concat_axis=0, tiled=True)  3.12 us
    pallas_call x1, Pallas kernels, local(): pl.pallas_call(send_kernel, in_specs=[anywhere, held, held] + [anywhere]...  2.85 us
  transfers between devices with their start and end apart: 28, of which 7 were waited for; matrix products, arithmetic and copies ran while one was open for 0% of the time, Pallas kernels for 34%

profile of v7, /device:TPU:0, one launch (start us, length us, event | category | flops | bytes accessed | tf_op | source)
XLA Modules:
  0.0 81.7 jit_solution(6869977593878510232)
XLA Ops:
  1.2 2.8 %send.1 = (bf16[16,88,128]{2,1,0:T(8,128)(2,1)}, bf16[160,512]{1,0:T(8,128)(2,1)}) custom-call(bf16[16,10240]{1,0:T(8,128)(2,1)} %mel.1, s32[1,16]{1,0:T(1,128)} %bitcast.2, s32[1,16]{1,0:T(1,128)} %bitcast.3, bf16[9,128]{1,0:T(8,128)(2,1)} %first.1, bf16[9,128]{1,0:T(8,128)(2,1)} %depth_a.1, bf16[256,128]{1,0:T(8,128)(2,1)} %point_a.1, ...), custom_call_target="tpu_custom_call" | custom-call | flops 200000000 | bytes 1000000 | tf_op jit(solution)/shard_map/send/pallas_call | solution.py:507
  4.1 8.3 %all-to-all-start = ((bf16[16,88,128]{2,1,0:T(8,128)(2,1)}), bf16[16,88,128]{2,1,0:T(8,128)(2,1)S(1)}, u32[]{:S(2)}, u32[]{:S(2)}) async-start(bf16[16,88,128]{2,1,0:T(8,128)(2,1)} %get-tuple-element.47), calls=%async_computation | async-start | bytes 720896 | tf_op jit(solution)/shard_map/all_to_all | solution.py:521
  12.5 2.8 %collective-permute-start.7 = (bf16[128,1024]{1,0:T(8,128)(2,1)}, bf16[128,1024]{1,0:T(8,128)(2,1)S(1)}, u32[]{:S(2)}, u32[]{:S(2)}) collective-permute-start(bf16[128,1024]{1,0:T(8,128)(2,1)} %refs_5_.1), channel_id=1, source_target_pairs={{0,6},{2,4},{4,2},{6,0},{8,14},{10,12},{12,10},{14,8},{16,22},{18,... | collective-permute-start | bytes 786440 | tf_op jit(solution)/shard_map/ppermute | solution.py:464
  16.0 0.9 %copy-done.3 = bf16[160,512]{1,0:T(8,128)(2,1)S(1)} copy-done((bf16[160,512]{1,0:T(8,128)(2,1)S(1)}, bf16[160,512]{1,0:T(8,128)(2,1)}, u32[]{:S(2)}) %copy-start.3) | copy-done | bytes 163864
  18.2 1.1 %copy-done.4 = bf16[256,2560]{1,0:T(8,128)(2,1)} copy-done((bf16[256,2560]{1,0:T(8,128)(2,1)}, bf16[256,2560]{1,0:T(8,128)(2,1)S(1)}, u32[]{:S(2)}) %copy-start.4) | copy-done | bytes 1310744
  21.7 3.1 %all-to-all-done.incoming_in = bf16[16,88,128]{2,1,0:T(8,128)(2,1)S(1)} async-done(((bf16[16,88,128]{2,1,0:T(8,128)(2,1)}), bf16[16,88,128]{2,1,0:T(8,128)(2,1)S(1)}, u32[]{:S(2)}, u32[]{:S(2)}) %all-to-all-start) | async-done | bytes 360480 | tf_op jit(solution)/shard_map/all_to_all | solution.py:521
  25.6 13.7 %forward.1 = (bf16[2,128,128]{2,1,0:T(8,128)(2,1)}, bf16[2,128,128]{2,1,0:T(8,128)(2,1)}, bf16[2,128,128]{2,1,0:T(8,128)(2,1)}, bf16[2,128,128]{2,1,0:T(8,128)(2...) custom-call(bf16[16,88,128]{2,1,0:T(8,128)(2,1)} %copy-done.9, ...), custom_call_target="tpu_custom_call" | custom-call | flops 20000000000 | bytes 10000000 | tf_op jit(solution)/shard_map/forward/pallas_call | solution.py:541
  40.7 2.2 %collective-permute-start.5 = (bf16[2,128,128]{2,1,0:T(8,128)(2,1)}, bf16[2,128,128]{2,1,0:T(8,128)(2,1)S(1)}, u32[]{:S(2)}, u32[]{:S(2)}) collective-permute-start(bf16[2,128,128]{2,1,0:T(8,128)(2,1)} %get-tuple-element.57), channel_id=1, source_target_pairs={{0,6},{2,4},{4,2},{6,0},{8,14},{10,12},{12,10},{14,8},{16,22},{18,... | collective-permute-start | bytes 196616 | tf_op jit(solution)/shard_map/ppermute | solution.py:464
  43.0 3.2 %layer.1 = bf16[128,1024]{1,0:T(8,128)(2,1)} custom-call(bf16[128,1024]{1,0:T(8,128)(2,1)} %get-tuple-element.58.refs_0_.refs_2_, f32[128,1024]{1,0:T(8,128)} %get-tuple-element.59.refs_1_.refs_0_, f32[128,128]{1,0:T(8,128)} %get-tuple-element.60.refs_2_.refs_4_.refs_3_, f32[16,1024]{1,0:T(8,128)} %copy-done.1, bf16[512,1024]{1,0:T(8,128)(2,1)} %refs_7_.1, ...), custom_call_target="tpu_custom_call" | custom-call | flops 1000000 | bytes 100000 | tf_op jit(solution)/shard_map/layer/pallas_call | solution.py:598
  47.8 1.1 %collective-permute-done.10.refs_1_ = bf16[4,128,128]{2,1,0:T(8,128)(2,1)S(1)} collective-permute-done((bf16[4,128,128]{2,1,0:T(8,128)(2,1)S(1)}, bf16[4,128,128]{2,1,0:T(8,128)(2,1)S(1)}, u32[]{:S(2)}, u32[]{:S(2)}) %collective-permute-start.10) | collective-permute-done | bytes 131104 | tf_op jit(solution)/shard_map/ppermute | solution.py:460
  49.2 1.0 %collective-permute-start.15 = (bf16[32,1024]{1,0:T(8,128)(2,1)S(1)}, bf16[32,1024]{1,0:T(8,128)(2,1)S(1)}, u32[]{:S(2)}, u32[]{:S(2)}) collective-permute-start(bf16[32,1024]{1,0:T(8,128)(2,1)S(1)} %get-tuple-element.71), channel_id=1, source_target_pairs={{0,8},{2,10},{4,12},{6,14},{8,0},{10,2},{12,4},{14,6},{16,24},{18,... | collective-permute-start | bytes 196616 | tf_op jit(solution)/shard_map/ppermute | solution.py:464
  50.3 0.9 %collective-permute-start.16 = (bf16[32,1024]{1,0:T(8,128)(2,1)S(1)}, bf16[32,1024]{1,0:T(8,128)(2,1)S(1)}, u32[]{:S(2)}, u32[]{:S(2)}) collective-permute-start(bf16[32,1024]{1,0:T(8,128)(2,1)S(1)} %get-tuple-element.72), channel_id=1, source_target_pairs={{0,16},{2,18},{4,20},{6,22},{8,24},{10,26},{12,28},{14,30},{16,0},... | collective-permute-start | bytes 196616 | tf_op jit(solution)/shard_map/ppermute | solution.py:464
  51.2 2.5 %collective-permute-start.17 = (bf16[32,1024]{1,0:T(8,128)(2,1)S(1)}, bf16[32,1024]{1,0:T(8,128)(2,1)S(1)}, u32[]{:S(2)}, u32[]{:S(2)}) collective-permute-start(bf16[32,1024]{1,0:T(8,128)(2,1)S(1)} %get-tuple-element.73), channel_id=1, source_target_pairs={{0,24},{2,26},{4,28},{6,30},{8,16},{10,18},{12,20},{14,22},{16,8},... | collective-permute-start | bytes 196616 | tf_op jit(solution)/shard_map/ppermute | solution.py:464
  53.7 4.5 %depth.1 = (bf16[128,1024]{1,0:T(8,128)(2,1)}, bf16[128,1024]{1,0:T(8,128)(2,1)}) custom-call(f32[128,1024]{1,0:T(8,128)} %get-tuple-element.59.refs_1_.refs_0_, f32[128,1024]{1,0:T(8,128)} %get-tuple-element.74.refs_1_, f32[128,1024]{1,0:T(8,128)} %get-tuple-element.75.refs_2_, f32[128,128]{1,0:T(8,128)} %get-tuple-element.76.refs_3_, ...), custom_call_target="tpu_custom_call" | custom-call | flops 1000000 | bytes 100000 | tf_op jit(solution)/shard_map/depth/pallas_call | solution.py:598
  58.7 1.4 %collective-permute-start.18 = (bf16[32,1024]{1,0:T(8,128)(2,1)S(1)}, bf16[32,1024]{1,0:T(8,128)(2,1)S(1)}, u32[]{:S(2)}, u32[]{:S(2)}) collective-permute-start(bf16[32,1024]{1,0:T(8,128)(2,1)S(1)} %multiply_convert_fusion.refs_0_), channel_id=1, source_target_pairs={{0,8},{2,10},{4,12},{6,14},{8,0},{10,2},{12,4},{14,6},{16,24},{18,... | collective-permute-start | bytes 196616 | tf_op jit(solution)/shard_map/ppermute | solution.py:464
  60.5 2.6 %collective-permute-start.20 = (bf16[32,1024]{1,0:T(8,128)(2,1)S(1)}, bf16[32,1024]{1,0:T(8,128)(2,1)S(1)}, u32[]{:S(2)}, u32[]{:S(2)}) collective-permute-start(bf16[32,1024]{1,0:T(8,128)(2,1)S(1)} %multiply_convert_fusion.refs_0_), channel_id=1, source_target_pairs={{0,24},{2,26},{4,28},{6,30},{8,16},{10,18},{12,20},{14,22},{16,8},... | collective-permute-start | bytes 196616 | tf_op jit(solution)/shard_map/ppermute | solution.py:464
  63.1 5.2 %up.1 = bf16[128,1024]{1,0:T(8,128)(2,1)} custom-call(bf16[128,1024]{1,0:T(8,128)(2,1)} %get-tuple-element.82.refs_0_, bf16[128,1024]{1,0:T(8,128)(2,1)} %get-tuple-element.83.refs_1_, bf16[128,1024]{1,0:T(8,128)(2,1)} %get-tuple-element.58.refs_0_.refs_2_, f32[128,128]{1,0:T(8,128)} %get-tuple-element.60.refs_2_.refs_4_.refs_3_, f32[16,1024]{1,0:T(8,128)} %copy-done.1, ...), custom_call_target="tpu_custom_call" | custom-call | flops 1000000 | bytes 100000 | tf_op jit(solution)/shard_map/up/pallas_call | solution.py:598
  69.2 0.9 %collective-permute-start.25 = (bf16[128,512]{1,0:T(8,128)(2,1)S(1)}, bf16[128,512]{1,0:T(8,128)(2,1)S(1)}, u32[]{:S(2)}, u32[]{:S(2)}) collective-permute-start(bf16[128,512]{1,0:T(8,128)(2,1)S(1)} %get-tuple-element.90.refs_4_), channel_id=1, source_target_pairs={{0,4},{2,6},{4,0},{6,2},{8,12},{10,14},{12,8},{14,10},{16,20},{18,... | collective-permute-start | bytes 393224 | tf_op jit(solution)/shard_map/ppermute | solution.py:464
  70.2 1.1 %collective-permute-start.22 = (bf16[128,512]{1,0:T(8,128)(2,1)S(1)}, bf16[128,512]{1,0:T(8,128)(2,1)S(1)}, u32[]{:S(2)}, u32[]{:S(2)}) collective-permute-start(bf16[128,512]{1,0:T(8,128)(2,1)S(1)} %get-tuple-element.89.refs_0_), channel_id=1, source_target_pairs={{0,4},{2,6},{4,0},{6,2},{8,12},{10,14},{12,8},{14,10},{16,20},{18,... | collective-permute-start | bytes 393224 | tf_op jit(solution)/shard_map/ppermute | solution.py:464
  71.3 1.3 %collective-permute-start.24 = (bf16[128,512]{1,0:T(8,128)(2,1)S(1)}, bf16[128,512]{1,0:T(8,128)(2,1)S(1)}, u32[]{:S(2)}, u32[]{:S(2)}) collective-permute-start(bf16[128,512]{1,0:T(8,128)(2,1)S(1)} %get-tuple-element.90.refs_4_), channel_id=1, source_target_pairs={{0,2},{2,0},{4,6},{6,4},{8,10},{10,8},{12,14},{14,12},{16,18},{18,... | collective-permute-start | bytes 393224 | tf_op jit(solution)/shard_map/ppermute | solution.py:464
  72.6 1.7 %collective-permute-done.21.refs_1_ = bf16[128,512]{1,0:T(8,128)(2,1)S(1)} collective-permute-done((bf16[128,512]{1,0:T(8,128)(2,1)S(1)}, bf16[128,512]{1,0:T(8,128)(2,1)S(1)}, u32[]{:S(2)}, u32[]{:S(2)}) %collective-permute-start.21) | collective-permute-done | bytes 131104 | tf_op jit(solution)/shard_map/ppermute | solution.py:464
  75.1 1.8 %collective-permute-start.26 = (bf16[128,512]{1,0:T(8,128)(2,1)S(1)}, bf16[128,512]{1,0:T(8,128)(2,1)S(1)}, u32[]{:S(2)}, u32[]{:S(2)}) collective-permute-start(bf16[128,512]{1,0:T(8,128)(2,1)S(1)} %collective-permute-done.25.refs_6_), channel_id=1, source_target_pairs={{0,2},{2,0},{4,6},{6,4},{8,10},{10,8},{12,14},{14,12},{16,18},{18,... | collective-permute-start | bytes 393224 | tf_op jit(solution)/shard_map/ppermute | solution.py:464
  77.0 2.3 %collective-permute-done.23.refs_3_ = bf16[128,512]{1,0:T(8,128)(2,1)S(1)} collective-permute-done((bf16[128,512]{1,0:T(8,128)(2,1)S(1)}, bf16[128,512]{1,0:T(8,128)(2,1)S(1)}, u32[]{:S(2)}, u32[]{:S(2)}) %collective-permute-start.23) | collective-permute-done | bytes 131104 | tf_op jit(solution)/shard_map/ppermute | solution.py:464
  80.1 1.4 %finish.1 = f32[512,1024]{1,0:T(8,128)} custom-call(bf16[128,512]{1,0:T(8,128)(2,1)S(1)} %get-tuple-element.89.refs_0_, bf16[128,512]{1,0:T(8,128)(2,1)S(1)} %collective-permute-done.21.refs_1_, bf16[128,512]{1,0:T(8,128)(2,1)S(1)} %collective-permute-done.22.refs_2_, bf16[128,512]{1,0:T(8,128)(2,1)S(1)} %collective-permute-done.23.refs_3_, ...), custom_call_target="tpu_custom_call" | custom-call | flops 1000000 | bytes 100000 | tf_op jit(solution)/shard_map/finish/pallas_call | solution.py:468
  (64 shorter events, 12.5 us)
Async XLA Ops:
  0.6 24.2 %collective-permute-start.1 = (bf16[2560,512]{1,0:T(8,128)(2,1)}, bf16[2560,512]{1,0:T(8,128)(2,1)}, u32[]{:S(2)}, u32[]{:S(2)}) collective-permute-start(bf16[2560,512]{1,0:T(8,128)(2,1)} %linear_mine.1), channel_id=1, source_target_pairs={{0,1},{1,0},{2,3},{3,2},{4,5},{5,4},{6,7},{7,6},{8,9},{9,8},{10,11... | collective-permute-start | bytes 7864328 | tf_op jit(solution)/shard_map/ppermute | solution.py:460
  1.2 20.6 %collective-permute-start.2 = (bf16[1024,1024]{1,0:T(8,128)(2,1)}, bf16[1024,1024]{1,0:T(8,128)(2,1)}, u32[]{:S(2)}, u32[]{:S(2)}) collective-permute-start(bf16[1024,1024]{1,0:T(8,128)(2,1)} %refs_6_.3), channel_id=1, source_target_pairs={{0,1},{1,0},{2,3},{3,2},{4,5},{5,4},{6,7},{7,6},{8,9},{9,8},{10,11... | collective-permute-start | bytes 6291464 | tf_op jit(solution)/shard_map/ppermute | solution.py:460
  4.1 20.8 %all-to-all-start = ((bf16[16,88,128]{2,1,0:T(8,128)(2,1)}), bf16[16,88,128]{2,1,0:T(8,128)(2,1)S(1)}, u32[]{:S(2)}, u32[]{:S(2)}) async-start(bf16[16,88,128]{2,1,0:T(8,128)(2,1)} %get-tuple-element.47), calls=%async_computation | async-start | bytes 720896 | tf_op jit(solution)/shard_map/all_to_all | solution.py:521
  12.4 3.5 %collective-permute-start = (bf16[160,512]{1,0:T(8,128)(2,1)}, bf16[160,512]{1,0:T(8,128)(2,1)S(1)}, u32[]{:S(2)}, u32[]{:S(2)}) collective-permute-start(bf16[160,512]{1,0:T(8,128)(2,1)} %get-tuple-element.48.mine), channel_id=1, source_target_pairs={{0,1},{1,0},{2,3},{3,2},{4,5},{5,4},{6,7},{7,6},{8,9},{9,8},{10,11... | collective-permute-start | bytes 491528 | tf_op jit(solution)/shard_map/ppermute | solution.py:460
  12.5 33.7 %collective-permute-start.7 = (bf16[128,1024]{1,0:T(8,128)(2,1)}, bf16[128,1024]{1,0:T(8,128)(2,1)S(1)}, u32[]{:S(2)}, u32[]{:S(2)}) collective-permute-start(bf16[128,1024]{1,0:T(8,128)(2,1)} %refs_5_.1), channel_id=1, source_target_pairs={{0,6},{2,4},{4,2},{6,0},{8,14},{10,12},{12,10},{14,8},{16,22},{18,... | collective-permute-start | bytes 786440 | tf_op jit(solution)/shard_map/ppermute | solution.py:464
  15.3 24.9 %collective-permute-start.8 = (bf16[128,1024]{1,0:T(8,128)(2,1)}, bf16[128,1024]{1,0:T(8,128)(2,1)S(1)}, u32[]{:S(2)}, u32[]{:S(2)}) collective-permute-start(bf16[128,1024]{1,0:T(8,128)(2,1)} %refs_5_.1), channel_id=1, source_target_pairs={{0,2},{2,0},{4,6},{6,4},{8,10},{10,8},{12,14},{14,12},{16,18},{18,... | collective-permute-start | bytes 786440 | tf_op jit(solution)/shard_map/ppermute | solution.py:464
  15.9 24.8 %collective-permute-start.9 = (bf16[128,1024]{1,0:T(8,128)(2,1)}, bf16[128,1024]{1,0:T(8,128)(2,1)S(1)}, u32[]{:S(2)}, u32[]{:S(2)}) collective-permute-start(bf16[128,1024]{1,0:T(8,128)(2,1)} %refs_5_.1), channel_id=1, source_target_pairs={{0,4},{2,6},{4,0},{6,2},{8,12},{10,14},{12,8},{14,10},{16,20},{18,... | collective-permute-start | bytes 786440 | tf_op jit(solution)/shard_map/ppermute | solution.py:464
  21.7 21.2 %collective-permute-start.6 = (bf16[512,1024]{1,0:T(8,128)(2,1)}, bf16[512,1024]{1,0:T(8,128)(2,1)}, u32[]{:S(2)}, u32[]{:S(2)}) collective-permute-start(bf16[512,1024]{1,0:T(8,128)(2,1)} %refs_7_.1), channel_id=1, source_target_pairs={{0,1},{1,0},{2,3},{3,2},{4,5},{5,4},{6,7},{7,6},{8,9},{9,8},{10,11... | collective-permute-start | bytes 3145736 | tf_op jit(solution)/shard_map/ppermute | solution.py:460
  39.4 7.4 %collective-permute-start.3 = (bf16[2,128,128]{2,1,0:T(8,128)(2,1)}, bf16[2,128,128]{2,1,0:T(8,128)(2,1)S(1)}, u32[]{:S(2)}, u32[]{:S(2)}) collective-permute-start(bf16[2,128,128]{2,1,0:T(8,128)(2,1)} %get-tuple-element.55), channel_id=1, source_target_pairs={{0,2},{2,0},{4,6},{6,4},{8,10},{10,8},{12,14},{14,12},{16,18},{18,... | collective-permute-start | bytes 196616 | tf_op jit(solution)/shard_map/ppermute | solution.py:464
  40.2 6.7 %collective-permute-start.4 = (bf16[2,128,128]{2,1,0:T(8,128)(2,1)}, bf16[2,128,128]{2,1,0:T(8,128)(2,1)S(1)}, u32[]{:S(2)}, u32[]{:S(2)}) collective-permute-start(bf16[2,128,128]{2,1,0:T(8,128)(2,1)} %get-tuple-element.56), channel_id=1, source_target_pairs={{0,4},{2,6},{4,0},{6,2},{8,12},{10,14},{12,8},{14,10},{16,20},{18,... | collective-permute-start | bytes 196616 | tf_op jit(solution)/shard_map/ppermute | solution.py:464
  40.7 6.1 %collective-permute-start.5 = (bf16[2,128,128]{2,1,0:T(8,128)(2,1)}, bf16[2,128,128]{2,1,0:T(8,128)(2,1)S(1)}, u32[]{:S(2)}, u32[]{:S(2)}) collective-permute-start(bf16[2,128,128]{2,1,0:T(8,128)(2,1)} %get-tuple-element.57), channel_id=1, source_target_pairs={{0,6},{2,4},{4,2},{6,0},{8,14},{10,12},{12,10},{14,8},{16,22},{18,... | collective-permute-start | bytes 196616 | tf_op jit(solution)/shard_map/ppermute | solution.py:464
  42.9 4.8 %collective-permute-start.11 = (bf16[128,1024]{1,0:T(8,128)(2,1)S(1)}, bf16[128,1024]{1,0:T(8,128)(2,1)S(1)}, u32[]{:S(2)}, u32[]{:S(2)}) collective-permute-start(bf16[128,1024]{1,0:T(8,128)(2,1)S(1)} %copy-done), channel_id=1, source_target_pairs={{0,1},{1,0},{2,3},{3,2},{4,5},{5,4},{6,7},{7,6},{8,9},{9,8},{10,11... | collective-permute-start | bytes 786440 | tf_op jit(solution)/shard_map/ppermute | solution.py:460
  49.2 9.0 %collective-permute-start.15 = (bf16[32,1024]{1,0:T(8,128)(2,1)S(1)}, bf16[32,1024]{1,0:T(8,128)(2,1)S(1)}, u32[]{:S(2)}, u32[]{:S(2)}) collective-permute-start(bf16[32,1024]{1,0:T(8,128)(2,1)S(1)} %get-tuple-element.71), channel_id=1, source_target_pairs={{0,8},{2,10},{4,12},{6,14},{8,0},{10,2},{12,4},{14,6},{16,24},{18,... | collective-permute-start | bytes 196616 | tf_op jit(solution)/shard_map/ppermute | solution.py:464
  50.3 8.4 %collective-permute-start.16 = (bf16[32,1024]{1,0:T(8,128)(2,1)S(1)}, bf16[32,1024]{1,0:T(8,128)(2,1)S(1)}, u32[]{:S(2)}, u32[]{:S(2)}) collective-permute-start(bf16[32,1024]{1,0:T(8,128)(2,1)S(1)} %get-tuple-element.72), channel_id=1, source_target_pairs={{0,16},{2,18},{4,20},{6,22},{8,24},{10,26},{12,28},{14,30},{16,0},... | collective-permute-start | bytes 196616 | tf_op jit(solution)/shard_map/ppermute | solution.py:464
  51.2 7.5 %collective-permute-start.17 = (bf16[32,1024]{1,0:T(8,128)(2,1)S(1)}, bf16[32,1024]{1,0:T(8,128)(2,1)S(1)}, u32[]{:S(2)}, u32[]{:S(2)}) collective-permute-start(bf16[32,1024]{1,0:T(8,128)(2,1)S(1)} %get-tuple-element.73), channel_id=1, source_target_pairs={{0,24},{2,26},{4,28},{6,30},{8,16},{10,18},{12,20},{14,22},{16,8},... | collective-permute-start | bytes 196616 | tf_op jit(solution)/shard_map/ppermute | solution.py:464
  58.7 9.7 %collective-permute-start.18 = (bf16[32,1024]{1,0:T(8,128)(2,1)S(1)}, bf16[32,1024]{1,0:T(8,128)(2,1)S(1)}, u32[]{:S(2)}, u32[]{:S(2)}) collective-permute-start(bf16[32,1024]{1,0:T(8,128)(2,1)S(1)} %multiply_convert_fusion.refs_0_), channel_id=1, source_target_pairs={{0,8},{2,10},{4,12},{6,14},{8,0},{10,2},{12,4},{14,6},{16,24},{18,... | collective-permute-start | bytes 196616 | tf_op jit(solution)/shard_map/ppermute | solution.py:464
  60.1 8.3 %collective-permute-start.19 = (bf16[32,1024]{1,0:T(8,128)(2,1)S(1)}, bf16[32,1024]{1,0:T(8,128)(2,1)S(1)}, u32[]{:S(2)}, u32[]{:S(2)}) collective-permute-start(bf16[32,1024]{1,0:T(8,128)(2,1)S(1)} %multiply_convert_fusion.refs_0_), channel_id=1, source_target_pairs={{0,16},{2,18},{4,20},{6,22},{8,24},{10,26},{12,28},{14,30},{16,0},... | collective-permute-start | bytes 196616 | tf_op jit(solution)/shard_map/ppermute | solution.py:464
  60.5 7.9 %collective-permute-start.20 = (bf16[32,1024]{1,0:T(8,128)(2,1)S(1)}, bf16[32,1024]{1,0:T(8,128)(2,1)S(1)}, u32[]{:S(2)}, u32[]{:S(2)}) collective-permute-start(bf16[32,1024]{1,0:T(8,128)(2,1)S(1)} %multiply_convert_fusion.refs_0_), channel_id=1, source_target_pairs={{0,24},{2,26},{4,28},{6,30},{8,16},{10,18},{12,20},{14,22},{16,8},... | collective-permute-start | bytes 196616 | tf_op jit(solution)/shard_map/ppermute | solution.py:464
  68.5 5.9 %collective-permute-start.21 = (bf16[128,512]{1,0:T(8,128)(2,1)S(1)}, bf16[128,512]{1,0:T(8,128)(2,1)S(1)}, u32[]{:S(2)}, u32[]{:S(2)}) collective-permute-start(bf16[128,512]{1,0:T(8,128)(2,1)S(1)} %get-tuple-element.89.refs_0_), channel_id=1, source_target_pairs={{0,2},{2,0},{4,6},{6,4},{8,10},{10,8},{12,14},{14,12},{16,18},{18,... | collective-permute-start | bytes 393224 | tf_op jit(solution)/shard_map/ppermute | solution.py:464
  69.2 5.9 %collective-permute-start.25 = (bf16[128,512]{1,0:T(8,128)(2,1)S(1)}, bf16[128,512]{1,0:T(8,128)(2,1)S(1)}, u32[]{:S(2)}, u32[]{:S(2)}) collective-permute-start(bf16[128,512]{1,0:T(8,128)(2,1)S(1)} %get-tuple-element.90.refs_4_), channel_id=1, source_target_pairs={{0,4},{2,6},{4,0},{6,2},{8,12},{10,14},{12,8},{14,10},{16,20},{18,... | collective-permute-start | bytes 393224 | tf_op jit(solution)/shard_map/ppermute | solution.py:464
  70.2 6.8 %collective-permute-start.22 = (bf16[128,512]{1,0:T(8,128)(2,1)S(1)}, bf16[128,512]{1,0:T(8,128)(2,1)S(1)}, u32[]{:S(2)}, u32[]{:S(2)}) collective-permute-start(bf16[128,512]{1,0:T(8,128)(2,1)S(1)} %get-tuple-element.89.refs_0_), channel_id=1, source_target_pairs={{0,4},{2,6},{4,0},{6,2},{8,12},{10,14},{12,8},{14,10},{16,20},{18,... | collective-permute-start | bytes 393224 | tf_op jit(solution)/shard_map/ppermute | solution.py:464
  71.3 5.8 %collective-permute-start.24 = (bf16[128,512]{1,0:T(8,128)(2,1)S(1)}, bf16[128,512]{1,0:T(8,128)(2,1)S(1)}, u32[]{:S(2)}, u32[]{:S(2)}) collective-permute-start(bf16[128,512]{1,0:T(8,128)(2,1)S(1)} %get-tuple-element.90.refs_4_), channel_id=1, source_target_pairs={{0,2},{2,0},{4,6},{6,4},{8,10},{10,8},{12,14},{14,12},{16,18},{18,... | collective-permute-start | bytes 393224 | tf_op jit(solution)/shard_map/ppermute | solution.py:464
  74.4 5.0 %collective-permute-start.23 = (bf16[128,512]{1,0:T(8,128)(2,1)S(1)}, bf16[128,512]{1,0:T(8,128)(2,1)S(1)}, u32[]{:S(2)}, u32[]{:S(2)}) collective-permute-start(bf16[128,512]{1,0:T(8,128)(2,1)S(1)} %collective-permute-done.21.refs_1_), channel_id=1, source_target_pairs={{0,4},{2,6},{4,0},{6,2},{8,12},{10,14},{12,8},{14,10},{16,20},{18,... | collective-permute-start | bytes 393224 | tf_op jit(solution)/shard_map/ppermute | solution.py:464
  75.1 5.0 %collective-permute-start.26 = (bf16[128,512]{1,0:T(8,128)(2,1)S(1)}, bf16[128,512]{1,0:T(8,128)(2,1)S(1)}, u32[]{:S(2)}, u32[]{:S(2)}) collective-permute-start(bf16[128,512]{1,0:T(8,128)(2,1)S(1)} %collective-permute-done.25.refs_6_), channel_id=1, source_target_pairs={{0,2},{2,0},{4,6},{6,4},{8,10},{10,8},{12,14},{14,12},{16,18},{18,... | collective-permute-start | bytes 393224 | tf_op jit(solution)/shard_map/ppermute | solution.py:464
  (14 other events, 39.4 us)

commit v8 on v7

--- a/solution.py
+++ b/solution.py
@@ -330,16 +330,16 @@
     right[...] = total[:, half:].astype(BF)
 
 
-def finish_kernel(*refs):
-    pieces, out, held, sems = refs[0:8], refs[8], refs[9], refs[10]
+def finish_kernel(places, *refs):
+    pieces, out, held, sems = refs[: len(places)], refs[-3], refs[-2], refs[-1]
     plane = lax.axis_index("dp") % 4
     size, half = pieces[0].shape
     copies = []
-    for n, piece in enumerate(pieces):
-        side = slice(n // 4 * half, (n // 4 + 1) * half)
+    for n, (piece, (offset, side)) in enumerate(zip(pieces, places)):
         held[n] = piece[...].astype(F32)
-        at = pl.multiple_of((plane ^ (n % 4)) * size, size)
-        copies.append(pltpu.make_async_copy(held.at[n], out.at[pl.ds(at, size), side], sems.at[n]))
+        at = pl.multiple_of((plane ^ offset) * size, size)
+        columns = slice(side * half, (side + 1) * half)
+        copies.append(pltpu.make_async_copy(held.at[n], out.at[pl.ds(at, size), columns], sems.at[n]))
         copies[-1].start()
     for copy in copies:
         copy.wait()
@@ -648,10 +648,18 @@
     left_x, right_y = swap_rank(left, 1, groups), swap_rank(right, 2, groups)
     left_y, right_x = swap_rank(left, 2, groups), swap_rank(right, 1, groups)
     left_xy, right_xy = swap_rank(left_x, 2, groups), swap_rank(right_y, 1, groups)
-    grad_down = held_call(
-        finish_kernel, shape((half, width), F32),
-        [pltpu.VMEM((8, block, width // 2), F32), pltpu.SemaphoreType.DMA((8,))], "finish",
-        left, left_x, left_y, left_xy, right, right_x, right_y, right_xy, out_specs=anywhere,
+    def finish(places, *operands, **specs):
+        return held_call(
+            functools.partial(finish_kernel, places), shape((half, width), F32),
+            [pltpu.VMEM((len(places), block, width // 2), F32), pltpu.SemaphoreType.DMA((len(places),))], "finish",
+            *operands, out_specs=anywhere, **specs,
+        )
+
+    places = ((0, 0), (0, 1), (1, 0), (1, 1), (2, 0), (2, 1))
+    grad_down = finish(places, left, right, left_x, right_x, left_y, right_y)
+    grad_down = finish(
+        ((3, 0), (3, 1)), left_xy, right_xy, grad_down,
+        in_specs=[pl.BlockSpec(memory_space=pltpu.VMEM)] * 2 + [anywhere], input_output_aliases={2: 0},
     )
     return (layer_out, grad_input, grad_down)
 

time: 82 us -> 81.7 us (level)
    pallas_call x6 -> x7, Pallas kernels: 2.75 us -> 3.38 us  [held_call(): pl.pallas_call(kernel, **specs, out_shape=outs, scratch_shapes=scratch, c...]
  transfers between devices with their start and end apart: 28 -> 28, of which waited for: 7 -> 8; matrix products, arithmetic and copies ran while one was open for 0% -> 0% of each run, Pallas kernels for 34% -> 35%
where the time goes in v8:
time: 81.7 us; the launch traced here: 81.3 us
  Pallas kernels  32.9 us (40%)
  starting transfers between devices  32.7 us (40%)
  waiting for transfers between devices  8.85 us (11%)
  local copies, waits for them, and re-layouts  5.85 us (7%)
  between operations  1 us (1%)
    ppermute x18, starting transfers between devices, swap_rank(): return lax.ppermute(block, 'dp', [(i, i ^ offset) for i in range(groups)])  22.5 us
    pallas_call x1, Pallas kernels, local(): pl.pallas_call(forward_kernel, grid=(blocks,), in_specs=[*[anywhere] * 11...  13.7 us
    pallas_call x3, Pallas kernels, back_call(): pl.pallas_call(functools.partial(bring, body, len(sources), outs), grid=(...  12.9 us
    all_to_all x1, starting transfers between devices, local(): lax.all_to_all(outgoing, 'dp', split_axis=0, concat_axis=0, tiled=True)  8.3 us
    unnamed x20, local copies, waits for them, and re-layouts  5.85 us
    ppermute x18, waiting for transfers between devices, swap_rank(): return lax.ppermute(block, 'dp', [(i, i ^ offset) for i in range(groups)])  4.64 us
    pallas_call x7, Pallas kernels, held_call(): pl.pallas_call(kernel, **specs, out_shape=outs, scratch_shapes=scratch, c...  3.38 us
    all_to_all x1, waiting for transfers between devices, local(): lax.all_to_all(outgoing, 'dp', split_axis=0, concat_axis=0, tiled=True)  3.12 us
  transfers between devices with their start and end apart: 28, of which 8 were waited for; matrix products, arithmetic and copies ran while one was open for 0% of the time, Pallas kernels for 35%

profile of v8, /device:TPU:0, one launch (start us, length us, event | category | flops | bytes accessed | tf_op | source)
XLA Modules:
  0.0 81.3 jit_solution(17838226217085032781)
XLA Ops:
  1.2 2.8 %send.1 = (bf16[16,88,128]{2,1,0:T(8,128)(2,1)}, bf16[160,512]{1,0:T(8,128)(2,1)}) custom-call(bf16[16,10240]{1,0:T(8,128)(2,1)} %mel.1, s32[1,16]{1,0:T(1,128)} %bitcast.2, s32[1,16]{1,0:T(1,128)} %bitcast.3, bf16[9,128]{1,0:T(8,128)(2,1)} %first.1, bf16[9,128]{1,0:T(8,128)(2,1)} %depth_a.1, bf16[256,128]{1,0:T(8,128)(2,1)} %point_a.1, ...), custom_call_target="tpu_custom_call" | custom-call | flops 200000000 | bytes 1000000 | tf_op jit(solution)/shard_map/send/pallas_call | solution.py:507
  4.1 8.3 %all-to-all-start = ((bf16[16,88,128]{2,1,0:T(8,128)(2,1)}), bf16[16,88,128]{2,1,0:T(8,128)(2,1)S(1)}, u32[]{:S(2)}, u32[]{:S(2)}) async-start(bf16[16,88,128]{2,1,0:T(8,128)(2,1)} %get-tuple-element.47), calls=%async_computation | async-start | bytes 720896 | tf_op jit(solution)/shard_map/all_to_all | solution.py:521
  12.5 2.8 %collective-permute-start.7 = (bf16[128,1024]{1,0:T(8,128)(2,1)}, bf16[128,1024]{1,0:T(8,128)(2,1)S(1)}, u32[]{:S(2)}, u32[]{:S(2)}) collective-permute-start(bf16[128,1024]{1,0:T(8,128)(2,1)} %refs_5_.1), channel_id=1, source_target_pairs={{0,6},{2,4},{4,2},{6,0},{8,14},{10,12},{12,10},{14,8},{16,22},{18,... | collective-permute-start | bytes 786440 | tf_op jit(solution)/shard_map/ppermute | solution.py:464
  16.0 0.9 %copy-done.3 = bf16[160,512]{1,0:T(8,128)(2,1)S(1)} copy-done((bf16[160,512]{1,0:T(8,128)(2,1)S(1)}, bf16[160,512]{1,0:T(8,128)(2,1)}, u32[]{:S(2)}) %copy-start.3) | copy-done | bytes 163864
  18.2 1.1 %copy-done.4 = bf16[256,2560]{1,0:T(8,128)(2,1)} copy-done((bf16[256,2560]{1,0:T(8,128)(2,1)}, bf16[256,2560]{1,0:T(8,128)(2,1)S(1)}, u32[]{:S(2)}) %copy-start.4) | copy-done | bytes 1310744
  21.7 3.1 %all-to-all-done.incoming_in = bf16[16,88,128]{2,1,0:T(8,128)(2,1)S(1)} async-done(((bf16[16,88,128]{2,1,0:T(8,128)(2,1)}), bf16[16,88,128]{2,1,0:T(8,128)(2,1)S(1)}, u32[]{:S(2)}, u32[]{:S(2)}) %all-to-all-start) | async-done | bytes 360480 | tf_op jit(solution)/shard_map/all_to_all | solution.py:521
  25.6 13.7 %forward.1 = (bf16[2,128,128]{2,1,0:T(8,128)(2,1)}, bf16[2,128,128]{2,1,0:T(8,128)(2,1)}, bf16[2,128,128]{2,1,0:T(8,128)(2,1)}, bf16[2,128,128]{2,1,0:T(8,128)(2...) custom-call(bf16[16,88,128]{2,1,0:T(8,128)(2,1)} %copy-done.9, ...), custom_call_target="tpu_custom_call" | custom-call | flops 20000000000 | bytes 10000000 | tf_op jit(solution)/shard_map/forward/pallas_call | solution.py:541
  40.7 2.2 %collective-permute-start.5 = (bf16[2,128,128]{2,1,0:T(8,128)(2,1)}, bf16[2,128,128]{2,1,0:T(8,128)(2,1)S(1)}, u32[]{:S(2)}, u32[]{:S(2)}) collective-permute-start(bf16[2,128,128]{2,1,0:T(8,128)(2,1)} %get-tuple-element.57), channel_id=1, source_target_pairs={{0,6},{2,4},{4,2},{6,0},{8,14},{10,12},{12,10},{14,8},{16,22},{18,... | collective-permute-start | bytes 196616 | tf_op jit(solution)/shard_map/ppermute | solution.py:464
  43.0 3.2 %layer.1 = bf16[128,1024]{1,0:T(8,128)(2,1)} custom-call(bf16[128,1024]{1,0:T(8,128)(2,1)} %get-tuple-element.58.refs_0_.refs_2_, f32[128,1024]{1,0:T(8,128)} %get-tuple-element.59.refs_1_.refs_0_, f32[128,128]{1,0:T(8,128)} %get-tuple-element.60.refs_2_.refs_4_.refs_3_, f32[16,1024]{1,0:T(8,128)} %copy-done.1, bf16[512,1024]{1,0:T(8,128)(2,1)} %refs_7_.1, ...), custom_call_target="tpu_custom_call" | custom-call | flops 1000000 | bytes 100000 | tf_op jit(solution)/shard_map/layer/pallas_call | solution.py:598
  47.8 1.1 %collective-permute-done.10.refs_1_ = bf16[4,128,128]{2,1,0:T(8,128)(2,1)S(1)} collective-permute-done((bf16[4,128,128]{2,1,0:T(8,128)(2,1)S(1)}, bf16[4,128,128]{2,1,0:T(8,128)(2,1)S(1)}, u32[]{:S(2)}, u32[]{:S(2)}) %collective-permute-start.10) | collective-permute-done | bytes 131104 | tf_op jit(solution)/shard_map/ppermute | solution.py:460
  49.2 1.0 %collective-permute-start.15 = (bf16[32,1024]{1,0:T(8,128)(2,1)S(1)}, bf16[32,1024]{1,0:T(8,128)(2,1)S(1)}, u32[]{:S(2)}, u32[]{:S(2)}) collective-permute-start(bf16[32,1024]{1,0:T(8,128)(2,1)S(1)} %get-tuple-element.71), channel_id=1, source_target_pairs={{0,8},{2,10},{4,12},{6,14},{8,0},{10,2},{12,4},{14,6},{16,24},{18,... | collective-permute-start | bytes 196616 | tf_op jit(solution)/shard_map/ppermute | solution.py:464
  50.3 0.9 %collective-permute-start.16 = (bf16[32,1024]{1,0:T(8,128)(2,1)S(1)}, bf16[32,1024]{1,0:T(8,128)(2,1)S(1)}, u32[]{:S(2)}, u32[]{:S(2)}) collective-permute-start(bf16[32,1024]{1,0:T(8,128)(2,1)S(1)} %get-tuple-element.72), channel_id=1, source_target_pairs={{0,16},{2,18},{4,20},{6,22},{8,24},{10,26},{12,28},{14,30},{16,0},... | collective-permute-start | bytes 196616 | tf_op jit(solution)/shard_map/ppermute | solution.py:464
  51.2 2.5 %collective-permute-start.17 = (bf16[32,1024]{1,0:T(8,128)(2,1)S(1)}, bf16[32,1024]{1,0:T(8,128)(2,1)S(1)}, u32[]{:S(2)}, u32[]{:S(2)}) collective-permute-start(bf16[32,1024]{1,0:T(8,128)(2,1)S(1)} %get-tuple-element.73), channel_id=1, source_target_pairs={{0,24},{2,26},{4,28},{6,30},{8,16},{10,18},{12,20},{14,22},{16,8},... | collective-permute-start | bytes 196616 | tf_op jit(solution)/shard_map/ppermute | solution.py:464
  53.7 4.5 %depth.1 = (bf16[128,1024]{1,0:T(8,128)(2,1)}, bf16[128,1024]{1,0:T(8,128)(2,1)}) custom-call(f32[128,1024]{1,0:T(8,128)} %get-tuple-element.59.refs_1_.refs_0_, f32[128,1024]{1,0:T(8,128)} %get-tuple-element.74.refs_1_, f32[128,1024]{1,0:T(8,128)} %get-tuple-element.75.refs_2_, f32[128,128]{1,0:T(8,128)} %get-tuple-element.76.refs_3_, ...), custom_call_target="tpu_custom_call" | custom-call | flops 1000000 | bytes 100000 | tf_op jit(solution)/shard_map/depth/pallas_call | solution.py:598
  58.7 1.4 %collective-permute-start.18 = (bf16[32,1024]{1,0:T(8,128)(2,1)S(1)}, bf16[32,1024]{1,0:T(8,128)(2,1)S(1)}, u32[]{:S(2)}, u32[]{:S(2)}) collective-permute-start(bf16[32,1024]{1,0:T(8,128)(2,1)S(1)} %multiply_convert_fusion.refs_0_), channel_id=1, source_target_pairs={{0,8},{2,10},{4,12},{6,14},{8,0},{10,2},{12,4},{14,6},{16,24},{18,... | collective-permute-start | bytes 196616 | tf_op jit(solution)/shard_map/ppermute | solution.py:464
  60.5 2.6 %collective-permute-start.20 = (bf16[32,1024]{1,0:T(8,128)(2,1)S(1)}, bf16[32,1024]{1,0:T(8,128)(2,1)S(1)}, u32[]{:S(2)}, u32[]{:S(2)}) collective-permute-start(bf16[32,1024]{1,0:T(8,128)(2,1)S(1)} %multiply_convert_fusion.refs_0_), channel_id=1, source_target_pairs={{0,24},{2,26},{4,28},{6,30},{8,16},{10,18},{12,20},{14,22},{16,8},... | collective-permute-start | bytes 196616 | tf_op jit(solution)/shard_map/ppermute | solution.py:464
  63.1 5.2 %up.1 = bf16[128,1024]{1,0:T(8,128)(2,1)} custom-call(bf16[128,1024]{1,0:T(8,128)(2,1)} %get-tuple-element.82.refs_0_, bf16[128,1024]{1,0:T(8,128)(2,1)} %get-tuple-element.83.refs_1_, bf16[128,1024]{1,0:T(8,128)(2,1)} %get-tuple-element.58.refs_0_.refs_2_, f32[128,128]{1,0:T(8,128)} %get-tuple-element.60.refs_2_.refs_4_.refs_3_, f32[16,1024]{1,0:T(8,128)} %copy-done.1, ...), custom_call_target="tpu_custom_call" | custom-call | flops 1000000 | bytes 100000 | tf_op jit(solution)/shard_map/up/pallas_call | solution.py:598
  69.2 0.9 %collective-permute-start.23 = (bf16[128,512]{1,0:T(8,128)(2,1)S(1)}, bf16[128,512]{1,0:T(8,128)(2,1)S(1)}, u32[]{:S(2)}, u32[]{:S(2)}) collective-permute-start(bf16[128,512]{1,0:T(8,128)(2,1)S(1)} %get-tuple-element.90.refs_1_), channel_id=1, source_target_pairs={{0,4},{2,6},{4,0},{6,2},{8,12},{10,14},{12,8},{14,10},{16,20},{18,... | collective-permute-start | bytes 393224 | tf_op jit(solution)/shard_map/ppermute | solution.py:464
  70.2 1.1 %collective-permute-start.25 = (bf16[128,512]{1,0:T(8,128)(2,1)S(1)}, bf16[128,512]{1,0:T(8,128)(2,1)S(1)}, u32[]{:S(2)}, u32[]{:S(2)}) collective-permute-start(bf16[128,512]{1,0:T(8,128)(2,1)S(1)} %get-tuple-element.90.refs_1_), channel_id=1, source_target_pairs={{0,2},{2,0},{4,6},{6,4},{8,10},{10,8},{12,14},{14,12},{16,18},{18,... | collective-permute-start | bytes 393224 | tf_op jit(solution)/shard_map/ppermute | solution.py:464
  71.3 1.3 %collective-permute-start.26 = (bf16[128,512]{1,0:T(8,128)(2,1)S(1)}, bf16[128,512]{1,0:T(8,128)(2,1)S(1)}, u32[]{:S(2)}, u32[]{:S(2)}) collective-permute-start(bf16[128,512]{1,0:T(8,128)(2,1)S(1)} %get-tuple-element.89.refs_0_), channel_id=1, source_target_pairs={{0,4},{2,6},{4,0},{6,2},{8,12},{10,14},{12,8},{14,10},{16,20},{18,... | collective-permute-start | bytes 393224 | tf_op jit(solution)/shard_map/ppermute | solution.py:464
  72.6 1.1 %collective-permute-done.21.refs_2_ = bf16[128,512]{1,0:T(8,128)(2,1)S(1)} collective-permute-done((bf16[128,512]{1,0:T(8,128)(2,1)S(1)}, bf16[128,512]{1,0:T(8,128)(2,1)S(1)}, u32[]{:S(2)}, u32[]{:S(2)}) %collective-permute-start.21) | collective-permute-done | bytes 131104 | tf_op jit(solution)/shard_map/ppermute | solution.py:464
  75.4 1.5 %collective-permute-start.24 = (bf16[128,512]{1,0:T(8,128)(2,1)S(1)}, bf16[128,512]{1,0:T(8,128)(2,1)S(1)}, u32[]{:S(2)}, u32[]{:S(2)}) collective-permute-start(bf16[128,512]{1,0:T(8,128)(2,1)S(1)} %collective-permute-done.23.refs_5_), channel_id=1, source_target_pairs={{0,2},{2,0},{4,6},{6,4},{8,10},{10,8},{12,14},{14,12},{16,18},{18,... | collective-permute-start | bytes 393224 | tf_op jit(solution)/shard_map/ppermute | solution.py:464
  77.1 1.2 %finish.2.refs_2_ = f32[512,1024]{1,0:T(8,128)} custom-call(bf16[128,512]{1,0:T(8,128)(2,1)S(1)} %get-tuple-element.89.refs_0_, bf16[128,512]{1,0:T(8,128)(2,1)S(1)} %get-tuple-element.90.refs_1_, bf16[128,512]{1,0:T(8,128)(2,1)S(1)} %collective-permute-done.21.refs_2_, bf16[128,512]{1,0:T(8,128)(2,1)S(1)} %collective-permute-done.25.refs_3_, ...), custom_call_target="tpu_custom_call" | custom-call | flops 1000000 | bytes 100000 | tf_op jit(solution)/shard_map/finish/pallas_call | solution.py:468
  78.7 1.6 %collective-permute-done.24.refs_1_ = bf16[128,512]{1,0:T(8,128)(2,1)S(1)} collective-permute-done((bf16[128,512]{1,0:T(8,128)(2,1)S(1)}, bf16[128,512]{1,0:T(8,128)(2,1)S(1)}, u32[]{:S(2)}, u32[]{:S(2)}) %collective-permute-start.24) | collective-permute-done | bytes 131104 | tf_op jit(solution)/shard_map/ppermute | solution.py:464
  (65 shorter events, 13.9 us)
Async XLA Ops:
  0.6 24.2 %collective-permute-start.1 = (bf16[2560,512]{1,0:T(8,128)(2,1)}, bf16[2560,512]{1,0:T(8,128)(2,1)}, u32[]{:S(2)}, u32[]{:S(2)}) collective-permute-start(bf16[2560,512]{1,0:T(8,128)(2,1)} %linear_mine.1), channel_id=1, source_target_pairs={{0,1},{1,0},{2,3},{3,2},{4,5},{5,4},{6,7},{7,6},{8,9},{9,8},{10,11... | collective-permute-start | bytes 7864328 | tf_op jit(solution)/shard_map/ppermute | solution.py:460
  1.2 20.6 %collective-permute-start.2 = (bf16[1024,1024]{1,0:T(8,128)(2,1)}, bf16[1024,1024]{1,0:T(8,128)(2,1)}, u32[]{:S(2)}, u32[]{:S(2)}) collective-permute-start(bf16[1024,1024]{1,0:T(8,128)(2,1)} %refs_6_.3), channel_id=1, source_target_pairs={{0,1},{1,0},{2,3},{3,2},{4,5},{5,4},{6,7},{7,6},{8,9},{9,8},{10,11... | collective-permute-start | bytes 6291464 | tf_op jit(solution)/shard_map/ppermute | solution.py:460
  4.1 20.8 %all-to-all-start = ((bf16[16,88,128]{2,1,0:T(8,128)(2,1)}), bf16[16,88,128]{2,1,0:T(8,128)(2,1)S(1)}, u32[]{:S(2)}, u32[]{:S(2)}) async-start(bf16[16,88,128]{2,1,0:T(8,128)(2,1)} %get-tuple-element.47), calls=%async_computation | async-start | bytes 720896 | tf_op jit(solution)/shard_map/all_to_all | solution.py:521
  12.4 3.5 %collective-permute-start = (bf16[160,512]{1,0:T(8,128)(2,1)}, bf16[160,512]{1,0:T(8,128)(2,1)S(1)}, u32[]{:S(2)}, u32[]{:S(2)}) collective-permute-start(bf16[160,512]{1,0:T(8,128)(2,1)} %get-tuple-element.48.mine), channel_id=1, source_target_pairs={{0,1},{1,0},{2,3},{3,2},{4,5},{5,4},{6,7},{7,6},{8,9},{9,8},{10,11... | collective-permute-start | bytes 491528 | tf_op jit(solution)/shard_map/ppermute | solution.py:460
  12.5 33.7 %collective-permute-start.7 = (bf16[128,1024]{1,0:T(8,128)(2,1)}, bf16[128,1024]{1,0:T(8,128)(2,1)S(1)}, u32[]{:S(2)}, u32[]{:S(2)}) collective-permute-start(bf16[128,1024]{1,0:T(8,128)(2,1)} %refs_5_.1), channel_id=1, source_target_pairs={{0,6},{2,4},{4,2},{6,0},{8,14},{10,12},{12,10},{14,8},{16,22},{18,... | collective-permute-start | bytes 786440 | tf_op jit(solution)/shard_map/ppermute | solution.py:464
  15.3 24.9 %collective-permute-start.8 = (bf16[128,1024]{1,0:T(8,128)(2,1)}, bf16[128,1024]{1,0:T(8,128)(2,1)S(1)}, u32[]{:S(2)}, u32[]{:S(2)}) collective-permute-start(bf16[128,1024]{1,0:T(8,128)(2,1)} %refs_5_.1), channel_id=1, source_target_pairs={{0,2},{2,0},{4,6},{6,4},{8,10},{10,8},{12,14},{14,12},{16,18},{18,... | collective-permute-start | bytes 786440 | tf_op jit(solution)/shard_map/ppermute | solution.py:464
  15.9 24.8 %collective-permute-start.9 = (bf16[128,1024]{1,0:T(8,128)(2,1)}, bf16[128,1024]{1,0:T(8,128)(2,1)S(1)}, u32[]{:S(2)}, u32[]{:S(2)}) collective-permute-start(bf16[128,1024]{1,0:T(8,128)(2,1)} %refs_5_.1), channel_id=1, source_target_pairs={{0,4},{2,6},{4,0},{6,2},{8,12},{10,14},{12,8},{14,10},{16,20},{18,... | collective-permute-start | bytes 786440 | tf_op jit(solution)/shard_map/ppermute | solution.py:464
  21.7 21.2 %collective-permute-start.6 = (bf16[512,1024]{1,0:T(8,128)(2,1)}, bf16[512,1024]{1,0:T(8,128)(2,1)}, u32[]{:S(2)}, u32[]{:S(2)}) collective-permute-start(bf16[512,1024]{1,0:T(8,128)(2,1)} %refs_7_.1), channel_id=1, source_target_pairs={{0,1},{1,0},{2,3},{3,2},{4,5},{5,4},{6,7},{7,6},{8,9},{9,8},{10,11... | collective-permute-start | bytes 3145736 | tf_op jit(solution)/shard_map/ppermute | solution.py:460
  39.4 7.4 %collective-permute-start.3 = (bf16[2,128,128]{2,1,0:T(8,128)(2,1)}, bf16[2,128,128]{2,1,0:T(8,128)(2,1)S(1)}, u32[]{:S(2)}, u32[]{:S(2)}) collective-permute-start(bf16[2,128,128]{2,1,0:T(8,128)(2,1)} %get-tuple-element.55), channel_id=1, source_target_pairs={{0,2},{2,0},{4,6},{6,4},{8,10},{10,8},{12,14},{14,12},{16,18},{18,... | collective-permute-start | bytes 196616 | tf_op jit(solution)/shard_map/ppermute | solution.py:464
  40.2 6.7 %collective-permute-start.4 = (bf16[2,128,128]{2,1,0:T(8,128)(2,1)}, bf16[2,128,128]{2,1,0:T(8,128)(2,1)S(1)}, u32[]{:S(2)}, u32[]{:S(2)}) collective-permute-start(bf16[2,128,128]{2,1,0:T(8,128)(2,1)} %get-tuple-element.56), channel_id=1, source_target_pairs={{0,4},{2,6},{4,0},{6,2},{8,12},{10,14},{12,8},{14,10},{16,20},{18,... | collective-permute-start | bytes 196616 | tf_op jit(solution)/shard_map/ppermute | solution.py:464
  40.7 6.1 %collective-permute-start.5 = (bf16[2,128,128]{2,1,0:T(8,128)(2,1)}, bf16[2,128,128]{2,1,0:T(8,128)(2,1)S(1)}, u32[]{:S(2)}, u32[]{:S(2)}) collective-permute-start(bf16[2,128,128]{2,1,0:T(8,128)(2,1)} %get-tuple-element.57), channel_id=1, source_target_pairs={{0,6},{2,4},{4,2},{6,0},{8,14},{10,12},{12,10},{14,8},{16,22},{18,... | collective-permute-start | bytes 196616 | tf_op jit(solution)/shard_map/ppermute | solution.py:464
  42.9 4.8 %collective-permute-start.11 = (bf16[128,1024]{1,0:T(8,128)(2,1)S(1)}, bf16[128,1024]{1,0:T(8,128)(2,1)S(1)}, u32[]{:S(2)}, u32[]{:S(2)}) collective-permute-start(bf16[128,1024]{1,0:T(8,128)(2,1)S(1)} %copy-done), channel_id=1, source_target_pairs={{0,1},{1,0},{2,3},{3,2},{4,5},{5,4},{6,7},{7,6},{8,9},{9,8},{10,11... | collective-permute-start | bytes 786440 | tf_op jit(solution)/shard_map/ppermute | solution.py:460
  49.2 9.0 %collective-permute-start.15 = (bf16[32,1024]{1,0:T(8,128)(2,1)S(1)}, bf16[32,1024]{1,0:T(8,128)(2,1)S(1)}, u32[]{:S(2)}, u32[]{:S(2)}) collective-permute-start(bf16[32,1024]{1,0:T(8,128)(2,1)S(1)} %get-tuple-element.71), channel_id=1, source_target_pairs={{0,8},{2,10},{4,12},{6,14},{8,0},{10,2},{12,4},{14,6},{16,24},{18,... | collective-permute-start | bytes 196616 | tf_op jit(solution)/shard_map/ppermute | solution.py:464
  50.3 8.4 %collective-permute-start.16 = (bf16[32,1024]{1,0:T(8,128)(2,1)S(1)}, bf16[32,1024]{1,0:T(8,128)(2,1)S(1)}, u32[]{:S(2)}, u32[]{:S(2)}) collective-permute-start(bf16[32,1024]{1,0:T(8,128)(2,1)S(1)} %get-tuple-element.72), channel_id=1, source_target_pairs={{0,16},{2,18},{4,20},{6,22},{8,24},{10,26},{12,28},{14,30},{16,0},... | collective-permute-start | bytes 196616 | tf_op jit(solution)/shard_map/ppermute | solution.py:464
  51.2 7.5 %collective-permute-start.17 = (bf16[32,1024]{1,0:T(8,128)(2,1)S(1)}, bf16[32,1024]{1,0:T(8,128)(2,1)S(1)}, u32[]{:S(2)}, u32[]{:S(2)}) collective-permute-start(bf16[32,1024]{1,0:T(8,128)(2,1)S(1)} %get-tuple-element.73), channel_id=1, source_target_pairs={{0,24},{2,26},{4,28},{6,30},{8,16},{10,18},{12,20},{14,22},{16,8},... | collective-permute-start | bytes 196616 | tf_op jit(solution)/shard_map/ppermute | solution.py:464
  58.7 9.7 %collective-permute-start.18 = (bf16[32,1024]{1,0:T(8,128)(2,1)S(1)}, bf16[32,1024]{1,0:T(8,128)(2,1)S(1)}, u32[]{:S(2)}, u32[]{:S(2)}) collective-permute-start(bf16[32,1024]{1,0:T(8,128)(2,1)S(1)} %multiply_convert_fusion.refs_0_), channel_id=1, source_target_pairs={{0,8},{2,10},{4,12},{6,14},{8,0},{10,2},{12,4},{14,6},{16,24},{18,... | collective-permute-start | bytes 196616 | tf_op jit(solution)/shard_map/ppermute | solution.py:464
  60.1 8.3 %collective-permute-start.19 = (bf16[32,1024]{1,0:T(8,128)(2,1)S(1)}, bf16[32,1024]{1,0:T(8,128)(2,1)S(1)}, u32[]{:S(2)}, u32[]{:S(2)}) collective-permute-start(bf16[32,1024]{1,0:T(8,128)(2,1)S(1)} %multiply_convert_fusion.refs_0_), channel_id=1, source_target_pairs={{0,16},{2,18},{4,20},{6,22},{8,24},{10,26},{12,28},{14,30},{16,0},... | collective-permute-start | bytes 196616 | tf_op jit(solution)/shard_map/ppermute | solution.py:464
  60.5 7.9 %collective-permute-start.20 = (bf16[32,1024]{1,0:T(8,128)(2,1)S(1)}, bf16[32,1024]{1,0:T(8,128)(2,1)S(1)}, u32[]{:S(2)}, u32[]{:S(2)}) collective-permute-start(bf16[32,1024]{1,0:T(8,128)(2,1)S(1)} %multiply_convert_fusion.refs_0_), channel_id=1, source_target_pairs={{0,24},{2,26},{4,28},{6,30},{8,16},{10,18},{12,20},{14,22},{16,8},... | collective-permute-start | bytes 196616 | tf_op jit(solution)/shard_map/ppermute | solution.py:464
  68.5 5.3 %collective-permute-start.21 = (bf16[128,512]{1,0:T(8,128)(2,1)S(1)}, bf16[128,512]{1,0:T(8,128)(2,1)S(1)}, u32[]{:S(2)}, u32[]{:S(2)}) collective-permute-start(bf16[128,512]{1,0:T(8,128)(2,1)S(1)} %get-tuple-element.89.refs_0_), channel_id=1, source_target_pairs={{0,2},{2,0},{4,6},{6,4},{8,10},{10,8},{12,14},{14,12},{16,18},{18,... | collective-permute-start | bytes 393224 | tf_op jit(solution)/shard_map/ppermute | solution.py:464
  69.2 6.1 %collective-permute-start.23 = (bf16[128,512]{1,0:T(8,128)(2,1)S(1)}, bf16[128,512]{1,0:T(8,128)(2,1)S(1)}, u32[]{:S(2)}, u32[]{:S(2)}) collective-permute-start(bf16[128,512]{1,0:T(8,128)(2,1)S(1)} %get-tuple-element.90.refs_1_), channel_id=1, source_target_pairs={{0,4},{2,6},{4,0},{6,2},{8,12},{10,14},{12,8},{14,10},{16,20},{18,... | collective-permute-start | bytes 393224 | tf_op jit(solution)/shard_map/ppermute | solution.py:464
  70.2 6.7 %collective-permute-start.25 = (bf16[128,512]{1,0:T(8,128)(2,1)S(1)}, bf16[128,512]{1,0:T(8,128)(2,1)S(1)}, u32[]{:S(2)}, u32[]{:S(2)}) collective-permute-start(bf16[128,512]{1,0:T(8,128)(2,1)S(1)} %get-tuple-element.90.refs_1_), channel_id=1, source_target_pairs={{0,2},{2,0},{4,6},{6,4},{8,10},{10,8},{12,14},{14,12},{16,18},{18,... | collective-permute-start | bytes 393224 | tf_op jit(solution)/shard_map/ppermute | solution.py:464
  71.3 5.8 %collective-permute-start.26 = (bf16[128,512]{1,0:T(8,128)(2,1)S(1)}, bf16[128,512]{1,0:T(8,128)(2,1)S(1)}, u32[]{:S(2)}, u32[]{:S(2)}) collective-permute-start(bf16[128,512]{1,0:T(8,128)(2,1)S(1)} %get-tuple-element.89.refs_0_), channel_id=1, source_target_pairs={{0,4},{2,6},{4,0},{6,2},{8,12},{10,14},{12,8},{14,10},{16,20},{18,... | collective-permute-start | bytes 393224 | tf_op jit(solution)/shard_map/ppermute | solution.py:464
  73.7 5.0 %collective-permute-start.22 = (bf16[128,512]{1,0:T(8,128)(2,1)S(1)}, bf16[128,512]{1,0:T(8,128)(2,1)S(1)}, u32[]{:S(2)}, u32[]{:S(2)}) collective-permute-start(bf16[128,512]{1,0:T(8,128)(2,1)S(1)} %collective-permute-done.21.refs_2_), channel_id=1, source_target_pairs={{0,4},{2,6},{4,0},{6,2},{8,12},{10,14},{12,8},{14,10},{16,20},{18,... | collective-permute-start | bytes 393224 | tf_op jit(solution)/shard_map/ppermute | solution.py:464
  75.4 5.0 %collective-permute-start.24 = (bf16[128,512]{1,0:T(8,128)(2,1)S(1)}, bf16[128,512]{1,0:T(8,128)(2,1)S(1)}, u32[]{:S(2)}, u32[]{:S(2)}) collective-permute-start(bf16[128,512]{1,0:T(8,128)(2,1)S(1)} %collective-permute-done.23.refs_5_), channel_id=1, source_target_pairs={{0,2},{2,0},{4,6},{6,4},{8,10},{10,8},{12,14},{14,12},{16,18},{18,... | collective-permute-start | bytes 393224 | tf_op jit(solution)/shard_map/ppermute | solution.py:464
  (14 other events, 39.4 us)
